TPU v7x, 512 devices: a whole 4x4x16 slice. The times are simulated.
512 devices in a mesh: dp: 32 (over y, x, z_hi), land: 16 (over z_lo, core).
Axes of the slice: x: 4, y: 4, z: 16 (z_hi: 2, z_lo: 8; z = z_hi * 8 + z_lo), core: 2. Of those that a mesh axis runs over, the one named last changes fastest.
Arguments:
- embeddings: bfloat16 [16384, 4096], P('dp', 'land'), may hold values from -6 to 6
- landmarks: bfloat16 [4096, 4096], P('land', 'dp'), may hold values from -6 to 6
- alpha: float32 [4096], P('land'), may hold values from -0.09375 to 0.09375
- pairs: int32 [2, 32768], P(None, 'dp'), may hold values from 0 to 511, as said below
Outputs:
- gram: float32 [4096, 4096], P('dp', 'land')
- gradient: float32 [4096], P('land')
Inputs may be any that keep to these rules, and one draw needn't show every extreme that they name: `pairs`: pairs come in blocks of 256 in each index of dp; block j of an index compares only responses j * 128 to (j + 1) * 128 - 1 of that index, and a pair's winner and loser differ.
All inputs are finite; a program needn't handle non-finite values.
Results may differ from a plain program's by a relative error of at most 0.0048.
Values may be sent and summed in bfloat16 or wider, within the bound.
No kernel may reach another device: no remote copies, remote signals or barrier semaphores. Data moves between devices by JAX's collectives and lax.ppermute only.
A program may use at most 64 MiB of HBM per device.

v0:
```python
import math

import jax
import jax.numpy as jnp
from jax import lax
from jax.sharding import PartitionSpec as P

EMBED_WIDTH = 4096
BLOCK_ROWS = 128


def make_features(inner, resp_square, landmark_square_norm):
    beta = 0.5 * math.sqrt(EMBED_WIDTH)
    value = (
        beta
        * inner
        * lax.rsqrt(resp_square + 1e-06)[:, None]
        * lax.rsqrt(landmark_square_norm + 1e-06)[None, :]
    )
    return jnp.exp(value).astype(jnp.bfloat16)


def pair_differences(nystrom_feature_matrix, winners, losers):
    blocks = winners.shape[0] // (2 * BLOCK_ROWS)
    base = (jnp.arange(blocks, dtype=jnp.int32) * BLOCK_ROWS)[:, None, None]
    column_ids = jnp.arange(BLOCK_ROWS, dtype=jnp.int32)[None, None, :]
    winner_local = winners.reshape(blocks, 2 * BLOCK_ROWS)[:, :, None] - base
    loser_local = losers.reshape(blocks, 2 * BLOCK_ROWS)[:, :, None] - base
    select_pair_index = (
        (winner_local == column_ids).astype(jnp.float32)
        - (loser_local == column_ids).astype(jnp.float32)
    ).astype(jnp.bfloat16)
    grouped_rows_view = nystrom_feature_matrix.reshape(
        blocks, BLOCK_ROWS, nystrom_feature_matrix.shape[1]
    )
    laplace_output = jnp.einsum(
        "fkt,fte->fke", select_pair_index, grouped_rows_view, preferred_element_type=jnp.float32
    )
    return laplace_output.reshape(winners.shape[0], nystrom_feature_matrix.shape[1]).astype(
        jnp.bfloat16
    )


def per_device(embeddings, landmarks, alpha, pairs):
    pair_count = pairs.shape[1]
    scale = 1.0 / math.sqrt(pair_count * lax.axis_size("dp"))
    centers = lax.all_gather(landmarks, "dp", axis=1, tiled=True)
    landmark_square_norm = jnp.sum(jnp.square(centers.astype(jnp.float32)), axis=1)
    piece = lax.all_gather(embeddings, "land", axis=1, tiled=True)
    columns = centers
    inner_sum = lax.dot_general(
        piece, columns, (((1,), (1,)), ((), ())), preferred_element_type=jnp.float32
    )
    square_sum = jnp.sum(jnp.square(piece.astype(jnp.float32)), axis=1)
    inner_sum, resp_square = (inner_sum, square_sum)
    nystrom_feature_matrix = make_features(inner_sum, resp_square, landmark_square_norm)
    local_diffs = pair_differences(nystrom_feature_matrix, pairs[0], pairs[1])
    partial_margin = jnp.dot(
        local_diffs.astype(jnp.float32), alpha, precision=lax.Precision.HIGHEST
    )
    margin = lax.psum(partial_margin, "land")
    prob = jax.nn.sigmoid(margin)
    weight = prob * (1.0 - prob)
    weighted = (local_diffs.astype(jnp.float32) * (weight * scale)[:, None]).astype(jnp.bfloat16)
    complete_feature_rows = lax.all_gather(nystrom_feature_matrix, "land", axis=1, tiled=True)
    full_diffs = pair_differences(complete_feature_rows, pairs[0], pairs[1])
    columns = full_diffs
    gram = lax.psum_scatter(
        lax.dot_general(
            columns, weighted, (((0,), (0,)), ((), ())), preferred_element_type=jnp.float32
        ),
        "dp",
        scatter_dimension=0,
        tiled=True,
    )
    grad_part = jnp.dot(
        (1.0 - prob) * scale, local_diffs.astype(jnp.float32), precision=lax.Precision.HIGHEST
    )
    gradient = lax.psum(grad_part, "dp")
    return (gram, gradient)


def solution(mesh):
    return jax.shard_map(
        per_device,
        mesh=mesh,
        in_specs=(P("dp", "land"), P("land", "dp"), P("land"), P(None, "dp")),
        out_specs=(P("dp", "land"), P("land")),
        check_vma=False,
    )
```

profile of v0, /device:TPU:96, one launch (start us, length us, event | category | flops | bytes accessed | tf_op | source)
XLA Modules:
  0.0 802.6 jit_solution(231517761229077491)
XLA Ops:
  7.2 0.0 copy-start
  7.2 0.0 all-gather.6.cloned.1.call-start
  7.2 0.7 all-gather.6.cloned.1.call-update
  7.9 0.0 all-gather.4.cloned.1.call-start
  8.0 0.7 all-gather.4.cloned.1.call-update
  8.7 0.0 all-gather.8.cloned.1.call-start
  8.7 150.9 %all-gather.6.cloned.1.call-done = bf16[256,4096]{1,0:T(8,128)(2,1)} async-done(((bf16[256,128]{1,0:T(8,128)(2,1)}), bf16[256,4096]{1,0:T(8,128)(2,1)}) %all-gather.6.cloned.1.call-update) | async-done | bytes 2097168 | tf_op jit(solution)/shard_map/all_gather | solution.py:47
  159.7 0.0 copy-start.2
  159.7 2.2 multiply_reduce_fusion.1
  161.9 75.3 %all-gather.4.cloned.1.call-done = bf16[512,4096]{1,0:T(8,128)(2,1)} async-done(((bf16[512,256]{1,0:T(8,128)(2,1)}), bf16[512,4096]{1,0:T(8,128)(2,1)}) %all-gather.4.cloned.1.call-update) | async-done | bytes 4194320 | tf_op jit(solution)/shard_map/all_gather | solution.py:49
  237.2 0.0 copy-start.1
  237.3 3.2 multiply_reduce_fusion
  240.5 0.0 copy-done.2
  240.5 0.2 copy-done.1
  240.7 0.0 copy-start.3
  240.7 2.0 fusion.9
  242.7 0.0 all-gather.8.cloned.1.call-update
  242.7 0.0 reduce-scatter.2.cloned.1.call-start
  242.8 0.0 copy-done.3
  242.8 0.1 broadcast_subtract_fusion.1
  242.9 1.4 convolution_convert_fusion
  244.3 0.0 copy-done
  244.3 0.5 fusion.18
  244.8 42.0 %psum.14 = f32[1024]{0:T(1024)S(1)} all-reduce(f32[1024]{0:T(1024)S(1)} %bitcast.22), channel_id=1, replica_groups=mesh['dp'=32,'land'=16] {'land'}, use_global_device_ids=true, to_apply=%region_2.0 | all-reduce | flops 1024 | bytes 8192 | tf_op jit(solution)/shard_map/psum | solution.py:61
  286.9 49.3 %all-gather.8.cloned.1.call-done = bf16[512,4096]{1,0:T(8,128)(2,1)} async-done(((bf16[512,256]{1,0:T(8,128)(2,1)}), bf16[512,4096]{1,0:T(8,128)(2,1)}) %all-gather.8.cloned.1.call-update) | async-done | bytes 4194320 | tf_op jit(solution)/shard_map/all_gather | solution.py:65
  336.1 8.9 %fusion.2 = f32[4096,256]{1,0:T(8,128)} fusion(bf16[4,128,4096]{2,1,0:T(8,128)(2,1)} %bitcast.24, bf16[4,256,256]{2,1,0:T(8,128)(2,1)S(1)} %convolution_convert_fusion, f32[4,256]{1,0:T(4,128)S(1)} %mul.61, s32[4,256]{1,0:T(4,128)S(1)} %get-tuple-element.7, s32[4,256]{1,0:T(4,128)S(1)} %get-tuple-element.6), kind=kOutput, calls=%fused_computation.3 | convolution fusion | flops 3226992640 | bytes 8925184 | tf_op jit(solution)/shard_map/dot_general | solution.py:69
  345.1 0.0 reduce-scatter.2.cloned.1.call-update
  345.1 0.3 fusion.19
  345.4 182.4 %psum.15 = f32[256]{0:T(256)} all-reduce(f32[256]{0:T(256)S(1)} %bitcast.23), channel_id=1, replica_groups=mesh['dp'=32,'land'=16] {'dp'}, use_global_device_ids=true, to_apply=%region_4.0 | all-reduce | flops 256 | bytes 2048 | tf_op jit(solution)/shard_map/psum | solution.py:79
  527.8 268.3 %reduce-scatter.2.cloned.1.call-done = f32[128,256]{1,0:T(8,128)} async-done(((f32[4096,256]{1,0:T(8,128)}), f32[128,256]{1,0:T(8,128)}) %reduce-scatter.2.cloned.1.call-update) | async-done | bytes 131088 | tf_op jit(solution)/shard_map/reduce_scatter | solution.py:68
  (8 shorter events, 0.1 us)
Async XLA Ops:
  7.2 237.2 %copy-start = (f32[256]{0:T(256)S(1)}, f32[256]{0:T(256)}, u32[]{:S(2)}) copy-start(f32[256]{0:T(256)} %param.6) | copy-start | bytes 3076
  7.2 152.5 %all-gather.6.cloned.1.call-start = ((), (), s32[]{:S(2)}) async-start(), calls=%async_computation.2 | async-start | bytes 2162688 | tf_op jit(solution)/shard_map/all_gather | solution.py:47
  7.9 229.3 %all-gather.4.cloned.1.call-start = ((), (), s32[]{:S(2)}) async-start(), calls=%async_computation.1 | async-start | bytes 4456448 | tf_op jit(solution)/shard_map/all_gather | solution.py:49
  8.7 327.5 %all-gather.8.cloned.1.call-start = ((), (), s32[]{:S(2)}) async-start(), calls=%async_computation.3 | async-start | bytes 4456448 | tf_op jit(solution)/shard_map/all_gather | solution.py:65
  159.7 80.8 %copy-start.2 = (bf16[256,4096]{1,0:T(8,128)(2,1)S(1)}, bf16[256,4096]{1,0:T(8,128)(2,1)}, u32[]{:S(2)}) copy-start(bf16[256,4096]{1,0:T(8,128)(2,1)} %all-gather.6.cloned.1.call-done) | copy-start | bytes 6291460
  237.2 3.4 copy-start.1
  240.7 2.1 copy-start.3
  242.7 553.4 %reduce-scatter.2.cloned.1.call-start = ((), (), s32[]{:S(2)}) async-start(), calls=%async_computation.4 | async-start | bytes 4325376 | tf_op jit(solution)/shard_map/reduce_scatter | solution.py:68
Sparse Core Ops, SparseCore 0:
  12.1 147.5 all-gather.5
  161.7 75.5 all-gather.3
  242.8 93.2 all-gather.7
  345.2 450.8 reduce-scatter.1
where the time goes:
time: 803 us
  waiting for transfers between devices  545 us (68%)
  blocking collectives  224 us (28%)
  between operations  13.8 us (2%)
  matrix products  13.1 us (2%)
    reduce_scatter x1, waiting for transfers between devices, per_device(): lax.psum_scatter(lax.dot_general(columns, weighted, (((0,), (0,)), ((), (...  268 us
    psum x1, blocking collectives, per_device(): gradient = lax.psum(grad_part, 'dp')  182 us
    all_gather x1, waiting for transfers between devices, per_device(): centers = lax.all_gather(landmarks, 'dp', axis=1, tiled=True)  151 us
    all_gather x1, waiting for transfers between devices, per_device(): piece = lax.all_gather(embeddings, 'land', axis=1, tiled=True)  75.3 us
    all_gather x1, waiting for transfers between devices, per_device(): lax.all_gather(nystrom_feature_matrix, 'land', axis=1, tiled=True)  49.3 us
    psum x1, blocking collectives, per_device(): margin = lax.psum(partial_margin, 'land')  42 us
  transfers between devices with their start and end apart: 4, of which 4 were waited for; matrix products, arithmetic and copies ran while one was open for 1% of the time, Pallas kernels for 0%

commit v1 on v0

v1 whole, which is shorter than its diff:
```python
import functools
import math

import jax
import jax.numpy as jnp
from jax import lax
from jax.experimental import pallas as pl
from jax.experimental.pallas import tpu as pltpu
from jax.sharding import Mesh, PartitionSpec as P

EMBED_WIDTH = 4096
BLOCK_ROWS = 128
BETA = 0.5 * math.sqrt(EMBED_WIDTH)
LINE = ("zh", "zl", "c")
PLANE = ("y", "x")
NT = (((1,), (1,)), ((), ()))


def features_kernel(emb_ref, land_ref, out_ref, acc, resp_sq, land_sq):
    step = pl.program_id(1)
    emb, land = emb_ref[...], land_ref[...]

    @pl.when(step == 0)
    def _():
        acc[...] = jnp.zeros_like(acc)
        resp_sq[...] = jnp.zeros_like(resp_sq)
        land_sq[...] = jnp.zeros_like(land_sq)

    acc[...] += lax.dot_general(land, emb, NT, preferred_element_type=jnp.float32)
    for sums, values in ((resp_sq, emb), (land_sq, land)):
        total = sums[...]
        for at in range(0, values.shape[1], 128):
            part = values[:, at : at + 128].astype(jnp.float32)
            total += part * part
        sums[...] = total

    @pl.when(step == pl.num_programs(1) - 1)
    def _():
        ones = jnp.ones((8, 128), jnp.float32)
        resp = lax.dot_general(
            ones, resp_sq[...], NT, precision=lax.Precision.HIGHEST, preferred_element_type=jnp.float32
        )[0:1]
        norm = jnp.sum(land_sq[...], axis=1, keepdims=True)
        value = BETA * acc[...] * lax.rsqrt(resp + 1e-06) * lax.rsqrt(norm + 1e-06)
        out_ref[...] = jnp.exp(value).astype(out_ref.dtype)


def make_features(emb, land, slabs, rows):
    count, width = land.shape
    tile = 1024
    steps = width // tile
    return pl.pallas_call(
        features_kernel,
        grid=(slabs, steps),
        in_specs=[
            pl.BlockSpec((rows, tile), lambda s, k: (0, s * steps + k)),
            pl.BlockSpec((count, tile), lambda s, k: (0, k)),
        ],
        out_specs=pl.BlockSpec((count, rows), lambda s, k: (0, s)),
        out_shape=jax.ShapeDtypeStruct((count, slabs * rows), jnp.bfloat16),
        scratch_shapes=[
            pltpu.VMEM((count, rows), jnp.float32),
            pltpu.VMEM((rows, 128), jnp.float32),
            pltpu.VMEM((count, 128), jnp.float32),
        ],
        compiler_params=pltpu.CompilerParams(vmem_limit_bytes=32 * 1024 * 1024),
        cost_estimate=pl.CostEstimate(
            flops=2 * count * slabs * rows * width,
            bytes_accessed=2 * slabs * rows * width,
            transcendentals=count * slabs * rows,
        ),
    )(emb, land)


def gram_kernel(scale, at_ref, feat_ref, alpha_ref, row_ref, col_ref, out_ref, v_ref):
    half, own = at_ref[0], at_ref[1]
    count, responses = feat_ref.shape
    blocks = responses // BLOCK_ROWS
    pairs = 2 * BLOCK_ROWS
    slab_blocks = blocks // 2
    alpha = alpha_ref[...]
    high = alpha.astype(jnp.bfloat16).astype(jnp.float32)
    middle = (alpha - high).astype(jnp.bfloat16).astype(jnp.float32)
    low = alpha - high - middle
    row = lax.broadcasted_iota(jnp.int32, (16, count), 0)
    split = jnp.where(row == 0, high, jnp.where(row == 1, middle, jnp.where(row == 2, low, 0.0)))
    scores = jnp.dot(split.astype(jnp.bfloat16), feat_ref[...], preferred_element_type=jnp.float32)
    scores = scores[0:1] + scores[1:2] + scores[2:3]

    first = pl.multiple_of(own * BLOCK_ROWS, BLOCK_ROWS)
    second = pl.multiple_of(count // 2 + own * BLOCK_ROWS, BLOCK_ROWS)
    grad = jnp.zeros((1, pairs), jnp.float32)
    lane = lax.broadcasted_iota(jnp.int32, (pairs, BLOCK_ROWS), 1)
    sub = lax.broadcasted_iota(jnp.int32, (BLOCK_ROWS, pairs), 0)
    for b in range(blocks):
        base = (b % slab_blocks) * BLOCK_ROWS
        cols = slice(b * BLOCK_ROWS, (b + 1) * BLOCK_ROWS)
        select = jnp.where(col_ref[b, :, 0:1] - base == lane, 1.0, 0.0) - jnp.where(
            col_ref[b, :, 1:2] - base == lane, 1.0, 0.0
        )
        margin = jnp.sum(select * scores[:, cols], axis=1, keepdims=True)
        prob = 1.0 / (1.0 + jnp.exp(-margin))
        weight = prob * (1.0 - prob) * scale
        features = jnp.concatenate(
            [feat_ref[pl.ds(first, BLOCK_ROWS), cols], feat_ref[pl.ds(second, BLOCK_ROWS), cols]], axis=0
        )
        diffs = lax.dot_general(
            select.astype(jnp.bfloat16), features, NT, preferred_element_type=jnp.float32
        )
        diffs = diffs.astype(jnp.bfloat16).astype(jnp.float32)
        weighted = (diffs * weight).astype(jnp.bfloat16)
        grad += jnp.sum(diffs * ((1.0 - prob) * scale), axis=0, keepdims=True)
        back = jnp.where(row_ref[b, 0:1, :] - base == sub, 1.0, 0.0) - jnp.where(
            row_ref[b, 1:2, :] - base == sub, 1.0, 0.0
        )
        v = jnp.dot(back.astype(jnp.bfloat16), weighted, preferred_element_type=jnp.float32)
        v_high = v.astype(jnp.bfloat16)
        v_ref[cols, 0:pairs] = v_high
        v_ref[cols, pairs : 2 * pairs] = (v - v_high.astype(jnp.float32)).astype(jnp.bfloat16)

    grad_high = grad.astype(jnp.bfloat16).astype(jnp.float32)
    tail_row = lax.broadcasted_iota(jnp.int32, (16, pairs), 0)
    tail = jnp.where(tail_row == 0, grad_high, jnp.where(tail_row == 1, grad - grad_high, 0.0))
    tail = tail.astype(jnp.bfloat16)
    v = v_ref[...]

    def block(d, _):
        at = pl.multiple_of(half * (count // 2) + d * BLOCK_ROWS, BLOCK_ROWS)
        part = jnp.dot(feat_ref[pl.ds(at, BLOCK_ROWS), :], v_ref[...], preferred_element_type=jnp.float32)
        out_ref[d, 0:BLOCK_ROWS, :] = (part[:, 0:pairs] + part[:, pairs:]).astype(jnp.bfloat16)
        out_ref[d, BLOCK_ROWS:, :] = tail
        return 0

    lax.fori_loop(0, out_ref.shape[0], block, 0)


def make_gram(at, features, alpha, row_pairs, col_pairs, scale, owners):
    count, responses = features.shape
    vmem = pl.BlockSpec(memory_space=pltpu.VMEM)
    return pl.pallas_call(
        functools.partial(gram_kernel, scale),
        in_specs=[pl.BlockSpec(memory_space=pltpu.SMEM), vmem, vmem, vmem, vmem],
        out_specs=vmem,
        out_shape=jax.ShapeDtypeStruct((owners, BLOCK_ROWS + 16, 2 * BLOCK_ROWS), jnp.bfloat16),
        scratch_shapes=[pltpu.VMEM((responses, 4 * BLOCK_ROWS), jnp.bfloat16)],
        compiler_params=pltpu.CompilerParams(vmem_limit_bytes=40 * 1024 * 1024),
        cost_estimate=pl.CostEstimate(
            flops=2 * count * responses * 256, bytes_accessed=2 * count * responses, transcendentals=2048
        ),
    )(at, features, alpha, row_pairs, col_pairs)


def per_device(embeddings, landmarks, alpha, pairs):
    rows, pair_count = embeddings.shape[0], pairs.shape[1]
    planes = lax.axis_size(PLANE)
    slabs = lax.axis_size("zh")
    scale = 1.0 / math.sqrt(pair_count * slabs * planes)
    zh = lax.axis_index("zh")
    own = lax.axis_index(("zl", "c"))

    emb = lax.all_gather(embeddings, LINE, axis=1, tiled=True)

    half = landmarks.shape[0] // slabs
    spread = jnp.broadcast_to(
        landmarks.reshape(1, slabs, half, landmarks.shape[1]), (planes, slabs, half, landmarks.shape[1])
    ).reshape(planes * slabs * half, landmarks.shape[1])
    land = lax.all_to_all(spread, PLANE + ("zh",), 0, 0, tiled=True)
    land = land.reshape(planes * slabs, half, -1).transpose(1, 0, 2).reshape(half, -1)

    lands = lax.axis_size(("zl", "c"))
    alphas = lax.all_to_all(jnp.broadcast_to(alpha[None], (lands, alpha.shape[0])), ("zl", "c"), 0, 0, tiled=True)
    alphas = alphas.reshape(lands, slabs, half).transpose(1, 0, 2).reshape(1, -1)

    other = lax.ppermute(pairs, "zh", [(0, 1), (1, 0)])
    both = jnp.where(zh == 0, jnp.stack([pairs, other]), jnp.stack([other, pairs]))
    blocks = slabs * rows // BLOCK_ROWS
    row_pairs = both.reshape(slabs, 2, blocks // slabs, -1).transpose(0, 2, 1, 3).reshape(blocks, 2, -1)
    col_pairs = row_pairs.transpose(0, 2, 1)

    mine = make_features(emb, land, slabs, rows)
    features = lax.all_gather(mine, LINE, axis=0, tiled=True)
    at = jnp.stack([zh, own]).astype(jnp.int32)
    parts = make_gram(at, features, alphas, row_pairs, col_pairs, scale, planes)
    parts = lax.all_to_all(parts, PLANE, 0, 0, tiled=True)
    total = jnp.sum(parts.astype(jnp.float32), axis=0)
    return total[:BLOCK_ROWS], total[BLOCK_ROWS] + total[BLOCK_ROWS + 1]


def solution(mesh):
    fine = Mesh(mesh.devices.reshape(4, 4, 2, 8, 2), ("y", "x", "zh", "zl", "c"))
    dp, land = ("y", "x", "zh"), ("zl", "c")
    return jax.shard_map(
        per_device,
        mesh=fine,
        in_specs=(P(dp, land), P(land, dp), P(land), P(None, dp)),
        out_specs=(P(dp, land), P(land)),
        check_vma=False,
    )
```

time: 803 us -> 289 us (0.36)
  the two profiles are of different devices: /device:TPU:96 before, /device:TPU:1 now
where the time goes in v1:
time: 289 us; the launch traced here: 288 us
  waiting for transfers between devices  145 us (50%)
  blocking collectives  85.4 us (30%)
  Pallas kernels  18.7 us (6%)
  starting transfers between devices  14.1 us (5%)
  between operations  14.1 us (5%)
  local copies, waits for them, and re-layouts  9.65 us (3%)
    all_gather x1, waiting for transfers between devices, per_device(): emb = lax.all_gather(embeddings, LINE, axis=1, tiled=True)  80.5 us
    all_to_all x1, blocking collectives, per_device(): land = lax.all_to_all(spread, PLANE + ('zh',), 0, 0, tiled=True)  61.1 us
    all_gather x1, waiting for transfers between devices, per_device(): features = lax.all_gather(mine, LINE, axis=0, tiled=True)  58.6 us
    all_to_all x1, blocking collectives, per_device(): parts = lax.all_to_all(parts, PLANE, 0, 0, tiled=True)  24.3 us
    pallas_call x1, Pallas kernels, make_features(): pl.pallas_call(features_kernel, grid=(slabs, steps), in_specs=[pl.BlockSp...  9.88 us
    pallas_call x1, Pallas kernels, make_gram(): pl.pallas_call(functools.partial(gram_kernel, scale), in_specs=[pl.BlockS...  8.79 us
    ppermute x1, starting transfers between devices, per_device(): other = lax.ppermute(pairs, 'zh', [(0, 1), (1, 0)])  7.48 us
    unnamed x8, local copies, waits for them, and re-layouts  6.77 us
  transfers between devices with their start and end apart: 4, of which 3 were waited for; matrix products, arithmetic and copies ran while one was open for 1% of the time, Pallas kernels for 0%

profile of v1, /device:TPU:1, one launch (start us, length us, event | category | flops | bytes accessed | tf_op | source)
XLA Modules:
  0.0 288.2 jit_solution(10125460260518111422)
XLA Ops:
  7.2 0.0 all-gather.3.cloned.1.call-start
  7.2 0.7 all-gather.3.cloned.1.call-update
  7.9 0.0 all-gather.5.cloned.1.call-start
  7.9 1.1 broadcast_in_dim.14
  9.0 61.1 %all_to_all.20 = bf16[32,128,128]{2,1,0:T(8,128)(2,1)S(1)} all-to-all(bf16[32,128,128]{2,1,0:T(8,128)(2,1)S(1)} %bitcast.20), channel_id=1, replica_groups=mesh['y'=4,'x'=4,'zh'=2,'zl'=8,'c'=2] {'y','x','zh'}, dimensions={0} | all-to-all | bytes 2097152 | tf_op jit(solution)/shard_map/all_to_all | solution.py:167
  70.1 0.1 copy_bitcast_fusion.land_ref
  70.3 80.5 %all-gather.3.cloned.1.call-done.emb_ref = bf16[512,8192]{1,0:T(8,128)(2,1)} async-done(((bf16[512,256]{1,0:T(8,128)(2,1)}), bf16[512,8192]{1,0:T(8,128)(2,1)}) %all-gather.3.cloned.1.call-update) | async-done | bytes 8388624 | tf_op jit(solution)/shard_map/all_gather | solution.py:161
  150.8 0.0 copy-start
  150.8 3.4 %copy-done = bf16[512,8192]{1,0:T(8,128)(2,1)S(1)} copy-done((bf16[512,8192]{1,0:T(8,128)(2,1)S(1)}, bf16[512,8192]{1,0:T(8,128)(2,1)}, u32[]{:S(2)}) %copy-start) | copy-done | bytes 8388632
  154.2 0.0 copy-start.3
  154.2 0.0 copy-start.2
  154.2 9.9 %shard_map.59 = bf16[128,1024]{1,0:T(8,128)(2,1)} custom-call(bf16[512,8192]{1,0:T(8,128)(2,1)S(1)} %copy-done, bf16[128,4096]{1,0:T(8,128)(2,1)S(1)} %copy_bitcast_fusion.land_ref), custom_call_target="tpu_custom_call" | custom-call | flops 1073741824 | bytes 8388608 | tf_op jit(solution)/shard_map/pallas_call | solution.py:52
  164.1 0.0 all-gather.5.cloned.1.call-update
  164.1 0.0 copy-done.3
  164.1 0.6 broadcast_in_dim.15
  164.7 6.5 %all-to-all-start.1 = ((f32[16,1,256]{2,1,0:T(1,128)}), f32[16,1,256]{2,1,0:T(1,128)S(1)}, u32[]{:S(2)}, u32[]{:S(2)}) async-start(f32[16,1,256]{2,1,0:T(1,128)} %broadcast_in_dim.15), calls=%async_computation.1 | async-start | bytes 32768 | tf_op jit(solution)/shard_map/all_to_all | solution.py:171
  171.2 0.0 copy-done.2
  171.2 7.5 %collective-permute-start = (s32[2,1024]{1,0:T(2,128)S(1)}, s32[2,1024]{1,0:T(2,128)S(1)}, u32[]{:S(2)}, u32[]{:S(2)}) collective-permute-start(s32[2,1024]{1,0:T(2,128)S(1)} %copy-done.2), channel_id=1, source_target_pairs={{0,16},{16,0},{1,17},{17,1},{2,18},{18,2},{3,19},{19,3},{4,20},{20... | collective-permute-start | bytes 24584 | tf_op jit(solution)/shard_map/ppermute | solution.py:174
  178.7 0.1 pad_add_fusion.1.at_ref
  178.8 5.7 %collective-permute-done = s32[2,1024]{1,0:T(2,128)S(1)} collective-permute-done((s32[2,1024]{1,0:T(2,128)S(1)}, s32[2,1024]{1,0:T(2,128)S(1)}, u32[]{:S(2)}, u32[]{:S(2)}) %collective-permute-start) | collective-permute-done | bytes 8224 | tf_op jit(solution)/shard_map/ppermute | solution.py:174
  184.5 0.4 copy.13
  184.9 0.0 all-to-all-done.1
  184.9 58.6 %all-gather.5.cloned.1.call-done.feat_ref = bf16[4096,1024]{1,0:T(8,128)(2,1)} async-done(((bf16[128,1024]{1,0:T(8,128)(2,1)}), bf16[4096,1024]{1,0:T(8,128)(2,1)}) %all-gather.5.cloned.1.call-update) | async-done | bytes 8388624 | tf_op jit(solution)/shard_map/all_gather | solution.py:181
  243.5 0.0 copy-start.1
  243.5 3.4 %copy-done.1 = bf16[4096,1024]{1,0:T(8,128)(2,1)S(1)} copy-done((bf16[4096,1024]{1,0:T(8,128)(2,1)S(1)}, bf16[4096,1024]{1,0:T(8,128)(2,1)}, u32[]{:S(2)}) %copy-start.1) | copy-done | bytes 8388632
  246.9 8.8 %shard_map.60 = bf16[16,144,256]{2,1,0:T(8,128)(2,1)S(1)} custom-call(s32[2]{0:T(128)S(1)} %pad_add_fusion.1.at_ref, bf16[4096,1024]{1,0:T(8,128)(2,1)S(1)} %copy-done.1, f32[1,4096]{1,0:T(1,128)S(1)} %bitcast.19, s32[8,2,256]{2,1,0:T(2,128)S(1)} %reshape.36.row_ref, s32[8,256,2]{2,1,0:T(8,128)S(1)} %bitcast.18), custom_call_target="tpu_custom_call" | custom-call | flops 2147483648 | bytes 8388608 | tf_op jit(solution)/shard_map/pallas_call | solution.py:140
  255.7 24.3 %all_to_all.21 = bf16[16,144,256]{2,1,0:T(8,128)(2,1)S(1)} all-to-all(bf16[16,144,256]{2,1,0:T(8,128)(2,1)S(1)} %shard_map.60), channel_id=1, replica_groups=mesh['y'=4,'x'=4,'zh'=2,'zl'=8,'c'=2] {'y','x'}, dimensions={0} | all-to-all | bytes 2359296 | tf_op jit(solution)/shard_map/all_to_all | solution.py:184
  280.0 0.2 convert_reduce_fusion
  280.2 0.7 slice.32
  280.8 0.6 slice_add_fusion
  (5 shorter events, 0.0 us)
Async XLA Ops:
  7.2 143.6 %all-gather.3.cloned.1.call-start = ((), (), s32[]{:S(2)}) async-start(), calls=%async_computation.3 | async-start | bytes 8650752 | tf_op jit(solution)/shard_map/all_gather | solution.py:161
  7.9 235.6 %all-gather.5.cloned.1.call-start = ((), (), s32[]{:S(2)}) async-start(), calls=%async_computation.4 | async-start | bytes 8650752 | tf_op jit(solution)/shard_map/all_gather | solution.py:181
  150.8 3.4 %copy-start = (bf16[512,8192]{1,0:T(8,128)(2,1)S(1)}, bf16[512,8192]{1,0:T(8,128)(2,1)}, u32[]{:S(2)}) copy-start(bf16[512,8192]{1,0:T(8,128)(2,1)} %all-gather.3.cloned.1.call-done.emb_ref) | copy-start | bytes 25165828
  154.2 9.9 %copy-start.3 = (f32[256]{0:T(256)S(1)}, f32[256]{0:T(256)}, u32[]{:S(2)}) copy-start(f32[256]{0:T(256)} %param.6) | copy-start | bytes 3076
  154.2 17.0 %copy-start.2 = (s32[2,1024]{1,0:T(2,128)S(1)}, s32[2,1024]{1,0:T(2,128)}, u32[]{:S(2)}) copy-start(s32[2,1024]{1,0:T(2,128)} %param.7) | copy-start | bytes 24580
  164.7 20.2 %all-to-all-start.1 = ((f32[16,1,256]{2,1,0:T(1,128)}), f32[16,1,256]{2,1,0:T(1,128)S(1)}, u32[]{:S(2)}, u32[]{:S(2)}) async-start(f32[16,1,256]{2,1,0:T(1,128)} %broadcast_in_dim.15), calls=%async_computation.1 | async-start | bytes 32768 | tf_op jit(solution)/shard_map/all_to_all | solution.py:171
  171.2 13.2 %collective-permute-start = (s32[2,1024]{1,0:T(2,128)S(1)}, s32[2,1024]{1,0:T(2,128)S(1)}, u32[]{:S(2)}, u32[]{:S(2)}) collective-permute-start(s32[2,1024]{1,0:T(2,128)S(1)} %copy-done.2), channel_id=1, source_target_pairs={{0,16},{16,0},{1,17},{17,1},{2,18},{18,2},{3,19},{19,3},{4,20},{20... | collective-permute-start | bytes 24584 | tf_op jit(solution)/shard_map/ppermute | solution.py:174
  243.5 3.4 %copy-start.1 = (bf16[4096,1024]{1,0:T(8,128)(2,1)S(1)}, bf16[4096,1024]{1,0:T(8,128)(2,1)}, u32[]{:S(2)}) copy-start(bf16[4096,1024]{1,0:T(8,128)(2,1)} %all-gather.5.cloned.1.call-done.feat_ref) | copy-start | bytes 25165828
Sparse Core Ops, SparseCore 0:
  10.0 140.6 all-gather.2
  164.2 79.2 all-gather.4

commit v2 on v1

--- a/solution.py
+++ b/solution.py
@@ -18,7 +18,6 @@
 
 def features_kernel(emb_ref, land_ref, out_ref, acc, resp_sq, land_sq):
     step = pl.program_id(1)
-    emb, land = emb_ref[...], land_ref[...]
 
     @pl.when(step == 0)
     def _():
@@ -26,23 +25,23 @@
         resp_sq[...] = jnp.zeros_like(resp_sq)
         land_sq[...] = jnp.zeros_like(land_sq)
 
-    acc[...] += lax.dot_general(land, emb, NT, preferred_element_type=jnp.float32)
-    for sums, values in ((resp_sq, emb), (land_sq, land)):
+    acc[...] += lax.dot_general(emb_ref[...], land_ref[...], NT, preferred_element_type=jnp.float32)
+    for sums, ref in ((resp_sq, emb_ref), (land_sq, land_ref)):
         total = sums[...]
-        for at in range(0, values.shape[1], 128):
-            part = values[:, at : at + 128].astype(jnp.float32)
+        for at in range(0, ref.shape[1], 128):
+            part = ref[:, at : at + 128].astype(jnp.float32)
             total += part * part
         sums[...] = total
 
     @pl.when(step == pl.num_programs(1) - 1)
     def _():
         ones = jnp.ones((8, 128), jnp.float32)
-        resp = lax.dot_general(
-            ones, resp_sq[...], NT, precision=lax.Precision.HIGHEST, preferred_element_type=jnp.float32
+        norm = lax.dot_general(
+            ones, land_sq[...], NT, precision=lax.Precision.HIGHEST, preferred_element_type=jnp.float32
         )[0:1]
-        norm = jnp.sum(land_sq[...], axis=1, keepdims=True)
+        resp = jnp.sum(resp_sq[...], axis=1, keepdims=True)
         value = BETA * acc[...] * lax.rsqrt(resp + 1e-06) * lax.rsqrt(norm + 1e-06)
-        out_ref[...] = jnp.exp(value).astype(out_ref.dtype)
+        out_ref[...] = jnp.exp(value).T.astype(out_ref.dtype)
 
 
 def make_features(emb, land, slabs, rows):
@@ -59,11 +58,11 @@
         out_specs=pl.BlockSpec((count, rows), lambda s, k: (0, s)),
         out_shape=jax.ShapeDtypeStruct((count, slabs * rows), jnp.bfloat16),
         scratch_shapes=[
-            pltpu.VMEM((count, rows), jnp.float32),
+            pltpu.VMEM((rows, count), jnp.float32),
             pltpu.VMEM((rows, 128), jnp.float32),
             pltpu.VMEM((count, 128), jnp.float32),
         ],
-        compiler_params=pltpu.CompilerParams(vmem_limit_bytes=32 * 1024 * 1024),
+        compiler_params=pltpu.CompilerParams(vmem_limit_bytes=60 * 1024 * 1024),
         cost_estimate=pl.CostEstimate(
             flops=2 * count * slabs * rows * width,
             bytes_accessed=2 * slabs * rows * width,
@@ -122,7 +121,6 @@
     tail_row = lax.broadcasted_iota(jnp.int32, (16, pairs), 0)
     tail = jnp.where(tail_row == 0, grad_high, jnp.where(tail_row == 1, grad - grad_high, 0.0))
     tail = tail.astype(jnp.bfloat16)
-    v = v_ref[...]
 
     def block(d, _):
         at = pl.multiple_of(half * (count // 2) + d * BLOCK_ROWS, BLOCK_ROWS)
@@ -143,7 +141,7 @@
         out_specs=vmem,
         out_shape=jax.ShapeDtypeStruct((owners, BLOCK_ROWS + 16, 2 * BLOCK_ROWS), jnp.bfloat16),
         scratch_shapes=[pltpu.VMEM((responses, 4 * BLOCK_ROWS), jnp.bfloat16)],
-        compiler_params=pltpu.CompilerParams(vmem_limit_bytes=40 * 1024 * 1024),
+        compiler_params=pltpu.CompilerParams(vmem_limit_bytes=60 * 1024 * 1024),
         cost_estimate=pl.CostEstimate(
             flops=2 * count * responses * 256, bytes_accessed=2 * count * responses, transcendentals=2048
         ),
@@ -161,11 +159,13 @@
     emb = lax.all_gather(embeddings, LINE, axis=1, tiled=True)
 
     half = landmarks.shape[0] // slabs
-    spread = jnp.broadcast_to(
-        landmarks.reshape(1, slabs, half, landmarks.shape[1]), (planes, slabs, half, landmarks.shape[1])
-    ).reshape(planes * slabs * half, landmarks.shape[1])
-    land = lax.all_to_all(spread, PLANE + ("zh",), 0, 0, tiled=True)
-    land = land.reshape(planes * slabs, half, -1).transpose(1, 0, 2).reshape(half, -1)
+    halves = landmarks.reshape(slabs, half, landmarks.shape[1])
+    kept, sent = jnp.where(zh == 0, halves, halves[::-1])
+    came = lax.ppermute(sent, "zh", [(0, 1), (1, 0)])
+    part = jnp.where(zh == 0, jnp.concatenate([kept, came], axis=1), jnp.concatenate([came, kept], axis=1))
+    spread = jnp.broadcast_to(part[None], (planes,) + part.shape).reshape(planes * half, -1)
+    land = lax.all_to_all(spread, PLANE, 0, 0, tiled=True)
+    land = land.reshape(planes, half, -1).transpose(1, 0, 2).reshape(half, -1)
 
     lands = lax.axis_size(("zl", "c"))
     alphas = lax.all_to_all(jnp.broadcast_to(alpha[None], (lands, alpha.shape[0])), ("zl", "c"), 0, 0, tiled=True)

time: 289 us -> 246 us (0.85)
  blocking collectives: 85.4 us -> 47.2 us
  waiting for transfers between devices: 145 us -> 125 us
  starting transfers between devices: 14.1 us -> 28.5 us
  Pallas kernels: 18.7 us -> 23.8 us
  local copies, waits for them, and re-layouts: 9.65 us -> 4.56 us
    all_to_all x1, blocking collectives: 61.1 us -> 22.2 us  [per_device(): land = lax.all_to_all(spread, PLANE, 0, 0, tiled=True)]
    all_gather x1, waiting for transfers between devices: 80.5 us -> 63.2 us  [per_device(): emb = lax.all_gather(embeddings, LINE, axis=1, tiled=True)]
    ppermute x0 -> x1, starting transfers between devices: none -> 16.3 us  [per_device(): came = lax.ppermute(sent, 'zh', [(0, 1), (1, 0)])]
    unnamed x8 -> x6, local copies, waits for them, and re-layouts: 6.77 us -> 0.01 us
    all_gather x1, waiting for transfers between devices: 58.6 us -> 54.1 us  [per_device(): features = lax.all_gather(mine, LINE, axis=0, tiled=True)]
    pallas_call x1, Pallas kernels: 8.79 us -> 12.9 us  [make_gram(): pl.pallas_call(functools.partial(gram_kernel, scale), in_specs=[pl.BlockS...]
  transfers between devices with their start and end apart: 4 -> 5, of which waited for: 3 -> 4; matrix products, arithmetic and copies ran while one was open for 1% -> 2% of each run, Pallas kernels for 0% -> 0%
where the time goes in v2:
time: 246 us; the launch traced here: 245 us
  waiting for transfers between devices  125 us (51%)
  blocking collectives  47.2 us (19%)
  starting transfers between devices  28.5 us (12%)
  Pallas kernels  23.8 us (10%)
  between operations  14.1 us (6%)
  local copies, waits for them, and re-layouts  4.56 us (2%)
    all_gather x1, waiting for transfers between devices, per_device(): emb = lax.all_gather(embeddings, LINE, axis=1, tiled=True)  63.2 us
    all_gather x1, waiting for transfers between devices, per_device(): features = lax.all_gather(mine, LINE, axis=0, tiled=True)  54.1 us
    all_to_all x1, blocking collectives, per_device(): parts = lax.all_to_all(parts, PLANE, 0, 0, tiled=True)  25 us
    all_to_all x1, blocking collectives, per_device(): land = lax.all_to_all(spread, PLANE, 0, 0, tiled=True)  22.2 us
    ppermute x1, starting transfers between devices, per_device(): came = lax.ppermute(sent, 'zh', [(0, 1), (1, 0)])  16.3 us
    pallas_call x1, Pallas kernels, make_gram(): pl.pallas_call(functools.partial(gram_kernel, scale), in_specs=[pl.BlockS...  12.9 us
    pallas_call x1, Pallas kernels, make_features(): pl.pallas_call(features_kernel, grid=(slabs, steps), in_specs=[pl.BlockSp...  10.9 us
    ppermute x1, starting transfers between devices, per_device(): other = lax.ppermute(pairs, 'zh', [(0, 1), (1, 0)])  7.38 us
  transfers between devices with their start and end apart: 5, of which 4 were waited for; matrix products, arithmetic and copies ran while one was open for 2% of the time, Pallas kernels for 0%

profile of v2, /device:TPU:1, one launch (start us, length us, event | category | flops | bytes accessed | tf_op | source)
XLA Modules:
  0.0 245.1 jit_solution(5088089757995757179)
XLA Ops:
  7.2 0.0 all-gather.3.cloned.1.call-start
  7.2 0.7 all-gather.3.cloned.1.call-update
  7.9 0.0 all-gather.5.cloned.1.call-start
  8.0 0.9 reverse_select_fusion
  8.9 16.3 %collective-permute-start = (bf16[128,128]{1,0:T(8,128)(2,1)S(1)}, bf16[128,128]{1,0:T(8,128)(2,1)S(1)}, u32[]{:S(2)}, u32[]{:S(2)}) collective-permute-start(bf16[128,128]{1,0:T(8,128)(2,1)S(1)} %get-tuple-element.3), channel_id=1, source_target_pairs={{0,16},{16,0},{1,17},{17,1},{2,18},{18,2},{3,19},{19,3},{4,20},{20... | collective-permute-start | bytes 98312 | tf_op jit(solution)/shard_map/ppermute | solution.py:164
  25.2 1.4 collective-permute-done
  26.6 0.1 broadcast_in_dim.4
  26.7 22.2 %all_to_all.17 = bf16[16,128,256]{2,1,0:T(8,128)(2,1)S(1)} all-to-all(bf16[16,128,256]{2,1,0:T(8,128)(2,1)S(1)} %broadcast_in_dim.4), channel_id=1, replica_groups=mesh['y'=4,'x'=4,'zh'=2,'zl'=8,'c'=2] {'y','x'}, dimensions={0} | all-to-all | bytes 2097152 | tf_op jit(solution)/shard_map/all_to_all | solution.py:167
  48.9 1.2 copy.12
  50.1 63.2 %all-gather.3.cloned.1.call-done.emb_ref = bf16[512,8192]{1,0:T(8,128)(2,1)} async-done(((bf16[512,256]{1,0:T(8,128)(2,1)}), bf16[512,8192]{1,0:T(8,128)(2,1)}) %all-gather.3.cloned.1.call-update) | async-done | bytes 8388624 | tf_op jit(solution)/shard_map/all_gather | solution.py:159
  113.3 0.0 copy-start.2
  113.3 0.0 copy-start.1
  113.3 10.9 %shard_map.59 = bf16[128,1024]{1,0:T(8,128)(2,1)} custom-call(bf16[512,8192]{1,0:T(8,128)(2,1)} %all-gather.3.cloned.1.call-done.emb_ref, bf16[128,4096]{1,0:T(8,128)(2,1)} %bitcast.18), custom_call_target="tpu_custom_call" | custom-call | flops 1073741824 | bytes 8388608 | tf_op jit(solution)/shard_map/pallas_call | solution.py:51
  124.1 0.0 all-gather.5.cloned.1.call-update
  124.2 0.0 copy-done.2
  124.2 0.6 broadcast_in_dim.5
  124.8 4.8 %all-to-all-start.1 = ((f32[16,1,256]{2,1,0:T(1,128)}), f32[16,1,256]{2,1,0:T(1,128)S(1)}, u32[]{:S(2)}, u32[]{:S(2)}) async-start(f32[16,1,256]{2,1,0:T(1,128)} %broadcast_in_dim.5), calls=%async_computation.1 | async-start | bytes 32768 | tf_op jit(solution)/shard_map/all_to_all | solution.py:171
  129.6 0.0 copy-done.1
  129.6 7.4 %collective-permute-start.1 = (s32[2,1024]{1,0:T(2,128)S(1)}, s32[2,1024]{1,0:T(2,128)S(1)}, u32[]{:S(2)}, u32[]{:S(2)}) collective-permute-start(s32[2,1024]{1,0:T(2,128)S(1)} %copy-done.1), channel_id=1, source_target_pairs={{0,16},{16,0},{1,17},{17,1},{2,18},{18,2},{3,19},{19,3},{4,20},{20... | collective-permute-start | bytes 24584 | tf_op jit(solution)/shard_map/ppermute | solution.py:174
  137.0 0.6 pad_add_fusion.1.at_ref
  137.6 5.3 %collective-permute-done.1 = s32[2,1024]{1,0:T(2,128)S(1)} collective-permute-done((s32[2,1024]{1,0:T(2,128)S(1)}, s32[2,1024]{1,0:T(2,128)S(1)}, u32[]{:S(2)}, u32[]{:S(2)}) %collective-permute-start.1) | collective-permute-done | bytes 8224 | tf_op jit(solution)/shard_map/ppermute | solution.py:174
  142.9 0.0 copy-start
  142.9 1.4 copy.11
  144.3 0.0 all-to-all-done.1
  144.3 0.6 copy.10
  144.9 54.1 %all-gather.5.cloned.1.call-done.feat_ref = bf16[4096,1024]{1,0:T(8,128)(2,1)} async-done(((bf16[128,1024]{1,0:T(8,128)(2,1)}), bf16[4096,1024]{1,0:T(8,128)(2,1)}) %all-gather.5.cloned.1.call-update) | async-done | bytes 8388624 | tf_op jit(solution)/shard_map/all_gather | solution.py:181
  199.0 0.0 copy-done
  199.0 12.9 %shard_map.60 = bf16[16,144,256]{2,1,0:T(8,128)(2,1)} custom-call(s32[2]{0:T(128)} %pad_add_fusion.1.at_ref, bf16[4096,1024]{1,0:T(8,128)(2,1)} %all-gather.5.cloned.1.call-done.feat_ref, f32[1,4096]{1,0:T(1,128)} %bitcast.21, s32[8,2,256]{2,1,0:T(2,128)} %copy-done, s32[8,256,2]{2,1,0:T(8,128)} %bitcast.20), custom_call_target="tpu_custom_call" | custom-call | flops 2147483648 | bytes 8388608 | tf_op jit(solution)/shard_map/pallas_call | solution.py:138
  211.9 25.0 %all_to_all.18 = bf16[16,144,256]{2,1,0:T(8,128)(2,1)S(1)} all-to-all(bf16[16,144,256]{2,1,0:T(8,128)(2,1)} %shard_map.60), channel_id=1, replica_groups=mesh['y'=4,'x'=4,'zh'=2,'zl'=8,'c'=2] {'y','x'}, dimensions={0} | all-to-all | bytes 2359296 | tf_op jit(solution)/shard_map/all_to_all | solution.py:184
  236.9 0.2 convert_reduce_fusion
  237.1 0.6 slice_add_fusion
  237.6 0.7 slice.32
  (6 shorter events, 0.1 us)
Async XLA Ops:
  7.2 106.1 %all-gather.3.cloned.1.call-start = ((), (), s32[]{:S(2)}) async-start(), calls=%async_computation.3 | async-start | bytes 8650752 | tf_op jit(solution)/shard_map/all_gather | solution.py:159
  7.9 191.1 %all-gather.5.cloned.1.call-start = ((), (), s32[]{:S(2)}) async-start(), calls=%async_computation.4 | async-start | bytes 8650752 | tf_op jit(solution)/shard_map/all_gather | solution.py:181
  8.9 17.7 %collective-permute-start = (bf16[128,128]{1,0:T(8,128)(2,1)S(1)}, bf16[128,128]{1,0:T(8,128)(2,1)S(1)}, u32[]{:S(2)}, u32[]{:S(2)}) collective-permute-start(bf16[128,128]{1,0:T(8,128)(2,1)S(1)} %get-tuple-element.3), channel_id=1, source_target_pairs={{0,16},{16,0},{1,17},{17,1},{2,18},{18,2},{3,19},{19,3},{4,20},{20... | collective-permute-start | bytes 98312 | tf_op jit(solution)/shard_map/ppermute | solution.py:164
  113.3 10.9 %copy-start.2 = (f32[256]{0:T(256)S(1)}, f32[256]{0:T(256)}, u32[]{:S(2)}) copy-start(f32[256]{0:T(256)} %param.6) | copy-start | bytes 3076
  113.3 16.3 %copy-start.1 = (s32[2,1024]{1,0:T(2,128)S(1)}, s32[2,1024]{1,0:T(2,128)}, u32[]{:S(2)}) copy-start(s32[2,1024]{1,0:T(2,128)} %param.7) | copy-start | bytes 24580
  124.8 19.5 %all-to-all-start.1 = ((f32[16,1,256]{2,1,0:T(1,128)}), f32[16,1,256]{2,1,0:T(1,128)S(1)}, u32[]{:S(2)}, u32[]{:S(2)}) async-start(f32[16,1,256]{2,1,0:T(1,128)} %broadcast_in_dim.5), calls=%async_computation.1 | async-start | bytes 32768 | tf_op jit(solution)/shard_map/all_to_all | solution.py:171
  129.6 13.2 %collective-permute-start.1 = (s32[2,1024]{1,0:T(2,128)S(1)}, s32[2,1024]{1,0:T(2,128)S(1)}, u32[]{:S(2)}, u32[]{:S(2)}) collective-permute-start(s32[2,1024]{1,0:T(2,128)S(1)} %copy-done.1), channel_id=1, source_target_pairs={{0,16},{16,0},{1,17},{17,1},{2,18},{18,2},{3,19},{19,3},{4,20},{20... | collective-permute-start | bytes 24584 | tf_op jit(solution)/shard_map/ppermute | solution.py:174
  142.9 56.1 %copy-start = (s32[8,2,256]{2,1,0:T(2,128)}, s32[8,2,256]{2,1,0:T(2,128)S(1)}, u32[]{:S(2)}) copy-start(s32[8,2,256]{2,1,0:T(2,128)S(1)} %reshape.67.row_ref) | copy-start | bytes 49156
Sparse Core Ops, SparseCore 0:
  10.0 103.1 all-gather.2
  124.3 74.6 all-gather.4

commit v3 on v2

v3 whole, which is shorter than its diff:
```python
import functools
import math

import jax
import jax.numpy as jnp
from jax import lax
from jax.experimental import pallas as pl
from jax.experimental.pallas import tpu as pltpu
from jax.sharding import Mesh, PartitionSpec as P

EMBED_WIDTH = 4096
BLOCK_ROWS = 128
BETA = 0.5 * math.sqrt(EMBED_WIDTH)
LINE = ("zh", "zl", "c")
PLANE = ("y", "x")
NT = (((1,), (1,)), ((), ()))


def features_kernel(emb_ref, land_ref, alpha_ref, out_ref, score_ref, acc, resp_sq, land_sq):
    step = pl.program_id(1)
    chunks, _, width = emb_ref.shape

    @pl.when(step == 0)
    def _():
        acc[...] = jnp.zeros_like(acc)
        resp_sq[...] = jnp.zeros_like(resp_sq)
        land_sq[...] = jnp.zeros_like(land_sq)

    total = acc[...]
    resp, land = resp_sq[...], land_sq[...]
    for j in range(chunks):
        cols = slice(j * width, (j + 1) * width)
        total += lax.dot_general(emb_ref[j], land_ref[:, cols], NT, preferred_element_type=jnp.float32)
        for at in range(0, width, 128):
            part = emb_ref[j, :, at : at + 128].astype(jnp.float32)
            resp += part * part
            part = land_ref[:, j * width + at : j * width + at + 128].astype(jnp.float32)
            land += part * part
    acc[...] = total
    resp_sq[...] = resp
    land_sq[...] = land

    @pl.when(step == pl.num_programs(1) - 1)
    def _():
        ones = jnp.ones((8, 128), jnp.float32)
        norm = lax.dot_general(
            ones, land_sq[...], NT, precision=lax.Precision.HIGHEST, preferred_element_type=jnp.float32
        )[0:1]
        square = jnp.sum(resp_sq[...], axis=1, keepdims=True)
        value = BETA * acc[...] * lax.rsqrt(square + 1e-06) * lax.rsqrt(norm + 1e-06)
        features = jnp.exp(value).T.astype(out_ref.dtype)
        out_ref[...] = features
        score_ref[...] = jnp.sum(features.astype(jnp.float32) * alpha_ref[...], axis=0, keepdims=True)


def make_features(emb, land, alpha, slabs):
    chunks, rows, part = emb.shape
    count, width = land.shape
    steps = 1
    tile = width // steps
    each = tile // part
    return pl.pallas_call(
        features_kernel,
        grid=(slabs, steps),
        in_specs=[
            pl.BlockSpec((each, rows, part), lambda s, k: (s * steps + k, 0, 0)),
            pl.BlockSpec((count, tile), lambda s, k: (0, k)),
            pl.BlockSpec((count, 1), lambda s, k: (0, 0)),
        ],
        out_specs=[
            pl.BlockSpec((count, rows), lambda s, k: (0, s)),
            pl.BlockSpec((1, rows), lambda s, k: (0, s)),
        ],
        out_shape=[
            jax.ShapeDtypeStruct((count, slabs * rows), jnp.bfloat16),
            jax.ShapeDtypeStruct((1, slabs * rows), jnp.float32),
        ],
        scratch_shapes=[
            pltpu.VMEM((rows, count), jnp.float32),
            pltpu.VMEM((rows, 128), jnp.float32),
            pltpu.VMEM((count, 128), jnp.float32),
        ],
        compiler_params=pltpu.CompilerParams(vmem_limit_bytes=60 * 1024 * 1024),
        cost_estimate=pl.CostEstimate(
            flops=2 * count * slabs * rows * width,
            bytes_accessed=2 * slabs * rows * width,
            transcendentals=count * slabs * rows,
        ),
    )(emb, land, alpha)


def gram_kernel(scale, at_ref, feat_ref, score_ref, row_ref, col_ref, out_ref, own_ref, half_ref, v_ref, sems):
    half, own = at_ref[0], at_ref[1]
    count, responses = feat_ref.shape
    blocks = responses // BLOCK_ROWS
    pairs = 2 * BLOCK_ROWS
    slab_blocks = blocks // 2
    copies = []
    for k in range(2):
        rows = pl.ds(pl.multiple_of(k * (count // 2) + own * BLOCK_ROWS, BLOCK_ROWS), BLOCK_ROWS)
        copies.append(
            pltpu.make_async_copy(feat_ref.at[rows], own_ref.at[pl.ds(k * BLOCK_ROWS, BLOCK_ROWS)], sems.at[k])
        )
    rows = pl.ds(pl.multiple_of(half * (count // 2), BLOCK_ROWS), count // 2)
    copies.append(pltpu.make_async_copy(feat_ref.at[rows], half_ref, sems.at[2]))
    for copy in copies:
        copy.start()
    scores = jnp.sum(score_ref[...], axis=0, keepdims=True)
    copies[0].wait()
    copies[1].wait()

    grad = jnp.zeros((1, pairs), jnp.float32)
    lane = lax.broadcasted_iota(jnp.int32, (pairs, BLOCK_ROWS), 1)
    sub = lax.broadcasted_iota(jnp.int32, (BLOCK_ROWS, pairs), 0)
    for b in range(blocks):
        base = (b % slab_blocks) * BLOCK_ROWS
        cols = slice(b * BLOCK_ROWS, (b + 1) * BLOCK_ROWS)
        select = jnp.where(col_ref[b, :, 0:1] - base == lane, 1.0, 0.0) - jnp.where(
            col_ref[b, :, 1:2] - base == lane, 1.0, 0.0
        )
        margin = jnp.sum(select * scores[:, cols], axis=1, keepdims=True)
        prob = 1.0 / (1.0 + jnp.exp(-margin))
        weight = prob * (1.0 - prob) * scale
        diffs = lax.dot_general(
            select.astype(jnp.bfloat16), own_ref[:, cols], NT, preferred_element_type=jnp.float32
        )
        diffs = diffs.astype(jnp.bfloat16).astype(jnp.float32)
        weighted = (diffs * weight).astype(jnp.bfloat16)
        grad += jnp.sum(diffs * ((1.0 - prob) * scale), axis=0, keepdims=True)
        back = jnp.where(row_ref[b, 0:1, :] - base == sub, 1.0, 0.0) - jnp.where(
            row_ref[b, 1:2, :] - base == sub, 1.0, 0.0
        )
        v = jnp.dot(back.astype(jnp.bfloat16), weighted, preferred_element_type=jnp.float32)
        v_high = v.astype(jnp.bfloat16)
        v_ref[cols, 0:pairs] = v_high
        v_ref[cols, pairs : 2 * pairs] = (v - v_high.astype(jnp.float32)).astype(jnp.bfloat16)

    grad_high = grad.astype(jnp.bfloat16).astype(jnp.float32)
    tail_row = lax.broadcasted_iota(jnp.int32, (16, pairs), 0)
    tail = jnp.where(tail_row == 0, grad_high, jnp.where(tail_row == 1, grad - grad_high, 0.0))
    tail = tail.astype(jnp.bfloat16)
    copies[2].wait()
    for d in range(0, out_ref.shape[0], 2):
        part = jnp.dot(
            half_ref[d * BLOCK_ROWS : (d + 2) * BLOCK_ROWS, :], v_ref[...], preferred_element_type=jnp.float32
        )
        part = (part[:, 0:pairs] + part[:, pairs:]).astype(jnp.bfloat16)
        for k in range(2):
            out_ref[d + k, 0:BLOCK_ROWS, :] = part[k * BLOCK_ROWS : (k + 1) * BLOCK_ROWS]
            out_ref[d + k, BLOCK_ROWS:, :] = tail


def make_gram(at, features, scores, row_pairs, col_pairs, scale, owners):
    count, responses = features.shape
    vmem = pl.BlockSpec(memory_space=pltpu.VMEM)
    return pl.pallas_call(
        functools.partial(gram_kernel, scale),
        in_specs=[
            pl.BlockSpec(memory_space=pltpu.SMEM),
            pl.BlockSpec(memory_space=pl.ANY),
            vmem,
            vmem,
            vmem,
        ],
        out_specs=vmem,
        out_shape=jax.ShapeDtypeStruct((owners, BLOCK_ROWS + 16, 2 * BLOCK_ROWS), jnp.bfloat16),
        scratch_shapes=[
            pltpu.VMEM((2 * BLOCK_ROWS, responses), jnp.bfloat16),
            pltpu.VMEM((count // 2, responses), jnp.bfloat16),
            pltpu.VMEM((responses, 4 * BLOCK_ROWS), jnp.bfloat16),
            pltpu.SemaphoreType.DMA((3,)),
        ],
        compiler_params=pltpu.CompilerParams(vmem_limit_bytes=60 * 1024 * 1024),
        cost_estimate=pl.CostEstimate(
            flops=2 * count * responses * 256, bytes_accessed=count * responses, transcendentals=2048
        ),
    )(at, features, scores, row_pairs, col_pairs)


def per_device(embeddings, landmarks, alpha, pairs):
    rows, pair_count = embeddings.shape[0], pairs.shape[1]
    planes = lax.axis_size(PLANE)
    slabs = lax.axis_size("zh")
    scale = 1.0 / math.sqrt(pair_count * slabs * planes)
    zh = lax.axis_index("zh")
    own = lax.axis_index(("zl", "c"))

    emb = lax.all_gather(embeddings, LINE)

    half = landmarks.shape[0] // slabs
    halves = landmarks.reshape(slabs, half, landmarks.shape[1])
    kept, sent = jnp.where(zh == 0, halves, halves[::-1])
    came = lax.ppermute(sent, "zh", [(0, 1), (1, 0)])
    part = jnp.where(zh == 0, jnp.concatenate([kept, came], axis=1), jnp.concatenate([came, kept], axis=1))
    spread = jnp.broadcast_to(part[None], (planes,) + part.shape).reshape(planes * half, -1)
    land = lax.all_to_all(spread, PLANE, 0, 0, tiled=True)
    land = land.reshape(planes, half, -1).transpose(1, 0, 2).reshape(half, -1)

    other = lax.ppermute(pairs, "zh", [(0, 1), (1, 0)])
    both = jnp.where(zh == 0, jnp.stack([pairs, other]), jnp.stack([other, pairs]))
    blocks = slabs * rows // BLOCK_ROWS
    row_pairs = both.reshape(slabs, 2, blocks // slabs, -1).transpose(0, 2, 1, 3).reshape(blocks, 2, -1)
    col_pairs = row_pairs.transpose(0, 2, 1)

    own_alpha = jnp.where(zh == 0, alpha[:half], alpha[half:])[:, None]
    mine, score = make_features(emb, land, own_alpha, slabs)
    features = lax.all_gather(mine, LINE, axis=0, tiled=True)
    line = lax.axis_size(LINE)
    scores = lax.all_to_all(jnp.broadcast_to(score, (line, score.shape[1])), LINE, 0, 0, tiled=True)
    at = jnp.stack([zh, own]).astype(jnp.int32)
    parts = make_gram(at, features, scores, row_pairs, col_pairs, scale, planes)
    parts = lax.all_to_all(parts, PLANE, 0, 0, tiled=True)
    total = jnp.sum(parts.astype(jnp.float32), axis=0)
    return total[:BLOCK_ROWS], total[BLOCK_ROWS] + total[BLOCK_ROWS + 1]


def solution(mesh):
    fine = Mesh(mesh.devices.reshape(4, 4, 2, 8, 2), ("y", "x", "zh", "zl", "c"))
    dp, land = ("y", "x", "zh"), ("zl", "c")
    return jax.shard_map(
        per_device,
        mesh=fine,
        in_specs=(P(dp, land), P(land, dp), P(land), P(None, dp)),
        out_specs=(P(dp, land), P(land)),
        check_vma=False,
    )
```

time: 246 us -> 225 us (0.915)
  blocking collectives: 47.2 us -> 24.9 us
  starting transfers between devices: 28.5 us -> 37.4 us
  Pallas kernels: 23.8 us -> 15.4 us
  local copies, waits for them, and re-layouts: 4.56 us -> 7.23 us
    all_to_all x1 -> x2, waiting for transfers between devices: 0.01 us -> 30.4 us  [the longest x1 16 us: per_device(): lax.all_to_all(jnp.broadcast_to(score, (line, score.shape[1])), LINE, 0,...]
    all_to_all x1 -> x0, blocking collectives: 22.2 us -> none  [per_device(): land = lax.all_to_all(spread, PLANE, 0, 0, tiled=True)]
    all_gather x1, waiting for transfers between devices: 63.2 us -> 44.5 us  [per_device(): emb = lax.all_gather(embeddings, LINE)]
    all_to_all x1 -> x2, starting transfers between devices: 4.78 us -> 13.4 us  [the longest x1 6.75 us: per_device(): land = lax.all_to_all(spread, PLANE, 0, 0, tiled=True)]
    all_gather x1, waiting for transfers between devices: 54.1 us -> 46.2 us  [per_device(): features = lax.all_gather(mine, LINE, axis=0, tiled=True)]
    ppermute x1, waiting for transfers between devices: 5.27 us -> 0.01 us  [per_device(): other = lax.ppermute(pairs, 'zh', [(0, 1), (1, 0)])]
    pallas_call x1, Pallas kernels: 12.9 us -> 7.93 us  [make_gram(): pl.pallas_call(functools.partial(gram_kernel, scale), in_specs=[pl.BlockS...]
    pallas_call x1, Pallas kernels: 10.9 us -> 7.49 us  [make_features(): pl.pallas_call(features_kernel, grid=(slabs, steps), in_specs=[pl.BlockSp...]
  transfers between devices with their start and end apart: 5 -> 6, of which waited for: 4 -> 5; matrix products, arithmetic and copies ran while one was open for 2% -> 4% of each run, Pallas kernels for 0% -> 0%
where the time goes in v3:
time: 225 us
  waiting for transfers between devices  123 us (55%)
  starting transfers between devices  37.4 us (17%)
  blocking collectives  24.9 us (11%)
  Pallas kernels  15.4 us (7%)
  between operations  14.2 us (6%)
  local copies, waits for them, and re-layouts  7.23 us (3%)
  other arithmetic  2.35 us (1%)
    all_gather x1, waiting for transfers between devices, per_device(): features = lax.all_gather(mine, LINE, axis=0, tiled=True)  46.2 us
    all_gather x1, waiting for transfers between devices, per_device(): emb = lax.all_gather(embeddings, LINE)  44.5 us
    all_to_all x1, blocking collectives, per_device(): parts = lax.all_to_all(parts, PLANE, 0, 0, tiled=True)  24.9 us
    ppermute x1, starting transfers between devices, per_device(): came = lax.ppermute(sent, 'zh', [(0, 1), (1, 0)])  16.3 us
    all_to_all x1, waiting for transfers between devices, per_device(): lax.all_to_all(jnp.broadcast_to(score, (line, score.shape[1])), LINE, 0,...  16 us
    all_to_all x1, waiting for transfers between devices, per_device(): land = lax.all_to_all(spread, PLANE, 0, 0, tiled=True)  14.5 us
    pallas_call x1, Pallas kernels, make_gram(): pl.pallas_call(functools.partial(gram_kernel, scale), in_specs=[pl.BlockS...  7.93 us
    ppermute x1, starting transfers between devices, per_device(): other = lax.ppermute(pairs, 'zh', [(0, 1), (1, 0)])  7.69 us
  transfers between devices with their start and end apart: 6, of which 5 were waited for; matrix products, arithmetic and copies ran while one was open for 4% of the time, Pallas kernels for 0%

profile of v3, /device:TPU:1, one launch (start us, length us, event | category | flops | bytes accessed | tf_op | source)
XLA Modules:
  0.0 224.8 jit_solution(11664019762742554094)
XLA Ops:
  7.2 0.0 copy-start.2
  7.2 0.0 all-gather.6.cloned.1.call-start
  7.2 0.7 all-gather.6.cloned.1.call-update
  7.9 0.9 reverse_select_fusion
  8.9 16.3 %collective-permute-start = (bf16[128,128]{1,0:T(8,128)(2,1)S(1)}, bf16[128,128]{1,0:T(8,128)(2,1)S(1)}, u32[]{:S(2)}, u32[]{:S(2)}) collective-permute-start(bf16[128,128]{1,0:T(8,128)(2,1)S(1)} %get-tuple-element.7), channel_id=1, source_target_pairs={{0,16},{16,0},{1,17},{17,1},{2,18},{18,2},{3,19},{19,3},{4,20},{20... | collective-permute-start | bytes 98312 | tf_op jit(solution)/shard_map/ppermute | solution.py:193
  25.2 1.4 collective-permute-done
  26.6 1.2 broadcast_in_dim.6
  27.7 6.8 %all-to-all-start = ((bf16[16,128,256]{2,1,0:T(8,128)(2,1)}), bf16[16,128,256]{2,1,0:T(8,128)(2,1)S(1)}, u32[]{:S(2)}, u32[]{:S(2)}) async-start(bf16[16,128,256]{2,1,0:T(8,128)(2,1)} %broadcast_in_dim.6), calls=%async_computation | async-start | bytes 2097152 | tf_op jit(solution)/shard_map/all_to_all | solution.py:196
  34.5 0.0 all-gather.4.cloned.1.call-start
  34.5 0.0 copy-done.2
  34.6 0.7 copy.11.alpha_ref
  35.3 14.5 %all-to-all-done = bf16[16,128,256]{2,1,0:T(8,128)(2,1)S(1)} async-done(((bf16[16,128,256]{2,1,0:T(8,128)(2,1)}), bf16[16,128,256]{2,1,0:T(8,128)(2,1)S(1)}, u32[]{:S(2)}, u32[]{:S(2)}) %all-to-all-start) | async-done | bytes 1048608 | tf_op jit(solution)/shard_map/all_to_all | solution.py:196
  49.8 1.2 copy.14
  50.9 44.5 %all-gather.6.cloned.1.call-done = bf16[16384,256]{1,0:T(8,128)(2,1)} async-done(((bf16[512,256]{1,0:T(8,128)(2,1)}), bf16[16384,256]{1,0:T(8,128)(2,1)}) %all-gather.6.cloned.1.call-update) | async-done | bytes 8388624 | tf_op jit(solution)/shard_map/all_gather | solution.py:188
  95.5 0.0 copy-start.1
  95.5 7.5 %shard_map.59 = (bf16[128,1024]{1,0:T(8,128)(2,1)}, f32[1,1024]{1,0:T(1,128)}) custom-call(bf16[32,512,256]{2,1,0:T(8,128)(2,1)} %bitcast.21, bf16[128,4096]{1,0:T(8,128)(2,1)} %bitcast.22, f32[128,1]{1,0:T(8,128)} %copy.11.alpha_ref), custom_call_target="tpu_custom_call" | custom-call | flops 1073741824 | bytes 8388608 | tf_op jit(solution)/shard_map/pallas_call | solution.py:62
  103.0 0.0 all-gather.4.cloned.1.call-update
  103.0 0.0 copy-done.1
  103.0 7.7 %collective-permute-start.1 = (s32[2,1024]{1,0:T(2,128)S(1)}, s32[2,1024]{1,0:T(2,128)S(1)}, u32[]{:S(2)}, u32[]{:S(2)}) collective-permute-start(s32[2,1024]{1,0:T(2,128)S(1)} %copy-done.1), channel_id=1, source_target_pairs={{0,16},{16,0},{1,17},{17,1},{2,18},{18,2},{3,19},{19,3},{4,20},{20... | collective-permute-start | bytes 24584 | tf_op jit(solution)/shard_map/ppermute | solution.py:199
  110.7 1.4 broadcast_in_dim.16
  112.1 6.6 %all-to-all-start.1 = ((f32[32,1,1024]{2,1,0:T(1,128)}), f32[32,1,1024]{2,1,0:T(1,128)S(1)}, u32[]{:S(2)}, u32[]{:S(2)}) async-start(f32[32,1,1024]{2,1,0:T(1,128)} %broadcast_in_dim.16), calls=%async_computation.1 | async-start | bytes 262144 | tf_op jit(solution)/shard_map/all_to_all | solution.py:209
  118.8 0.6 pad_add_fusion.1.at_ref
  119.4 0.0 collective-permute-done.1
  119.5 0.0 copy-start
  119.5 1.4 copy.12
  120.9 16.0 %all-to-all-done.1 = f32[32,1,1024]{2,1,0:T(1,128)S(1)} async-done(((f32[32,1,1024]{2,1,0:T(1,128)}), f32[32,1,1024]{2,1,0:T(1,128)S(1)}, u32[]{:S(2)}, u32[]{:S(2)}) %all-to-all-start.1) | async-done | bytes 131104 | tf_op jit(solution)/shard_map/all_to_all | solution.py:209
  136.8 0.7 copy.16
  137.5 46.2 %all-gather.4.cloned.1.call-done.feat_ref = bf16[4096,1024]{1,0:T(8,128)(2,1)} async-done(((bf16[128,1024]{1,0:T(8,128)(2,1)}), bf16[4096,1024]{1,0:T(8,128)(2,1)}) %all-gather.4.cloned.1.call-update) | async-done | bytes 8388624 | tf_op jit(solution)/shard_map/all_gather | solution.py:207
  183.7 0.0 copy-done
  183.7 7.9 %shard_map.60 = bf16[16,144,256]{2,1,0:T(8,128)(2,1)} custom-call(s32[2]{0:T(128)} %pad_add_fusion.1.at_ref, bf16[4096,1024]{1,0:T(8,128)(2,1)} %all-gather.4.cloned.1.call-done.feat_ref, f32[32,1024]{1,0:T(8,128)} %bitcast.25, s32[8,2,256]{2,1,0:T(2,128)} %copy-done, s32[8,256,2]{2,1,0:T(8,128)} %bitcast.24), custom_call_target="tpu_custom_call" | custom-call | flops 2147483648 | bytes 4194304 | tf_op jit(solution)/shard_map/pallas_call | solution.py:156
  191.7 24.9 %all_to_all.19 = bf16[16,144,256]{2,1,0:T(8,128)(2,1)S(1)} all-to-all(bf16[16,144,256]{2,1,0:T(8,128)(2,1)} %shard_map.60), channel_id=1, replica_groups=mesh['y'=4,'x'=4,'zh'=2,'zl'=8,'c'=2] {'y','x'}, dimensions={0} | all-to-all | bytes 2359296 | tf_op jit(solution)/shard_map/all_to_all | solution.py:212
  216.5 0.2 convert_reduce_fusion
  216.7 0.6 slice_add_fusion
  217.3 0.7 slice.40
  (7 shorter events, 0.1 us)
Async XLA Ops:
  7.2 27.4 %copy-start.2 = (f32[256]{0:T(256)S(1)}, f32[256]{0:T(256)}, u32[]{:S(2)}) copy-start(f32[256]{0:T(256)} %param.6) | copy-start | bytes 3076
  7.2 88.3 %all-gather.6.cloned.1.call-start = ((), (), s32[]{:S(2)}) async-start(), calls=%async_computation.4 | async-start | bytes 8650752 | tf_op jit(solution)/shard_map/all_gather | solution.py:188
  8.9 17.7 %collective-permute-start = (bf16[128,128]{1,0:T(8,128)(2,1)S(1)}, bf16[128,128]{1,0:T(8,128)(2,1)S(1)}, u32[]{:S(2)}, u32[]{:S(2)}) collective-permute-start(bf16[128,128]{1,0:T(8,128)(2,1)S(1)} %get-tuple-element.7), channel_id=1, source_target_pairs={{0,16},{16,0},{1,17},{17,1},{2,18},{18,2},{3,19},{19,3},{4,20},{20... | collective-permute-start | bytes 98312 | tf_op jit(solution)/shard_map/ppermute | solution.py:193
  27.7 22.0 %all-to-all-start = ((bf16[16,128,256]{2,1,0:T(8,128)(2,1)}), bf16[16,128,256]{2,1,0:T(8,128)(2,1)S(1)}, u32[]{:S(2)}, u32[]{:S(2)}) async-start(bf16[16,128,256]{2,1,0:T(8,128)(2,1)} %broadcast_in_dim.6), calls=%async_computation | async-start | bytes 2097152 | tf_op jit(solution)/shard_map/all_to_all | solution.py:196
  34.5 149.2 %all-gather.4.cloned.1.call-start = ((), (), s32[]{:S(2)}) async-start(), calls=%async_computation.3 | async-start | bytes 8650752 | tf_op jit(solution)/shard_map/all_gather | solution.py:207
  95.5 7.5 %copy-start.1 = (s32[2,1024]{1,0:T(2,128)S(1)}, s32[2,1024]{1,0:T(2,128)}, u32[]{:S(2)}) copy-start(s32[2,1024]{1,0:T(2,128)} %param.7) | copy-start | bytes 24580
  103.0 16.4 %collective-permute-start.1 = (s32[2,1024]{1,0:T(2,128)S(1)}, s32[2,1024]{1,0:T(2,128)S(1)}, u32[]{:S(2)}, u32[]{:S(2)}) collective-permute-start(s32[2,1024]{1,0:T(2,128)S(1)} %copy-done.1), channel_id=1, source_target_pairs={{0,16},{16,0},{1,17},{17,1},{2,18},{18,2},{3,19},{19,3},{4,20},{20... | collective-permute-start | bytes 24584 | tf_op jit(solution)/shard_map/ppermute | solution.py:199
  112.1 24.7 %all-to-all-start.1 = ((f32[32,1,1024]{2,1,0:T(1,128)}), f32[32,1,1024]{2,1,0:T(1,128)S(1)}, u32[]{:S(2)}, u32[]{:S(2)}) async-start(f32[32,1,1024]{2,1,0:T(1,128)} %broadcast_in_dim.16), calls=%async_computation.1 | async-start | bytes 262144 | tf_op jit(solution)/shard_map/all_to_all | solution.py:209
  119.5 64.3 %copy-start = (s32[8,2,256]{2,1,0:T(2,128)}, s32[8,2,256]{2,1,0:T(2,128)S(1)}, u32[]{:S(2)}) copy-start(s32[8,2,256]{2,1,0:T(2,128)S(1)} %reshape.58.row_ref) | copy-start | bytes 49156
Sparse Core Ops, SparseCore 0:
  10.1 85.2 all-gather.5
  103.1 80.5 all-gather.3

commit v4 on v3

v4 whole, which is shorter than its diff:
```python
import functools
import math

import jax
import jax.numpy as jnp
from jax import lax
from jax.experimental import pallas as pl
from jax.experimental.pallas import tpu as pltpu
from jax.sharding import Mesh, PartitionSpec as P

EMBED_WIDTH = 4096
BLOCK_ROWS = 128
BETA = 0.5 * math.sqrt(EMBED_WIDTH)
RING = ("zh", "zm", "c")
PLANE = ("y", "x")
NT = (((1,), (1,)), ((), ()))


def features_kernel(emb_ref, land_ref, alpha_ref, out_ref, score_ref):
    chunks, rows, width = emb_ref.shape
    count = land_ref.shape[1]
    total = jnp.zeros((rows, count), jnp.float32)
    resp = jnp.zeros((rows, 128), jnp.float32)
    land = jnp.zeros((count, 128), jnp.float32)
    for j in range(chunks):
        zm, c, zp = j // 4, j // 2 % 2, j % 2
        at = zm * 4 + zp * 2 + c
        total += lax.dot_general(emb_ref[j], land_ref[at], NT, preferred_element_type=jnp.float32)
        for lane in range(0, width, 128):
            part = emb_ref[j, :, lane : lane + 128].astype(jnp.float32)
            resp += part * part
            part = land_ref[at, :, lane : lane + 128].astype(jnp.float32)
            land += part * part
    ones = jnp.ones((8, 128), jnp.float32)
    norm = lax.dot_general(ones, land, NT, precision=lax.Precision.HIGHEST, preferred_element_type=jnp.float32)[0:1]
    square = jnp.sum(resp, axis=1, keepdims=True)
    value = BETA * total * lax.rsqrt(square + 1e-06) * lax.rsqrt(norm + 1e-06)
    features = jnp.exp(value).T.astype(out_ref.dtype)
    out_ref[...] = features
    score_ref[...] = jnp.sum(features.astype(jnp.float32) * alpha_ref[...], axis=0, keepdims=True)


def make_features(emb, land, alpha, slabs):
    chunks, rows, part = emb.shape
    count = land.shape[1]
    each = chunks // slabs
    return pl.pallas_call(
        features_kernel,
        grid=(slabs,),
        in_specs=[
            pl.BlockSpec((each, rows, part), lambda s: (s, 0, 0)),
            pl.BlockSpec(land.shape, lambda s: (0, 0, 0)),
            pl.BlockSpec((count, 1), lambda s: (0, 0)),
        ],
        out_specs=[
            pl.BlockSpec((count, rows), lambda s: (0, s)),
            pl.BlockSpec((1, rows), lambda s: (0, s)),
        ],
        out_shape=[
            jax.ShapeDtypeStruct((count, slabs * rows), jnp.bfloat16),
            jax.ShapeDtypeStruct((1, slabs * rows), jnp.float32),
        ],
        compiler_params=pltpu.CompilerParams(vmem_limit_bytes=60 * 1024 * 1024),
        cost_estimate=pl.CostEstimate(
            flops=2 * count * chunks * rows * part,
            bytes_accessed=2 * chunks * rows * part,
            transcendentals=count * slabs * rows,
        ),
    )(emb, land, alpha)


def gram_kernel(scale, at_ref, feat_ref, score_ref, row_ref, col_ref, out_ref, own_ref, half_ref, v_ref, sems):
    half, own = at_ref[0], at_ref[1]
    count, responses = feat_ref.shape
    blocks = responses // BLOCK_ROWS
    pairs = 2 * BLOCK_ROWS
    wide = 4 * BLOCK_ROWS
    copies = []
    for k in range(4):
        zp, zh = k // 2, k % 2
        rows = pl.ds(
            pl.multiple_of(zh * (count // 2) + own * pairs + zp * BLOCK_ROWS, BLOCK_ROWS), BLOCK_ROWS
        )
        copies.append(
            pltpu.make_async_copy(feat_ref.at[rows], own_ref.at[pl.ds(k * BLOCK_ROWS, BLOCK_ROWS)], sems.at[k])
        )
    rows = pl.ds(pl.multiple_of(half * (count // 2), BLOCK_ROWS), count // 2)
    copies.append(pltpu.make_async_copy(feat_ref.at[rows], half_ref, sems.at[4]))
    for copy in copies:
        copy.start()
    scores = jnp.sum(score_ref[...], axis=0, keepdims=True)
    for copy in copies[:4]:
        copy.wait()

    grad = jnp.zeros((1, wide), jnp.float32)
    lane = lax.broadcasted_iota(jnp.int32, (pairs, BLOCK_ROWS), 1)
    sub = lax.broadcasted_iota(jnp.int32, (BLOCK_ROWS, pairs), 0)
    for b in range(blocks):
        cols = slice(b * BLOCK_ROWS, (b + 1) * BLOCK_ROWS)
        select = jnp.where(col_ref[b, :, 0:1] == lane, 1.0, 0.0) - jnp.where(col_ref[b, :, 1:2] == lane, 1.0, 0.0)
        margin = jnp.sum(select * scores[:, cols], axis=1, keepdims=True)
        prob = 1.0 / (1.0 + jnp.exp(-margin))
        weight = prob * (1.0 - prob) * scale
        diffs = lax.dot_general(
            select.astype(jnp.bfloat16), own_ref[:, cols], NT, preferred_element_type=jnp.float32
        )
        diffs = diffs.astype(jnp.bfloat16).astype(jnp.float32)
        weighted = (diffs * weight).astype(jnp.bfloat16)
        grad += jnp.sum(diffs * ((1.0 - prob) * scale), axis=0, keepdims=True)
        back = jnp.where(row_ref[b, 0:1, :] == sub, 1.0, 0.0) - jnp.where(row_ref[b, 1:2, :] == sub, 1.0, 0.0)
        v = jnp.dot(back.astype(jnp.bfloat16), weighted, preferred_element_type=jnp.float32)
        v_high = v.astype(jnp.bfloat16)
        v_ref[cols, 0:wide] = v_high
        v_ref[cols, wide : 2 * wide] = (v - v_high.astype(jnp.float32)).astype(jnp.bfloat16)

    grad_high = grad.astype(jnp.bfloat16).astype(jnp.float32)
    tail_row = lax.broadcasted_iota(jnp.int32, (16, wide), 0)
    tail = jnp.where(tail_row == 0, grad_high, jnp.where(tail_row == 1, grad - grad_high, 0.0))
    tail = tail.astype(jnp.bfloat16)
    copies[4].wait()
    for e in range(0, count // 2 // BLOCK_ROWS, 2):
        part = jnp.dot(
            half_ref[e * BLOCK_ROWS : (e + 2) * BLOCK_ROWS, :], v_ref[...], preferred_element_type=jnp.float32
        )
        part = (part[:, 0:wide] + part[:, wide:]).astype(jnp.bfloat16)
        for zp in range(2):
            d = e // 4 * 4 + zp * 2 + e // 2 % 2
            for k in range(2):
                cols = slice(k * pairs, (k + 1) * pairs)
                out_ref[2 * d + k, 0:BLOCK_ROWS, :] = part[zp * BLOCK_ROWS : (zp + 1) * BLOCK_ROWS, cols]
                out_ref[2 * d + k, BLOCK_ROWS:, :] = tail[:, cols]


def make_gram(at, features, scores, row_pairs, col_pairs, scale, owners):
    count, responses = features.shape
    vmem = pl.BlockSpec(memory_space=pltpu.VMEM)
    return pl.pallas_call(
        functools.partial(gram_kernel, scale),
        in_specs=[
            pl.BlockSpec(memory_space=pltpu.SMEM),
            pl.BlockSpec(memory_space=pl.ANY),
            vmem,
            vmem,
            vmem,
        ],
        out_specs=vmem,
        out_shape=jax.ShapeDtypeStruct((owners, BLOCK_ROWS + 16, 2 * BLOCK_ROWS), jnp.bfloat16),
        scratch_shapes=[
            pltpu.VMEM((4 * BLOCK_ROWS, responses), jnp.bfloat16),
            pltpu.VMEM((count // 2, responses), jnp.bfloat16),
            pltpu.VMEM((responses, 8 * BLOCK_ROWS), jnp.bfloat16),
            pltpu.SemaphoreType.DMA((5,)),
        ],
        compiler_params=pltpu.CompilerParams(vmem_limit_bytes=60 * 1024 * 1024),
        cost_estimate=pl.CostEstimate(
            flops=2 * count * responses * 512, bytes_accessed=count * responses, transcendentals=1024
        ),
    )(at, features, scores, row_pairs, col_pairs)


def swap(value, axis):
    return lax.ppermute(value, axis, [(0, 1), (1, 0)])


def in_order(index, mine, other):
    return jnp.where(index == 0, jnp.stack([mine, other]), jnp.stack([other, mine]))


def per_device(embeddings, landmarks, alpha, pairs):
    rows, pair_count = embeddings.shape[0], pairs.shape[1]
    planes = lax.axis_size(PLANE)
    slabs = lax.axis_size("zh")
    scale = 1.0 / math.sqrt(pair_count * slabs * planes)
    zh, zp = lax.axis_index("zh"), lax.axis_index("zp")

    low, high = embeddings[: rows // 2], embeddings[rows // 2 :]
    kept, sent = jnp.where(zp == 0, low, high), jnp.where(zp == 0, high, low)
    emb = lax.all_gather(in_order(zp, kept, swap(sent, "zp")), RING)
    emb = emb.reshape((-1,) + emb.shape[-2:])

    half = landmarks.shape[0] // slabs
    low, high = landmarks[:half], landmarks[half:]
    kept, sent = jnp.where(zh == 0, low, high), jnp.where(zh == 0, high, low)
    part = in_order(zh, kept, swap(sent, "zh")).transpose(1, 0, 2).reshape(half, -1)
    part = in_order(zp, part, swap(part, "zp")).reshape(2 * half, -1)
    land = lax.all_to_all(jnp.broadcast_to(part[None], (planes,) + part.shape), PLANE, 0, 0, tiled=True)

    own_alpha = jnp.where(zh == 0, alpha[:half], alpha[half:])
    own_alpha = in_order(zp, own_alpha, swap(own_alpha, "zp")).reshape(-1, 1)

    blocks = rows // BLOCK_ROWS
    local = pairs.reshape(2, blocks, -1) - BLOCK_ROWS * jnp.arange(blocks, dtype=pairs.dtype)[None, :, None]
    local = jnp.where(zp == 0, local[:, : blocks // 2], local[:, blocks // 2 :]).transpose(1, 0, 2)
    row_pairs = in_order(zh, local, swap(local, "zh")).reshape(blocks, 2, -1)
    col_pairs = row_pairs.transpose(0, 2, 1)

    mine, score = make_features(emb, land, own_alpha, slabs)
    features = lax.all_gather(mine, RING, axis=0, tiled=True)
    ring = lax.axis_size(RING)
    scores = lax.all_to_all(jnp.broadcast_to(score, (ring, score.shape[1])), RING, 0, 0, tiled=True)
    at = jnp.stack([zh, lax.axis_index(("zm", "c"))]).astype(jnp.int32)
    parts = make_gram(at, features, scores, row_pairs, col_pairs, scale, 2 * planes)
    parts = lax.all_to_all(parts, PLANE + ("zp",), 0, 0, tiled=True)
    total = jnp.sum(parts.astype(jnp.float32), axis=0)
    return total[:BLOCK_ROWS], total[BLOCK_ROWS] + total[BLOCK_ROWS + 1]


def solution(mesh):
    fine = Mesh(mesh.devices.reshape(4, 4, 2, 4, 2, 2), ("y", "x", "zh", "zm", "zp", "c"))
    dp, land = ("y", "x", "zh"), ("zm", "zp", "c")
    return jax.shard_map(
        per_device,
        mesh=fine,
        in_specs=(P(dp, land), P(land, dp), P(land), P(None, dp)),
        out_specs=(P(dp, land), P(land)),
        check_vma=False,
    )
```

time: 225 us -> 212 us (0.942)
  waiting for transfers between devices: 123 us -> 90.1 us
  blocking collectives: 24.9 us -> 36.9 us
  starting transfers between devices: 37.4 us -> 46.9 us
    all_gather x2, waiting for transfers between devices: 90.7 us -> 48.7 us  [the longest x1 33.2 us: per_device(): features = lax.all_gather(mine, RING, axis=0, tiled=True)]
    all_to_all x1, blocking collectives: 24.9 us -> 36.9 us  [per_device(): parts = lax.all_to_all(parts, PLANE + ('zp',), 0, 0, tiled=True)]
    ppermute x2 -> x5, starting transfers between devices: 24 us -> 32.7 us  [swap(): return lax.ppermute(value, axis, [(0, 1), (1, 0)])]
    ppermute x2 -> x5, waiting for transfers between devices: 1.4 us -> 9.27 us  [swap(): return lax.ppermute(value, axis, [(0, 1), (1, 0)])]
    reshape x3 -> x0, local copies, waits for them, and re-layouts: 2.56 us -> none  [the longest x2 1.39 us: per_device(): both.reshape(slabs, 2, blocks // slabs, -1).transpose(0, 2, 1, 3)]
  transfers between devices with their start and end apart: 6 -> 9, of which waited for: 5 -> 8; matrix products, arithmetic and copies ran while one was open for 4% -> 3% of each run, Pallas kernels for 0% -> 0%
where the time goes in v4:
time: 212 us
  waiting for transfers between devices  90.1 us (42%)
  starting transfers between devices  46.9 us (22%)
  blocking collectives  36.9 us (17%)
  between operations  14.2 us (7%)
  Pallas kernels  13.3 us (6%)
  local copies, waits for them, and re-layouts  7.12 us (3%)
  other arithmetic  3.41 us (2%)
    all_to_all x1, blocking collectives, per_device(): parts = lax.all_to_all(parts, PLANE + ('zp',), 0, 0, tiled=True)  36.9 us
    all_gather x1, waiting for transfers between devices, per_device(): features = lax.all_gather(mine, RING, axis=0, tiled=True)  33.2 us
    ppermute x5, starting transfers between devices, swap(): return lax.ppermute(value, axis, [(0, 1), (1, 0)])  32.7 us
    all_to_all x1, waiting for transfers between devices, per_device(): lax.all_to_all(jnp.broadcast_to(part[None], (planes,) + part.shape), PLAN...  17.6 us
    all_gather x1, waiting for transfers between devices, per_device(): emb = lax.all_gather(in_order(zp, kept, swap(sent, 'zp')), RING)  15.5 us
    all_to_all x1, waiting for transfers between devices, per_device(): lax.all_to_all(jnp.broadcast_to(score, (ring, score.shape[1])), RING, 0,...  14.5 us
    ppermute x5, waiting for transfers between devices, swap(): return lax.ppermute(value, axis, [(0, 1), (1, 0)])  9.27 us
    pallas_call x1, Pallas kernels, make_gram(): pl.pallas_call(functools.partial(gram_kernel, scale), in_specs=[pl.BlockS...  7.41 us
  transfers between devices with their start and end apart: 9, of which 8 were waited for; matrix products, arithmetic and copies ran while one was open for 3% of the time, Pallas kernels for 0%

profile of v4, /device:TPU:1, one launch (start us, length us, event | category | flops | bytes accessed | tf_op | source)
XLA Modules:
  0.0 211.8 jit_solution(3845045641346694193)
XLA Ops:
  7.2 0.0 all-gather.3.cloned.1.call-start
  7.2 1.0 select_bitcast_fusion
  8.2 4.4 %collective-permute-start = (bf16[256,256]{1,0:T(8,128)(2,1)S(1)}, bf16[256,256]{1,0:T(8,128)(2,1)S(1)}, u32[]{:S(2)}, u32[]{:S(2)}) collective-permute-start(bf16[256,256]{1,0:T(8,128)(2,1)S(1)} %get-tuple-element.7), channel_id=1, source_target_pairs={{0,2},{2,0},{1,3},{3,1},{4,6},{6,4},{5,7},{7,5},{8,10},{10,8},{9,1... | collective-permute-start | bytes 393224 | tf_op jit(solution)/shard_map/ppermute | solution.py:162
  12.6 2.3 %collective-permute-done = bf16[256,256]{1,0:T(8,128)(2,1)S(1)} collective-permute-done((bf16[256,256]{1,0:T(8,128)(2,1)S(1)}, bf16[256,256]{1,0:T(8,128)(2,1)S(1)}, u32[]{:S(2)}, u32[]{:S(2)}) %collective-permute-start) | collective-permute-done | bytes 131104 | tf_op jit(solution)/shard_map/ppermute | solution.py:162
  14.9 0.7 maximum_select_fusion
  15.7 0.0 all-gather.3.cloned.1.call-update
  15.7 0.8 fusion.2
  16.5 0.1 copy.26
  16.6 0.1 copy.27
  16.8 15.8 %collective-permute-start.1 = (bf16[128,128]{0,1:T(8,128)(2,1)S(1)}, bf16[128,128]{0,1:T(8,128)(2,1)S(1)}, u32[]{:S(2)}, u32[]{:S(2)}) collective-permute-start(bf16[128,128]{0,1:T(8,128)(2,1)S(1)} %get-tuple-element.9), channel_id=1, source_target_pairs={{0,16},{16,0},{1,17},{17,1},{2,18},{18,2},{3,19},{19,3},{4,20},{20... | collective-permute-start | bytes 98312 | tf_op jit(solution)/shard_map/ppermute | solution.py:162
  32.6 1.4 collective-permute-done.1
  34.0 2.5 %collective-permute-start.2 = (bf16[128,256]{0,1:T(8,128)(2,1)S(1)}, bf16[128,256]{0,1:T(8,128)(2,1)S(1)}, u32[]{:S(2)}, u32[]{:S(2)}) collective-permute-start(bf16[128,256]{0,1:T(8,128)(2,1)S(1)} %bitcast.39), channel_id=1, source_target_pairs={{0,2},{2,0},{1,3},{3,1},{4,6},{6,4},{5,7},{7,5},{8,10},{10,8},{9,1... | collective-permute-start | bytes 196616 | tf_op jit(solution)/shard_map/ppermute | solution.py:162
  36.5 2.9 %collective-permute-done.2 = bf16[128,256]{0,1:T(8,128)(2,1)S(1)} collective-permute-done((bf16[128,256]{0,1:T(8,128)(2,1)S(1)}, bf16[128,256]{0,1:T(8,128)(2,1)S(1)}, u32[]{:S(2)}, u32[]{:S(2)}) %collective-permute-start.2) | collective-permute-done | bytes 65568 | tf_op jit(solution)/shard_map/ppermute | solution.py:162
  39.5 0.1 copy.21
  39.6 1.6 broadcast_in_dim.4
  41.2 0.0 copy-start.3
  41.2 6.9 %all-to-all-start = ((bf16[16,256,256]{2,1,0:T(8,128)(2,1)}), bf16[16,256,256]{2,1,0:T(8,128)(2,1)S(1)}, u32[]{:S(2)}, u32[]{:S(2)}) async-start(bf16[16,256,256]{2,1,0:T(8,128)(2,1)} %broadcast_in_dim.4), calls=%async_computation | async-start | bytes 4194304 | tf_op jit(solution)/shard_map/all_to_all | solution.py:186
  48.0 0.0 all-gather.5.cloned.1.call-start
  48.1 0.0 copy-done.3
  48.1 2.1 collective-permute-start.3
  50.2 2.6 %collective-permute-done.3 = f32[128]{0:T(128)S(1)} collective-permute-done((f32[128]{0:T(128)S(1)}, f32[128]{0:T(128)S(1)}, u32[]{:S(2)}, u32[]{:S(2)}) %collective-permute-start.3) | collective-permute-done | bytes 544 | tf_op jit(solution)/shard_map/ppermute | solution.py:162
  52.8 0.8 copy.22.alpha_ref
  53.6 17.6 %all-to-all-done.land_ref = bf16[16,256,256]{2,1,0:T(8,128)(2,1)S(1)} async-done(((bf16[16,256,256]{2,1,0:T(8,128)(2,1)}), bf16[16,256,256]{2,1,0:T(8,128)(2,1)S(1)}, u32[]{:S(2)}, u32[]{:S(2)}) %all-to-all-start) | async-done | bytes 2097184 | tf_op jit(solution)/shard_map/all_to_all | solution.py:186
  71.2 0.0 copy-start
  71.2 15.5 %all-gather.3.cloned.1.call-done = bf16[16,2,256,256]{3,2,1,0:T(8,128)(2,1)} async-done(((bf16[1,2,256,256]{3,2,1,0:T(8,128)(2,1)}), bf16[16,2,256,256]{3,2,1,0:T(8,128)(2,1)}) %all-gather.3.cloned.1.call-update) | async-done | bytes 4194320 | tf_op jit(solution)/shard_map/all_gather | solution.py:178
  86.7 0.0 copy-done
  86.7 0.0 copy-start.2
  86.7 5.9 %shard_map.59 = (bf16[256,512]{1,0:T(8,128)(2,1)}, f32[1,512]{1,0:T(1,128)}) custom-call(bf16[32,256,256]{2,1,0:T(8,128)(2,1)} %bitcast.35, bf16[16,256,256]{2,1,0:T(8,128)(2,1)} %copy-done, f32[256,1]{1,0:T(8,128)} %copy.22.alpha_ref), custom_call_target="tpu_custom_call" | custom-call | flops 1073741824 | bytes 4194304 | tf_op jit(solution)/shard_map/pallas_call | solution.py:47
  92.5 0.0 all-gather.5.cloned.1.call-update
  92.6 0.0 copy-done.2
  92.6 0.1 broadcast_subtract_fusion
  92.7 7.9 %collective-permute-start.4 = (s32[2,2,256]{2,1,0:T(2,128)S(1)}, s32[2,2,256]{2,1,0:T(2,128)S(1)}, u32[]{:S(2)}, u32[]{:S(2)}) collective-permute-start(s32[2,2,256]{2,1,0:T(2,128)S(1)} %get-tuple-element.13), channel_id=1, source_target_pairs={{0,16},{16,0},{1,17},{17,1},{2,18},{18,2},{3,19},{19,3},{4,20},{20... | collective-permute-start | bytes 12296 | tf_op jit(solution)/shard_map/ppermute | solution.py:162
  100.5 1.3 broadcast_in_dim.5
  101.9 7.2 %all-to-all-start.1 = ((f32[16,1,512]{2,1,0:T(1,128)}), f32[16,1,512]{2,1,0:T(1,128)S(1)}, u32[]{:S(2)}, u32[]{:S(2)}) async-start(f32[16,1,512]{2,1,0:T(1,128)} %broadcast_in_dim.5), calls=%async_computation.1 | async-start | bytes 65536 | tf_op jit(solution)/shard_map/all_to_all | solution.py:200
  109.1 0.6 pad_add_fusion.at_ref
  109.7 0.0 collective-permute-done.4
  109.8 0.2 copy.23
  110.0 0.0 copy-start.1
  110.0 0.8 copy.24.row_ref
  110.8 14.5 %all-to-all-done.1 = f32[16,1,512]{2,1,0:T(1,128)S(1)} async-done(((f32[16,1,512]{2,1,0:T(1,128)}), f32[16,1,512]{2,1,0:T(1,128)S(1)}, u32[]{:S(2)}, u32[]{:S(2)}) %all-to-all-start.1) | async-done | bytes 32800 | tf_op jit(solution)/shard_map/all_to_all | solution.py:200
  125.3 0.6 copy.29
  125.9 33.2 %all-gather.5.cloned.1.call-done.feat_ref = bf16[4096,512]{1,0:T(8,128)(2,1)} async-done(((bf16[256,512]{1,0:T(8,128)(2,1)}), bf16[4096,512]{1,0:T(8,128)(2,1)}) %all-gather.5.cloned.1.call-update) | async-done | bytes 4194320 | tf_op jit(solution)/shard_map/all_gather | solution.py:198
  159.2 0.0 copy-done.1
  159.2 7.4 %shard_map.60 = bf16[32,144,256]{2,1,0:T(8,128)(2,1)} custom-call(s32[2]{0:T(128)} %pad_add_fusion.at_ref, bf16[4096,512]{1,0:T(8,128)(2,1)} %all-gather.5.cloned.1.call-done.feat_ref, f32[16,512]{1,0:T(8,128)} %bitcast.43, s32[4,2,256]{2,1,0:T(2,128)} %copy.24.row_ref, s32[4,256,2]{2,1,0:T(8,128)} %bitcast.37), custom_call_target="tpu_custom_call" | custom-call | flops 2147483648 | bytes 2097152 | tf_op jit(solution)/shard_map/pallas_call | solution.py:137
  166.6 36.9 %all_to_all.18 = bf16[32,144,256]{2,1,0:T(8,128)(2,1)S(1)} all-to-all(bf16[32,144,256]{2,1,0:T(8,128)(2,1)} %shard_map.60), channel_id=1, replica_groups=mesh['y'=4,'x'=4,'zh'=2,'zm'=4,'zp'=2,'c'=2] {'y','x','zp'}, dimensions={0} | all-to-all | bytes 4718592 | tf_op jit(solution)/shard_map/all_to_all | solution.py:203
  203.5 0.3 convert_reduce_fusion
  203.8 0.7 slice.46
  204.4 0.6 slice_add_fusion
  (9 shorter events, 0.1 us)
Async XLA Ops:
  7.2 79.5 %all-gather.3.cloned.1.call-start = ((), (), s32[]{:S(2)}) async-start(), calls=%async_computation.3 | async-start | bytes 4456448 | tf_op jit(solution)/shard_map/all_gather | solution.py:178
  8.2 6.7 %collective-permute-start = (bf16[256,256]{1,0:T(8,128)(2,1)S(1)}, bf16[256,256]{1,0:T(8,128)(2,1)S(1)}, u32[]{:S(2)}, u32[]{:S(2)}) collective-permute-start(bf16[256,256]{1,0:T(8,128)(2,1)S(1)} %get-tuple-element.7), channel_id=1, source_target_pairs={{0,2},{2,0},{1,3},{3,1},{4,6},{6,4},{5,7},{7,5},{8,10},{10,8},{9,1... | collective-permute-start | bytes 393224 | tf_op jit(solution)/shard_map/ppermute | solution.py:162
  16.8 17.2 %collective-permute-start.1 = (bf16[128,128]{0,1:T(8,128)(2,1)S(1)}, bf16[128,128]{0,1:T(8,128)(2,1)S(1)}, u32[]{:S(2)}, u32[]{:S(2)}) collective-permute-start(bf16[128,128]{0,1:T(8,128)(2,1)S(1)} %get-tuple-element.9), channel_id=1, source_target_pairs={{0,16},{16,0},{1,17},{17,1},{2,18},{18,2},{3,19},{19,3},{4,20},{20... | collective-permute-start | bytes 98312 | tf_op jit(solution)/shard_map/ppermute | solution.py:162
  34.0 5.5 %collective-permute-start.2 = (bf16[128,256]{0,1:T(8,128)(2,1)S(1)}, bf16[128,256]{0,1:T(8,128)(2,1)S(1)}, u32[]{:S(2)}, u32[]{:S(2)}) collective-permute-start(bf16[128,256]{0,1:T(8,128)(2,1)S(1)} %bitcast.39), channel_id=1, source_target_pairs={{0,2},{2,0},{1,3},{3,1},{4,6},{6,4},{5,7},{7,5},{8,10},{10,8},{9,1... | collective-permute-start | bytes 196616 | tf_op jit(solution)/shard_map/ppermute | solution.py:162
  41.2 6.9 %copy-start.3 = (f32[256]{0:T(256)S(1)}, f32[256]{0:T(256)}, u32[]{:S(2)}) copy-start(f32[256]{0:T(256)} %param.6) | copy-start | bytes 3076
  41.2 30.1 %all-to-all-start = ((bf16[16,256,256]{2,1,0:T(8,128)(2,1)}), bf16[16,256,256]{2,1,0:T(8,128)(2,1)S(1)}, u32[]{:S(2)}, u32[]{:S(2)}) async-start(bf16[16,256,256]{2,1,0:T(8,128)(2,1)} %broadcast_in_dim.4), calls=%async_computation | async-start | bytes 4194304 | tf_op jit(solution)/shard_map/all_to_all | solution.py:186
  48.0 111.1 %all-gather.5.cloned.1.call-start = ((), (), s32[]{:S(2)}) async-start(), calls=%async_computation.4 | async-start | bytes 4456448 | tf_op jit(solution)/shard_map/all_gather | solution.py:198
  48.1 4.7 %collective-permute-start.3 = (f32[128]{0:T(128)S(1)}, f32[128]{0:T(128)S(1)}, u32[]{:S(2)}, u32[]{:S(2)}) collective-permute-start(f32[128]{0:T(128)S(1)} %broadcast_select_fusion.2), channel_id=1, source_target_pairs={{0,2},{2,0},{1,3},{3,1},{4,6},{6,4},{5,7},{7,5},{8,10},{10,8},{9,1... | collective-permute-start | bytes 1544 | tf_op jit(solution)/shard_map/ppermute | solution.py:162
  71.2 15.5 %copy-start = (bf16[16,256,256]{2,1,0:T(8,128)(2,1)}, bf16[16,256,256]{2,1,0:T(8,128)(2,1)S(1)}, u32[]{:S(2)}) copy-start(bf16[16,256,256]{2,1,0:T(8,128)(2,1)S(1)} %all-to-all-done.land_ref) | copy-start | bytes 6291460
  86.7 5.9 %copy-start.2 = (s32[2,1024]{1,0:T(2,128)S(1)}, s32[2,1024]{1,0:T(2,128)}, u32[]{:S(2)}) copy-start(s32[2,1024]{1,0:T(2,128)} %param.7) | copy-start | bytes 24580
  92.7 17.1 %collective-permute-start.4 = (s32[2,2,256]{2,1,0:T(2,128)S(1)}, s32[2,2,256]{2,1,0:T(2,128)S(1)}, u32[]{:S(2)}, u32[]{:S(2)}) collective-permute-start(s32[2,2,256]{2,1,0:T(2,128)S(1)} %get-tuple-element.13), channel_id=1, source_target_pairs={{0,16},{16,0},{1,17},{17,1},{2,18},{18,2},{3,19},{19,3},{4,20},{20... | collective-permute-start | bytes 12296 | tf_op jit(solution)/shard_map/ppermute | solution.py:162
  101.9 23.5 %all-to-all-start.1 = ((f32[16,1,512]{2,1,0:T(1,128)}), f32[16,1,512]{2,1,0:T(1,128)S(1)}, u32[]{:S(2)}, u32[]{:S(2)}) async-start(f32[16,1,512]{2,1,0:T(1,128)} %broadcast_in_dim.5), calls=%async_computation.1 | async-start | bytes 65536 | tf_op jit(solution)/shard_map/all_to_all | solution.py:200
  110.0 49.2 %copy-start.1 = (s32[2,2,2,256]{2,3,1,0:T(8,128)}, s32[2,2,2,256]{2,3,1,0:T(8,128)S(1)}, u32[]{:S(2)}) copy-start(s32[2,2,2,256]{2,3,1,0:T(8,128)S(1)} %copy.23) | copy-start | bytes 24580
Sparse Core Ops, SparseCore 0:
  15.8 70.8 all-gather.2
  92.7 66.4 all-gather.4

commit v5 on v4

--- a/solution.py
+++ b/solution.py
@@ -69,33 +69,14 @@
     )(emb, land, alpha)
 
 
-def gram_kernel(scale, at_ref, feat_ref, score_ref, row_ref, col_ref, out_ref, own_ref, half_ref, v_ref, sems):
-    half, own = at_ref[0], at_ref[1]
-    count, responses = feat_ref.shape
-    blocks = responses // BLOCK_ROWS
+def factor_kernel(scale, own_ref, score_ref, row_ref, col_ref, v_ref, tail_ref):
+    wide, responses = own_ref.shape
     pairs = 2 * BLOCK_ROWS
-    wide = 4 * BLOCK_ROWS
-    copies = []
-    for k in range(4):
-        zp, zh = k // 2, k % 2
-        rows = pl.ds(
-            pl.multiple_of(zh * (count // 2) + own * pairs + zp * BLOCK_ROWS, BLOCK_ROWS), BLOCK_ROWS
-        )
-        copies.append(
-            pltpu.make_async_copy(feat_ref.at[rows], own_ref.at[pl.ds(k * BLOCK_ROWS, BLOCK_ROWS)], sems.at[k])
-        )
-    rows = pl.ds(pl.multiple_of(half * (count // 2), BLOCK_ROWS), count // 2)
-    copies.append(pltpu.make_async_copy(feat_ref.at[rows], half_ref, sems.at[4]))
-    for copy in copies:
-        copy.start()
     scores = jnp.sum(score_ref[...], axis=0, keepdims=True)
-    for copy in copies[:4]:
-        copy.wait()
-
     grad = jnp.zeros((1, wide), jnp.float32)
     lane = lax.broadcasted_iota(jnp.int32, (pairs, BLOCK_ROWS), 1)
     sub = lax.broadcasted_iota(jnp.int32, (BLOCK_ROWS, pairs), 0)
-    for b in range(blocks):
+    for b in range(responses // BLOCK_ROWS):
         cols = slice(b * BLOCK_ROWS, (b + 1) * BLOCK_ROWS)
         select = jnp.where(col_ref[b, :, 0:1] == lane, 1.0, 0.0) - jnp.where(col_ref[b, :, 1:2] == lane, 1.0, 0.0)
         margin = jnp.sum(select * scores[:, cols], axis=1, keepdims=True)
@@ -113,49 +94,75 @@
         v_ref[cols, 0:wide] = v_high
         v_ref[cols, wide : 2 * wide] = (v - v_high.astype(jnp.float32)).astype(jnp.bfloat16)
 
-    grad_high = grad.astype(jnp.bfloat16).astype(jnp.float32)
-    tail_row = lax.broadcasted_iota(jnp.int32, (16, wide), 0)
-    tail = jnp.where(tail_row == 0, grad_high, jnp.where(tail_row == 1, grad - grad_high, 0.0))
-    tail = tail.astype(jnp.bfloat16)
-    copies[4].wait()
-    for e in range(0, count // 2 // BLOCK_ROWS, 2):
-        part = jnp.dot(
-            half_ref[e * BLOCK_ROWS : (e + 2) * BLOCK_ROWS, :], v_ref[...], preferred_element_type=jnp.float32
-        )
+    high = grad.astype(jnp.bfloat16).astype(jnp.float32)
+    low = grad - high
+    row = lax.broadcasted_iota(jnp.int32, (16, BLOCK_ROWS), 0)
+    for k in range(2):
+        left = slice(2 * k * BLOCK_ROWS, (2 * k + 1) * BLOCK_ROWS)
+        right = slice((2 * k + 1) * BLOCK_ROWS, (2 * k + 2) * BLOCK_ROWS)
+        tail = jnp.zeros((16, BLOCK_ROWS), jnp.float32)
+        for at, value in enumerate((high[:, left], high[:, right], low[:, left], low[:, right])):
+            tail = jnp.where(row == at, value, tail)
+        tail_ref[k] = tail.astype(jnp.bfloat16)
+
+
+def make_factor(own, scores, row_pairs, col_pairs, scale):
+    wide, responses = own.shape
+    vmem = pl.BlockSpec(memory_space=pltpu.VMEM)
+    return pl.pallas_call(
+        functools.partial(factor_kernel, scale),
+        in_specs=[vmem] * 4,
+        out_specs=[vmem, vmem],
+        out_shape=[
+            jax.ShapeDtypeStruct((responses, 2 * wide), jnp.bfloat16),
+            jax.ShapeDtypeStruct((2, 16, BLOCK_ROWS), jnp.bfloat16),
+        ],
+        compiler_params=pltpu.CompilerParams(vmem_limit_bytes=40 * 1024 * 1024),
+        cost_estimate=pl.CostEstimate(
+            flops=4 * 2 * responses * BLOCK_ROWS * wide, bytes_accessed=6 * wide * responses, transcendentals=1024
+        ),
+    )(own, scores, row_pairs, col_pairs)
+
+
+def gram_kernel(at_ref, feat_ref, v_ref, tail_ref, out_ref):
+    wide = v_ref.shape[1] // 2
+    step = 2 * BLOCK_ROWS
+    for c in range(2):
+        part = jnp.dot(feat_ref[c * step : (c + 1) * step, :], v_ref[...], preferred_element_type=jnp.float32)
         part = (part[:, 0:wide] + part[:, wide:]).astype(jnp.bfloat16)
         for zp in range(2):
-            d = e // 4 * 4 + zp * 2 + e // 2 % 2
             for k in range(2):
-                cols = slice(k * pairs, (k + 1) * pairs)
-                out_ref[2 * d + k, 0:BLOCK_ROWS, :] = part[zp * BLOCK_ROWS : (zp + 1) * BLOCK_ROWS, cols]
-                out_ref[2 * d + k, BLOCK_ROWS:, :] = tail[:, cols]
-
-
-def make_gram(at, features, scores, row_pairs, col_pairs, scale, owners):
+                for side in range(2):
+                    at = (2 * k + side) * BLOCK_ROWS
+                    out_ref[0, zp, c, k, side * BLOCK_ROWS : (side + 1) * BLOCK_ROWS, :] = part[
+                        zp * BLOCK_ROWS : (zp + 1) * BLOCK_ROWS, at : at + BLOCK_ROWS
+                    ]
+                out_ref[0, zp, c, k, 2 * BLOCK_ROWS :, :] = tail_ref[k]
+
+
+def make_gram(at, features, factor, tail, owners):
     count, responses = features.shape
-    vmem = pl.BlockSpec(memory_space=pltpu.VMEM)
-    return pl.pallas_call(
-        functools.partial(gram_kernel, scale),
-        in_specs=[
-            pl.BlockSpec(memory_space=pltpu.SMEM),
-            pl.BlockSpec(memory_space=pl.ANY),
-            vmem,
-            vmem,
-            vmem,
-        ],
-        out_specs=vmem,
-        out_shape=jax.ShapeDtypeStruct((owners, BLOCK_ROWS + 16, 2 * BLOCK_ROWS), jnp.bfloat16),
-        scratch_shapes=[
-            pltpu.VMEM((4 * BLOCK_ROWS, responses), jnp.bfloat16),
-            pltpu.VMEM((count // 2, responses), jnp.bfloat16),
-            pltpu.VMEM((responses, 8 * BLOCK_ROWS), jnp.bfloat16),
-            pltpu.SemaphoreType.DMA((5,)),
-        ],
+    steps = owners // 8
+    rows = 2 * BLOCK_ROWS + 16
+    part = pl.pallas_call(
+        gram_kernel,
+        grid_spec=pltpu.PrefetchScalarGridSpec(
+            num_scalar_prefetch=1,
+            grid=(steps,),
+            in_specs=[
+                pl.BlockSpec((count // 2 // steps, responses), lambda n, at: (at[0] * steps + n, 0)),
+                pl.BlockSpec(factor.shape, lambda n, at: (0, 0)),
+                pl.BlockSpec(tail.shape, lambda n, at: (0, 0, 0)),
+            ],
+            out_specs=pl.BlockSpec((1, 2, 2, 2, rows, BLOCK_ROWS), lambda n, at: (n, 0, 0, 0, 0, 0)),
+        ),
+        out_shape=jax.ShapeDtypeStruct((steps, 2, 2, 2, rows, BLOCK_ROWS), jnp.bfloat16),
         compiler_params=pltpu.CompilerParams(vmem_limit_bytes=60 * 1024 * 1024),
         cost_estimate=pl.CostEstimate(
-            flops=2 * count * responses * 512, bytes_accessed=count * responses, transcendentals=1024
-        ),
-    )(at, features, scores, row_pairs, col_pairs)
+            flops=2 * count * responses * 512, bytes_accessed=count * responses, transcendentals=0
+        ),
+    )(at, features, factor, tail)
+    return part.reshape(owners, rows, BLOCK_ROWS)
 
 
 def swap(value, axis):
@@ -179,11 +186,14 @@
     emb = emb.reshape((-1,) + emb.shape[-2:])
 
     half = landmarks.shape[0] // slabs
-    low, high = landmarks[:half], landmarks[half:]
-    kept, sent = jnp.where(zh == 0, low, high), jnp.where(zh == 0, high, low)
-    part = in_order(zh, kept, swap(sent, "zh")).transpose(1, 0, 2).reshape(half, -1)
-    part = in_order(zp, part, swap(part, "zp")).reshape(2 * half, -1)
-    land = lax.all_to_all(jnp.broadcast_to(part[None], (planes,) + part.shape), PLANE, 0, 0, tiled=True)
+    part = in_order(zh, landmarks, swap(landmarks, "zh")).transpose(1, 0, 2).reshape(slabs * half, -1)
+    part = in_order(zp, part, swap(part, "zp"))
+    low, high = part[:, :half].reshape(2 * half, -1), part[:, half:].reshape(2 * half, -1)
+
+    def spread(part):
+        return lax.all_to_all(jnp.broadcast_to(part[None], (planes,) + part.shape), PLANE, 0, 0, tiled=True)
+
+    land = spread(jnp.where(zh == 0, low, high))
 
     own_alpha = jnp.where(zh == 0, alpha[:half], alpha[half:])
     own_alpha = in_order(zp, own_alpha, swap(own_alpha, "zp")).reshape(-1, 1)
@@ -198,11 +208,21 @@
     features = lax.all_gather(mine, RING, axis=0, tiled=True)
     ring = lax.axis_size(RING)
     scores = lax.all_to_all(jnp.broadcast_to(score, (ring, score.shape[1])), RING, 0, 0, tiled=True)
-    at = jnp.stack([zh, lax.axis_index(("zm", "c"))]).astype(jnp.int32)
-    parts = make_gram(at, features, scores, row_pairs, col_pairs, scale, 2 * planes)
+
+    ready = (score[0, 0] == score[0, 0]) | (zh < 0)
+    other_land = spread(jnp.where(ready, jnp.where(zh == 0, high, low), jnp.zeros_like(low)))
+    other, _ = make_features(emb, other_land, own_alpha, slabs)
+    own = in_order(zh, mine.reshape(2, half, -1), other.reshape(2, half, -1))
+    own = own.transpose(1, 0, 2, 3).reshape(4 * half, -1)
+    factor, tail = make_factor(own, scores, row_pairs, col_pairs, scale)
+
+    at = zh.astype(jnp.int32).reshape(1)
+    parts = make_gram(at, features, factor, tail, 2 * planes)
     parts = lax.all_to_all(parts, PLANE + ("zp",), 0, 0, tiled=True)
     total = jnp.sum(parts.astype(jnp.float32), axis=0)
-    return total[:BLOCK_ROWS], total[BLOCK_ROWS] + total[BLOCK_ROWS + 1]
+    gram = jnp.concatenate([total[:BLOCK_ROWS], total[BLOCK_ROWS : 2 * BLOCK_ROWS]], axis=1)
+    tail = total[2 * BLOCK_ROWS :]
+    return gram, jnp.concatenate([tail[0] + tail[2], tail[1] + tail[3]])
 
 
 def solution(mesh):

time: 212 us -> 224 us (1.057)
  Pallas kernels: 13.3 us -> 18.8 us
  local copies, waits for them, and re-layouts: 7.12 us -> 10.9 us
    all_gather x1, waiting for transfers between devices: 33.2 us -> 0.01 us  [per_device(): features = lax.all_gather(mine, RING, axis=0, tiled=True)]
    ppermute x5, waiting for transfers between devices: 9.27 us -> 32.7 us  [swap(): return lax.ppermute(value, axis, [(0, 1), (1, 0)])]
    all_to_all x1 -> x2, waiting for transfers between devices: 17.6 us -> 39.2 us  [spread(): lax.all_to_all(jnp.broadcast_to(part[None], (planes,) + part.shape), PLAN...]
    all_gather x1, waiting for transfers between devices: 15.5 us -> 4.65 us  [per_device(): emb = lax.all_gather(in_order(zp, kept, swap(sent, 'zp')), RING)]
    pallas_call x1 -> x2, Pallas kernels: 5.86 us -> 11.7 us  [make_features(): pl.pallas_call(features_kernel, grid=(slabs,), in_specs=[pl.BlockSpec((ea...]
    ppermute x5, starting transfers between devices: 32.7 us -> 26.9 us  [swap(): return lax.ppermute(value, axis, [(0, 1), (1, 0)])]
    all_to_all x1, starting transfers between devices: 7.25 us -> 11.2 us  [per_device(): lax.all_to_all(jnp.broadcast_to(score, (ring, score.shape[1])), RING, 0,...]
    all_to_all x1 -> x2, starting transfers between devices: 6.89 us -> 10.6 us  [spread(): lax.all_to_all(jnp.broadcast_to(part[None], (planes,) + part.shape), PLAN...]
  transfers between devices with their start and end apart: 9 -> 10, of which waited for: 8 -> 9; matrix products, arithmetic and copies ran while one was open for 3% -> 4% of each run, Pallas kernels for 0% -> 3%
where the time goes in v5:
time: 224 us; the launch traced here: 223 us
  waiting for transfers between devices  88.8 us (40%)
  starting transfers between devices  48.7 us (22%)
  blocking collectives  35.2 us (16%)
  Pallas kernels  18.8 us (8%)
  between operations  15.5 us (7%)
  local copies, waits for them, and re-layouts  10.9 us (5%)
  other arithmetic  4.55 us (2%)
    all_to_all x2, waiting for transfers between devices, spread(): lax.all_to_all(jnp.broadcast_to(part[None], (planes,) + part.shape), PLAN...  39.2 us
    all_to_all x1, blocking collectives, per_device(): parts = lax.all_to_all(parts, PLANE + ('zp',), 0, 0, tiled=True)  35.2 us
    ppermute x5, waiting for transfers between devices, swap(): return lax.ppermute(value, axis, [(0, 1), (1, 0)])  32.7 us
    ppermute x5, starting transfers between devices, swap(): return lax.ppermute(value, axis, [(0, 1), (1, 0)])  26.9 us
    all_to_all x1, waiting for transfers between devices, per_device(): lax.all_to_all(jnp.broadcast_to(score, (ring, score.shape[1])), RING, 0,...  12.2 us
    pallas_call x2, Pallas kernels, make_features(): pl.pallas_call(features_kernel, grid=(slabs,), in_specs=[pl.BlockSpec((ea...  11.7 us
    all_to_all x1, starting transfers between devices, per_device(): lax.all_to_all(jnp.broadcast_to(score, (ring, score.shape[1])), RING, 0,...  11.2 us
    all_to_all x2, starting transfers between devices, spread(): lax.all_to_all(jnp.broadcast_to(part[None], (planes,) + part.shape), PLAN...  10.6 us
  transfers between devices with their start and end apart: 10, of which 9 were waited for; matrix products, arithmetic and copies ran while one was open for 4% of the time, Pallas kernels for 3%

profile of v5, /device:TPU:1, one launch (start us, length us, event | category | flops | bytes accessed | tf_op | source)
XLA Modules:
  0.0 222.6 jit_solution(6968922364973334246)
XLA Ops:
  7.2 0.0 all-gather.3.cloned.1.call-start
  7.2 1.0 select_bitcast_fusion
  8.2 4.4 %collective-permute-start = (bf16[256,256]{1,0:T(8,128)(2,1)S(1)}, bf16[256,256]{1,0:T(8,128)(2,1)S(1)}, u32[]{:S(2)}, u32[]{:S(2)}) collective-permute-start(bf16[256,256]{1,0:T(8,128)(2,1)S(1)} %get-tuple-element.13), channel_id=1, source_target_pairs={{0,2},{2,0},{1,3},{3,1},{4,6},{6,4},{5,7},{7,5},{8,10},{10,8},{9,1... | collective-permute-start | bytes 393224 | tf_op jit(solution)/shard_map/ppermute | solution.py:169
  12.6 2.3 %collective-permute-done = bf16[256,256]{1,0:T(8,128)(2,1)S(1)} collective-permute-done((bf16[256,256]{1,0:T(8,128)(2,1)S(1)}, bf16[256,256]{1,0:T(8,128)(2,1)S(1)}, u32[]{:S(2)}, u32[]{:S(2)}) %collective-permute-start) | collective-permute-done | bytes 131104 | tf_op jit(solution)/shard_map/ppermute | solution.py:169
  14.9 0.7 maximum_select_fusion.1
  15.7 0.0 all-gather.3.cloned.1.call-update
  15.7 0.9 copy.34
  16.6 15.8 %collective-permute-start.1 = (bf16[256,128]{0,1:T(8,128)(2,1)S(1)}, bf16[256,128]{0,1:T(8,128)(2,1)S(1)}, u32[]{:S(2)}, u32[]{:S(2)}) collective-permute-start(bf16[256,128]{0,1:T(8,128)(2,1)S(1)} %copy.34), channel_id=1, source_target_pairs={{0,16},{16,0},{1,17},{17,1},{2,18},{18,2},{3,19},{19,3},{4,20},{20... | collective-permute-start | bytes 196616 | tf_op jit(solution)/shard_map/ppermute | solution.py:169
  32.4 1.7 collective-permute-done.1
  34.2 2.5 %collective-permute-start.2 = (bf16[256,256]{0,1:T(8,128)(2,1)S(1)}, bf16[256,256]{0,1:T(8,128)(2,1)S(1)}, u32[]{:S(2)}, u32[]{:S(2)}) collective-permute-start(bf16[256,256]{0,1:T(8,128)(2,1)S(1)} %bitcast.56), channel_id=1, source_target_pairs={{0,2},{2,0},{1,3},{3,1},{4,6},{6,4},{5,7},{7,5},{8,10},{10,8},{9,1... | collective-permute-start | bytes 393224 | tf_op jit(solution)/shard_map/ppermute | solution.py:169
  36.8 14.9 %collective-permute-done.2 = bf16[256,256]{0,1:T(8,128)(2,1)S(1)} collective-permute-done((bf16[256,256]{0,1:T(8,128)(2,1)S(1)}, bf16[256,256]{0,1:T(8,128)(2,1)S(1)}, u32[]{:S(2)}, u32[]{:S(2)}) %collective-permute-start.2) | collective-permute-done | bytes 131104 | tf_op jit(solution)/shard_map/ppermute | solution.py:169
  51.7 0.1 copy.36
  51.8 1.6 broadcast_in_dim.8
  53.4 6.7 %all-to-all-start = ((bf16[16,256,256]{2,1,0:T(8,128)(2,1)}), bf16[16,256,256]{2,1,0:T(8,128)(2,1)S(1)}, u32[]{:S(2)}, u32[]{:S(2)}) async-start(bf16[16,256,256]{2,1,0:T(8,128)(2,1)} %broadcast_in_dim.8), calls=%async_computation | async-start | bytes 4194304 | tf_op jit(solution)/shard_map/all_to_all | solution.py:194
  60.1 0.0 all-gather.5.cloned.1.call-start
  60.2 0.0 copy-done.6
  60.2 1.9 collective-permute-start.3
  62.1 2.7 %collective-permute-done.3 = f32[128]{0:T(128)S(1)} collective-permute-done((f32[128]{0:T(128)S(1)}, f32[128]{0:T(128)S(1)}, u32[]{:S(2)}, u32[]{:S(2)}) %collective-permute-start.3) | collective-permute-done | bytes 544 | tf_op jit(solution)/shard_map/ppermute | solution.py:169
  64.9 0.8 copy.37.alpha_ref
  65.7 19.9 %all-to-all-done.land_ref = bf16[16,256,256]{2,1,0:T(8,128)(2,1)S(1)} async-done(((bf16[16,256,256]{2,1,0:T(8,128)(2,1)}), bf16[16,256,256]{2,1,0:T(8,128)(2,1)S(1)}, u32[]{:S(2)}, u32[]{:S(2)}) %all-to-all-start) | async-done | bytes 2097184 | tf_op jit(solution)/shard_map/all_to_all | solution.py:194
  85.6 4.7 %all-gather.3.cloned.1.call-done = bf16[16,2,256,256]{3,2,1,0:T(8,128)(2,1)} async-done(((bf16[1,2,256,256]{3,2,1,0:T(8,128)(2,1)}), bf16[16,2,256,256]{3,2,1,0:T(8,128)(2,1)}) %all-gather.3.cloned.1.call-update) | async-done | bytes 4194320 | tf_op jit(solution)/shard_map/all_gather | solution.py:185
  90.3 5.9 %shard_map.59 = (bf16[256,512]{1,0:T(8,128)(2,1)}, f32[1,512]{1,0:T(1,128)}) custom-call(bf16[32,256,256]{2,1,0:T(8,128)(2,1)} %bitcast.52, bf16[16,256,256]{2,1,0:T(8,128)(2,1)} %copy-done.3, f32[256,1]{1,0:T(8,128)} %copy.37.alpha_ref), custom_call_target="tpu_custom_call" | custom-call | flops 1073741824 | bytes 4194304 | tf_op jit(solution)/shard_map/pallas_call | solution.py:47
  96.1 0.0 all-gather.5.cloned.1.call-update
  96.1 1.1 slice.57
  98.5 1.3 broadcast_in_dim.11
  99.8 11.2 %all-to-all-start.2 = ((f32[16,1,512]{2,1,0:T(1,128)}), f32[16,1,512]{2,1,0:T(1,128)S(1)}, u32[]{:S(2)}, u32[]{:S(2)}) async-start(f32[16,1,512]{2,1,0:T(1,128)} %broadcast_in_dim.11), calls=%async_computation.2 | async-start | bytes 65536 | tf_op jit(solution)/shard_map/all_to_all | solution.py:210
  111.1 0.1 copy.38
  111.2 12.2 %all-to-all-done.2 = f32[16,1,512]{2,1,0:T(1,128)S(1)} async-done(((f32[16,1,512]{2,1,0:T(1,128)}), f32[16,1,512]{2,1,0:T(1,128)S(1)}, u32[]{:S(2)}, u32[]{:S(2)}) %all-to-all-start.2) | async-done | bytes 32800 | tf_op jit(solution)/shard_map/all_to_all | solution.py:210
  123.3 1.6 broadcast_in_dim.10
  124.9 3.8 %all-to-all-start.1 = ((bf16[16,256,256]{2,1,0:T(8,128)(2,1)}), bf16[16,256,256]{2,1,0:T(8,128)(2,1)S(1)}, u32[]{:S(2)}, u32[]{:S(2)}) async-start(bf16[16,256,256]{2,1,0:T(8,128)(2,1)} %broadcast_in_dim.10), calls=%async_computation.1 | async-start | bytes 4194304 | tf_op jit(solution)/shard_map/all_to_all | solution.py:194
  128.8 0.1 broadcast_subtract_fusion
  128.9 2.2 %collective-permute-start.4 = (s32[2,2,256]{2,1,0:T(2,128)S(1)}, s32[2,2,256]{2,1,0:T(2,128)S(1)}, u32[]{:S(2)}, u32[]{:S(2)}) collective-permute-start(s32[2,2,256]{2,1,0:T(2,128)S(1)} %get-tuple-element.19), channel_id=1, source_target_pairs={{0,16},{16,0},{1,17},{17,1},{2,18},{18,2},{3,19},{19,3},{4,20},{20... | collective-permute-start | bytes 12296 | tf_op jit(solution)/shard_map/ppermute | solution.py:169
  131.1 11.0 %collective-permute-done.4 = s32[2,2,256]{2,1,0:T(2,128)S(1)} collective-permute-done((s32[2,2,256]{2,1,0:T(2,128)S(1)}, s32[2,2,256]{2,1,0:T(2,128)S(1)}, u32[]{:S(2)}, u32[]{:S(2)}) %collective-permute-start.4) | collective-permute-done | bytes 4128 | tf_op jit(solution)/shard_map/ppermute | solution.py:169
  142.2 0.2 copy.44
  142.4 0.2 copy.45.row_ref
  142.6 19.3 %all-to-all-done.1.land_ref = bf16[16,256,256]{2,1,0:T(8,128)(2,1)S(1)} async-done(((bf16[16,256,256]{2,1,0:T(8,128)(2,1)}), bf16[16,256,256]{2,1,0:T(8,128)(2,1)S(1)}, u32[]{:S(2)}, u32[]{:S(2)}) %all-to-all-start.1) | async-done | bytes 2097184 | tf_op jit(solution)/shard_map/all_to_all | solution.py:194
  161.9 1.4 copy-done.2
  163.3 5.9 %shard_map.60 = (bf16[256,512]{1,0:T(8,128)(2,1)}, f32[1,512]{1,0:T(1,128)}) custom-call(bf16[32,256,256]{2,1,0:T(8,128)(2,1)} %bitcast.53, bf16[16,256,256]{2,1,0:T(8,128)(2,1)} %copy-done.2, f32[256,1]{1,0:T(8,128)} %copy.37.alpha_ref), custom_call_target="tpu_custom_call" | custom-call | flops 1073741824 | bytes 4194304 | tf_op jit(solution)/shard_map/pallas_call | solution.py:47
  169.1 1.1 maximum_select_fusion
  170.2 1.4 shard_map.61
  171.7 0.0 copy-start
  171.7 1.0 copy-done
  172.7 0.6 copy-done.1
  173.3 5.6 %shard_map.62 = bf16[4,2,2,2,272,128]{5,4,3,2,1,0:T(8,128)(2,1)} custom-call(s32[1]{0:T(128)} %bitcast.at_ref, bf16[4096,512]{1,0:T(8,128)(2,1)} %all-gather.5.cloned.1.call-done.feat_ref, bf16[512,1024]{1,0:T(8,128)(2,1)} %copy-done, bf16[2,16,128]{2,1,0:T(8,128)(2,1)} %copy-done.1), custom_call_target="tpu_custom_call" | custom-call | flops 2147483648 | bytes 2097152 | tf_op jit(solution)/shard_map/pallas_call | solution.py:147
  178.9 35.2 %all_to_all.23 = bf16[32,272,128]{2,1,0:T(8,128)(2,1)S(1)} all-to-all(bf16[32,272,128]{2,1,0:T(8,128)(2,1)} %bitcast.54), channel_id=1, replica_groups=mesh['y'=4,'x'=4,'zh'=2,'zm'=4,'zp'=2,'c'=2] {'y','x','zp'}, dimensions={0} | all-to-all | bytes 4456448 | tf_op jit(solution)/shard_map/all_to_all | solution.py:221
  214.1 0.3 convert_reduce_fusion
  214.5 0.6 pad_maximum_fusion.1
  215.1 0.7 pad_maximum_fusion
  (23 shorter events, 0.2 us)
Async XLA Ops:
  7.2 83.1 %all-gather.3.cloned.1.call-start = ((), (), s32[]{:S(2)}) async-start(), calls=%async_computation.4 | async-start | bytes 4456448 | tf_op jit(solution)/shard_map/all_gather | solution.py:185
  8.2 6.7 %collective-permute-start = (bf16[256,256]{1,0:T(8,128)(2,1)S(1)}, bf16[256,256]{1,0:T(8,128)(2,1)S(1)}, u32[]{:S(2)}, u32[]{:S(2)}) collective-permute-start(bf16[256,256]{1,0:T(8,128)(2,1)S(1)} %get-tuple-element.13), channel_id=1, source_target_pairs={{0,2},{2,0},{1,3},{3,1},{4,6},{6,4},{5,7},{7,5},{8,10},{10,8},{9,1... | collective-permute-start | bytes 393224 | tf_op jit(solution)/shard_map/ppermute | solution.py:169
  16.6 17.6 %collective-permute-start.1 = (bf16[256,128]{0,1:T(8,128)(2,1)S(1)}, bf16[256,128]{0,1:T(8,128)(2,1)S(1)}, u32[]{:S(2)}, u32[]{:S(2)}) collective-permute-start(bf16[256,128]{0,1:T(8,128)(2,1)S(1)} %copy.34), channel_id=1, source_target_pairs={{0,16},{16,0},{1,17},{17,1},{2,18},{18,2},{3,19},{19,3},{4,20},{20... | collective-permute-start | bytes 196616 | tf_op jit(solution)/shard_map/ppermute | solution.py:169
  34.2 17.5 %collective-permute-start.2 = (bf16[256,256]{0,1:T(8,128)(2,1)S(1)}, bf16[256,256]{0,1:T(8,128)(2,1)S(1)}, u32[]{:S(2)}, u32[]{:S(2)}) collective-permute-start(bf16[256,256]{0,1:T(8,128)(2,1)S(1)} %bitcast.56), channel_id=1, source_target_pairs={{0,2},{2,0},{1,3},{3,1},{4,6},{6,4},{5,7},{7,5},{8,10},{10,8},{9,1... | collective-permute-start | bytes 393224 | tf_op jit(solution)/shard_map/ppermute | solution.py:169
  53.4 6.8 %copy-start.6 = (f32[256]{0:T(256)S(1)}, f32[256]{0:T(256)}, u32[]{:S(2)}) copy-start(f32[256]{0:T(256)} %param.6) | copy-start | bytes 3076
  53.4 32.2 %all-to-all-start = ((bf16[16,256,256]{2,1,0:T(8,128)(2,1)}), bf16[16,256,256]{2,1,0:T(8,128)(2,1)S(1)}, u32[]{:S(2)}, u32[]{:S(2)}) async-start(bf16[16,256,256]{2,1,0:T(8,128)(2,1)} %broadcast_in_dim.8), calls=%async_computation | async-start | bytes 4194304 | tf_op jit(solution)/shard_map/all_to_all | solution.py:194
  60.1 113.1 %all-gather.5.cloned.1.call-start = ((), (), s32[]{:S(2)}) async-start(), calls=%async_computation.5 | async-start | bytes 4456448 | tf_op jit(solution)/shard_map/all_gather | solution.py:208
  60.2 4.7 %collective-permute-start.3 = (f32[128]{0:T(128)S(1)}, f32[128]{0:T(128)S(1)}, u32[]{:S(2)}, u32[]{:S(2)}) collective-permute-start(f32[128]{0:T(128)S(1)} %broadcast_select_fusion.2), channel_id=1, source_target_pairs={{0,2},{2,0},{1,3},{3,1},{4,6},{6,4},{5,7},{7,5},{8,10},{10,8},{9,1... | collective-permute-start | bytes 1544 | tf_op jit(solution)/shard_map/ppermute | solution.py:169
  85.6 4.7 %copy-start.3 = (bf16[16,256,256]{2,1,0:T(8,128)(2,1)}, bf16[16,256,256]{2,1,0:T(8,128)(2,1)S(1)}, u32[]{:S(2)}) copy-start(bf16[16,256,256]{2,1,0:T(8,128)(2,1)S(1)} %all-to-all-done.land_ref) | copy-start | bytes 6291460
  99.8 23.5 %all-to-all-start.2 = ((f32[16,1,512]{2,1,0:T(1,128)}), f32[16,1,512]{2,1,0:T(1,128)S(1)}, u32[]{:S(2)}, u32[]{:S(2)}) async-start(f32[16,1,512]{2,1,0:T(1,128)} %broadcast_in_dim.11), calls=%async_computation.2 | async-start | bytes 65536 | tf_op jit(solution)/shard_map/all_to_all | solution.py:210
  124.9 3.9 %copy-start.5 = (s32[2,1024]{1,0:T(2,128)S(1)}, s32[2,1024]{1,0:T(2,128)}, u32[]{:S(2)}) copy-start(s32[2,1024]{1,0:T(2,128)} %param.7) | copy-start | bytes 24580
  124.9 37.0 %all-to-all-start.1 = ((bf16[16,256,256]{2,1,0:T(8,128)(2,1)}), bf16[16,256,256]{2,1,0:T(8,128)(2,1)S(1)}, u32[]{:S(2)}, u32[]{:S(2)}) async-start(bf16[16,256,256]{2,1,0:T(8,128)(2,1)} %broadcast_in_dim.10), calls=%async_computation.1 | async-start | bytes 4194304 | tf_op jit(solution)/shard_map/all_to_all | solution.py:194
  128.9 13.3 %collective-permute-start.4 = (s32[2,2,256]{2,1,0:T(2,128)S(1)}, s32[2,2,256]{2,1,0:T(2,128)S(1)}, u32[]{:S(2)}, u32[]{:S(2)}) collective-permute-start(s32[2,2,256]{2,1,0:T(2,128)S(1)} %get-tuple-element.19), channel_id=1, source_target_pairs={{0,16},{16,0},{1,17},{17,1},{2,18},{18,2},{3,19},{19,3},{4,20},{20... | collective-permute-start | bytes 12296 | tf_op jit(solution)/shard_map/ppermute | solution.py:169
  142.6 26.6 %copy-start.4 = (bf16[256,512]{1,0:T(8,128)(2,1)S(1)}, bf16[256,512]{1,0:T(8,128)(2,1)}, u32[]{:S(2)}) copy-start(bf16[256,512]{1,0:T(8,128)(2,1)} %get-tuple-element.7) | copy-start | bytes 786436
  161.9 1.4 copy-start.2
  171.7 1.0 copy-start
  172.7 0.6 copy-start.1
Sparse Core Ops, SparseCore 0:
  15.8 74.4 all-gather.2
  96.3 66.2 all-gather.4

commit v6 on v4

--- a/solution.py
+++ b/solution.py
@@ -113,10 +113,17 @@
         v_ref[cols, 0:wide] = v_high
         v_ref[cols, wide : 2 * wide] = (v - v_high.astype(jnp.float32)).astype(jnp.bfloat16)
 
-    grad_high = grad.astype(jnp.bfloat16).astype(jnp.float32)
-    tail_row = lax.broadcasted_iota(jnp.int32, (16, wide), 0)
-    tail = jnp.where(tail_row == 0, grad_high, jnp.where(tail_row == 1, grad - grad_high, 0.0))
-    tail = tail.astype(jnp.bfloat16)
+    high = grad.astype(jnp.bfloat16).astype(jnp.float32)
+    low = grad - high
+    row = lax.broadcasted_iota(jnp.int32, (16, BLOCK_ROWS), 0)
+    tails = []
+    for k in range(2):
+        left = slice(2 * k * BLOCK_ROWS, (2 * k + 1) * BLOCK_ROWS)
+        right = slice((2 * k + 1) * BLOCK_ROWS, (2 * k + 2) * BLOCK_ROWS)
+        tail = jnp.zeros((16, BLOCK_ROWS), jnp.float32)
+        for at, value in enumerate((high[:, left], high[:, right], low[:, left], low[:, right])):
+            tail = jnp.where(row == at, value, tail)
+        tails.append(tail.astype(jnp.bfloat16))
     copies[4].wait()
     for e in range(0, count // 2 // BLOCK_ROWS, 2):
         part = jnp.dot(
@@ -126,9 +133,12 @@
         for zp in range(2):
             d = e // 4 * 4 + zp * 2 + e // 2 % 2
             for k in range(2):
-                cols = slice(k * pairs, (k + 1) * pairs)
-                out_ref[2 * d + k, 0:BLOCK_ROWS, :] = part[zp * BLOCK_ROWS : (zp + 1) * BLOCK_ROWS, cols]
-                out_ref[2 * d + k, BLOCK_ROWS:, :] = tail[:, cols]
+                for side in range(2):
+                    at = (2 * k + side) * BLOCK_ROWS
+                    out_ref[2 * d + k, side * BLOCK_ROWS : (side + 1) * BLOCK_ROWS, :] = part[
+                        zp * BLOCK_ROWS : (zp + 1) * BLOCK_ROWS, at : at + BLOCK_ROWS
+                    ]
+                out_ref[2 * d + k, 2 * BLOCK_ROWS :, :] = tails[k]
 
 
 def make_gram(at, features, scores, row_pairs, col_pairs, scale, owners):
@@ -144,7 +154,7 @@
             vmem,
         ],
         out_specs=vmem,
-        out_shape=jax.ShapeDtypeStruct((owners, BLOCK_ROWS + 16, 2 * BLOCK_ROWS), jnp.bfloat16),
+        out_shape=jax.ShapeDtypeStruct((owners, 2 * BLOCK_ROWS + 16, BLOCK_ROWS), jnp.bfloat16),
         scratch_shapes=[
             pltpu.VMEM((4 * BLOCK_ROWS, responses), jnp.bfloat16),
             pltpu.VMEM((count // 2, responses), jnp.bfloat16),
@@ -202,7 +212,9 @@
     parts = make_gram(at, features, scores, row_pairs, col_pairs, scale, 2 * planes)
     parts = lax.all_to_all(parts, PLANE + ("zp",), 0, 0, tiled=True)
     total = jnp.sum(parts.astype(jnp.float32), axis=0)
-    return total[:BLOCK_ROWS], total[BLOCK_ROWS] + total[BLOCK_ROWS + 1]
+    gram = jnp.concatenate([total[:BLOCK_ROWS], total[BLOCK_ROWS : 2 * BLOCK_ROWS]], axis=1)
+    tail = total[2 * BLOCK_ROWS :]
+    return gram, jnp.concatenate([tail[0] + tail[2], tail[1] + tail[3]])
 
 
 def solution(mesh):

time: 212 us -> 212 us (level)
  no operation moved by 1% of the time
where the time goes in v6:
time: 212 us; the launch traced here: 211 us
  waiting for transfers between devices  88.5 us (42%)
  starting transfers between devices  46.9 us (22%)
  blocking collectives  37.6 us (18%)
  between operations  14.2 us (7%)
  Pallas kernels  13.2 us (6%)
  local copies, waits for them, and re-layouts  6.44 us (3%)
  other arithmetic  4.05 us (2%)
    all_to_all x1, blocking collectives, per_device(): parts = lax.all_to_all(parts, PLANE + ('zp',), 0, 0, tiled=True)  37.6 us
    ppermute x5, starting transfers between devices, swap(): return lax.ppermute(value, axis, [(0, 1), (1, 0)])  32.7 us
    all_gather x1, waiting for transfers between devices, per_device(): features = lax.all_gather(mine, RING, axis=0, tiled=True)  31.7 us
    all_to_all x1, waiting for transfers between devices, per_device(): lax.all_to_all(jnp.broadcast_to(part[None], (planes,) + part.shape), PLAN...  17.6 us
    all_gather x1, waiting for transfers between devices, per_device(): emb = lax.all_gather(in_order(zp, kept, swap(sent, 'zp')), RING)  15.5 us
    all_to_all x1, waiting for transfers between devices, per_device(): lax.all_to_all(jnp.broadcast_to(score, (ring, score.shape[1])), RING, 0,...  14.4 us
    ppermute x5, waiting for transfers between devices, swap(): return lax.ppermute(value, axis, [(0, 1), (1, 0)])  9.27 us
    pallas_call x1, Pallas kernels, make_gram(): pl.pallas_call(functools.partial(gram_kernel, scale), in_specs=[pl.BlockS...  7.35 us
  transfers between devices with their start and end apart: 9, of which 8 were waited for; matrix products, arithmetic and copies ran while one was open for 3% of the time, Pallas kernels for 0%

profile of v6, /device:TPU:1, one launch (start us, length us, event | category | flops | bytes accessed | tf_op | source)
XLA Modules:
  0.0 211.0 jit_solution(14780118623198030323)
XLA Ops:
  7.2 0.0 all-gather.3.cloned.1.call-start
  7.2 1.0 select_bitcast_fusion
  8.2 4.4 %collective-permute-start = (bf16[256,256]{1,0:T(8,128)(2,1)S(1)}, bf16[256,256]{1,0:T(8,128)(2,1)S(1)}, u32[]{:S(2)}, u32[]{:S(2)}) collective-permute-start(bf16[256,256]{1,0:T(8,128)(2,1)S(1)} %get-tuple-element.7), channel_id=1, source_target_pairs={{0,2},{2,0},{1,3},{3,1},{4,6},{6,4},{5,7},{7,5},{8,10},{10,8},{9,1... | collective-permute-start | bytes 393224 | tf_op jit(solution)/shard_map/ppermute | solution.py:172
  12.6 2.3 %collective-permute-done = bf16[256,256]{1,0:T(8,128)(2,1)S(1)} collective-permute-done((bf16[256,256]{1,0:T(8,128)(2,1)S(1)}, bf16[256,256]{1,0:T(8,128)(2,1)S(1)}, u32[]{:S(2)}, u32[]{:S(2)}) %collective-permute-start) | collective-permute-done | bytes 131104 | tf_op jit(solution)/shard_map/ppermute | solution.py:172
  14.9 0.7 maximum_select_fusion
  15.7 0.0 all-gather.3.cloned.1.call-update
  15.7 0.8 fusion.5
  16.5 0.1 copy.26
  16.6 0.1 copy.27
  16.7 15.8 %collective-permute-start.1 = (bf16[128,128]{0,1:T(8,128)(2,1)S(1)}, bf16[128,128]{0,1:T(8,128)(2,1)S(1)}, u32[]{:S(2)}, u32[]{:S(2)}) collective-permute-start(bf16[128,128]{0,1:T(8,128)(2,1)S(1)} %get-tuple-element.13), channel_id=1, source_target_pairs={{0,16},{16,0},{1,17},{17,1},{2,18},{18,2},{3,19},{19,3},{4,20},{20... | collective-permute-start | bytes 98312 | tf_op jit(solution)/shard_map/ppermute | solution.py:172
  32.6 1.4 collective-permute-done.1
  34.0 2.5 %collective-permute-start.2 = (bf16[128,256]{0,1:T(8,128)(2,1)S(1)}, bf16[128,256]{0,1:T(8,128)(2,1)S(1)}, u32[]{:S(2)}, u32[]{:S(2)}) collective-permute-start(bf16[128,256]{0,1:T(8,128)(2,1)S(1)} %bitcast.42), channel_id=1, source_target_pairs={{0,2},{2,0},{1,3},{3,1},{4,6},{6,4},{5,7},{7,5},{8,10},{10,8},{9,1... | collective-permute-start | bytes 196616 | tf_op jit(solution)/shard_map/ppermute | solution.py:172
  36.5 2.9 %collective-permute-done.2 = bf16[128,256]{0,1:T(8,128)(2,1)S(1)} collective-permute-done((bf16[128,256]{0,1:T(8,128)(2,1)S(1)}, bf16[128,256]{0,1:T(8,128)(2,1)S(1)}, u32[]{:S(2)}, u32[]{:S(2)}) %collective-permute-start.2) | collective-permute-done | bytes 65568 | tf_op jit(solution)/shard_map/ppermute | solution.py:172
  39.5 0.1 copy.21
  39.6 1.5 broadcast_in_dim.4
  41.1 0.0 copy-start.3
  41.1 6.9 %all-to-all-start = ((bf16[16,256,256]{2,1,0:T(8,128)(2,1)}), bf16[16,256,256]{2,1,0:T(8,128)(2,1)S(1)}, u32[]{:S(2)}, u32[]{:S(2)}) async-start(bf16[16,256,256]{2,1,0:T(8,128)(2,1)} %broadcast_in_dim.4), calls=%async_computation | async-start | bytes 4194304 | tf_op jit(solution)/shard_map/all_to_all | solution.py:196
  48.0 0.0 all-gather.5.cloned.1.call-start
  48.1 0.0 copy-done.3
  48.1 2.1 collective-permute-start.3
  50.2 2.6 %collective-permute-done.3 = f32[128]{0:T(128)S(1)} collective-permute-done((f32[128]{0:T(128)S(1)}, f32[128]{0:T(128)S(1)}, u32[]{:S(2)}, u32[]{:S(2)}) %collective-permute-start.3) | collective-permute-done | bytes 544 | tf_op jit(solution)/shard_map/ppermute | solution.py:172
  52.8 0.8 copy.22.alpha_ref
  53.6 17.6 %all-to-all-done.land_ref = bf16[16,256,256]{2,1,0:T(8,128)(2,1)S(1)} async-done(((bf16[16,256,256]{2,1,0:T(8,128)(2,1)}), bf16[16,256,256]{2,1,0:T(8,128)(2,1)S(1)}, u32[]{:S(2)}, u32[]{:S(2)}) %all-to-all-start) | async-done | bytes 2097184 | tf_op jit(solution)/shard_map/all_to_all | solution.py:196
  71.2 0.0 copy-start
  71.2 15.5 %all-gather.3.cloned.1.call-done = bf16[16,2,256,256]{3,2,1,0:T(8,128)(2,1)} async-done(((bf16[1,2,256,256]{3,2,1,0:T(8,128)(2,1)}), bf16[16,2,256,256]{3,2,1,0:T(8,128)(2,1)}) %all-gather.3.cloned.1.call-update) | async-done | bytes 4194320 | tf_op jit(solution)/shard_map/all_gather | solution.py:188
  86.7 0.0 copy-done
  86.7 0.0 copy-start.2
  86.7 5.9 %shard_map.59 = (bf16[256,512]{1,0:T(8,128)(2,1)}, f32[1,512]{1,0:T(1,128)}) custom-call(bf16[32,256,256]{2,1,0:T(8,128)(2,1)} %bitcast.38, bf16[16,256,256]{2,1,0:T(8,128)(2,1)} %copy-done, f32[256,1]{1,0:T(8,128)} %copy.22.alpha_ref), custom_call_target="tpu_custom_call" | custom-call | flops 1073741824 | bytes 4194304 | tf_op jit(solution)/shard_map/pallas_call | solution.py:47
  92.5 0.0 all-gather.5.cloned.1.call-update
  92.6 0.0 copy-done.2
  92.6 0.1 broadcast_subtract_fusion
  92.7 7.9 %collective-permute-start.4 = (s32[2,2,256]{2,1,0:T(2,128)S(1)}, s32[2,2,256]{2,1,0:T(2,128)S(1)}, u32[]{:S(2)}, u32[]{:S(2)}) collective-permute-start(s32[2,2,256]{2,1,0:T(2,128)S(1)} %get-tuple-element.17), channel_id=1, source_target_pairs={{0,16},{16,0},{1,17},{17,1},{2,18},{18,2},{3,19},{19,3},{4,20},{20... | collective-permute-start | bytes 12296 | tf_op jit(solution)/shard_map/ppermute | solution.py:172
  100.5 1.3 broadcast_in_dim.5
  101.9 7.3 %all-to-all-start.1 = ((f32[16,1,512]{2,1,0:T(1,128)}), f32[16,1,512]{2,1,0:T(1,128)S(1)}, u32[]{:S(2)}, u32[]{:S(2)}) async-start(f32[16,1,512]{2,1,0:T(1,128)} %broadcast_in_dim.5), calls=%async_computation.1 | async-start | bytes 65536 | tf_op jit(solution)/shard_map/all_to_all | solution.py:210
  109.1 0.6 pad_add_fusion.at_ref
  109.8 0.0 collective-permute-done.4
  109.8 0.2 copy.23
  110.0 0.0 copy-start.1
  110.0 0.8 copy.24.row_ref
  110.8 14.4 %all-to-all-done.1 = f32[16,1,512]{2,1,0:T(1,128)S(1)} async-done(((f32[16,1,512]{2,1,0:T(1,128)}), f32[16,1,512]{2,1,0:T(1,128)S(1)}, u32[]{:S(2)}, u32[]{:S(2)}) %all-to-all-start.1) | async-done | bytes 32800 | tf_op jit(solution)/shard_map/all_to_all | solution.py:210
  125.2 0.6 copy.29
  125.9 31.7 %all-gather.5.cloned.1.call-done.feat_ref = bf16[4096,512]{1,0:T(8,128)(2,1)} async-done(((bf16[256,512]{1,0:T(8,128)(2,1)}), bf16[4096,512]{1,0:T(8,128)(2,1)}) %all-gather.5.cloned.1.call-update) | async-done | bytes 4194320 | tf_op jit(solution)/shard_map/all_gather | solution.py:208
  157.6 0.0 copy-done.1
  157.6 7.4 %shard_map.60 = bf16[32,272,128]{2,1,0:T(8,128)(2,1)} custom-call(s32[2]{0:T(128)} %pad_add_fusion.at_ref, bf16[4096,512]{1,0:T(8,128)(2,1)} %all-gather.5.cloned.1.call-done.feat_ref, f32[16,512]{1,0:T(8,128)} %bitcast.46, s32[4,2,256]{2,1,0:T(2,128)} %copy.24.row_ref, s32[4,256,2]{2,1,0:T(8,128)} %bitcast.40), custom_call_target="tpu_custom_call" | custom-call | flops 2147483648 | bytes 2097152 | tf_op jit(solution)/shard_map/pallas_call | solution.py:147
  165.0 37.6 %all_to_all.18 = bf16[32,272,128]{2,1,0:T(8,128)(2,1)S(1)} all-to-all(bf16[32,272,128]{2,1,0:T(8,128)(2,1)} %shard_map.60), channel_id=1, replica_groups=mesh['y'=4,'x'=4,'zh'=2,'zm'=4,'zp'=2,'c'=2] {'y','x','zp'}, dimensions={0} | all-to-all | bytes 4456448 | tf_op jit(solution)/shard_map/all_to_all | solution.py:213
  202.6 0.3 convert_reduce_fusion
  202.9 0.6 pad_maximum_fusion.1
  203.5 0.7 pad_maximum_fusion
  (11 shorter events, 0.1 us)
Async XLA Ops:
  7.2 79.5 %all-gather.3.cloned.1.call-start = ((), (), s32[]{:S(2)}) async-start(), calls=%async_computation.3 | async-start | bytes 4456448 | tf_op jit(solution)/shard_map/all_gather | solution.py:188
  8.2 6.7 %collective-permute-start = (bf16[256,256]{1,0:T(8,128)(2,1)S(1)}, bf16[256,256]{1,0:T(8,128)(2,1)S(1)}, u32[]{:S(2)}, u32[]{:S(2)}) collective-permute-start(bf16[256,256]{1,0:T(8,128)(2,1)S(1)} %get-tuple-element.7), channel_id=1, source_target_pairs={{0,2},{2,0},{1,3},{3,1},{4,6},{6,4},{5,7},{7,5},{8,10},{10,8},{9,1... | collective-permute-start | bytes 393224 | tf_op jit(solution)/shard_map/ppermute | solution.py:172
  16.7 17.2 %collective-permute-start.1 = (bf16[128,128]{0,1:T(8,128)(2,1)S(1)}, bf16[128,128]{0,1:T(8,128)(2,1)S(1)}, u32[]{:S(2)}, u32[]{:S(2)}) collective-permute-start(bf16[128,128]{0,1:T(8,128)(2,1)S(1)} %get-tuple-element.13), channel_id=1, source_target_pairs={{0,16},{16,0},{1,17},{17,1},{2,18},{18,2},{3,19},{19,3},{4,20},{20... | collective-permute-start | bytes 98312 | tf_op jit(solution)/shard_map/ppermute | solution.py:172
  34.0 5.5 %collective-permute-start.2 = (bf16[128,256]{0,1:T(8,128)(2,1)S(1)}, bf16[128,256]{0,1:T(8,128)(2,1)S(1)}, u32[]{:S(2)}, u32[]{:S(2)}) collective-permute-start(bf16[128,256]{0,1:T(8,128)(2,1)S(1)} %bitcast.42), channel_id=1, source_target_pairs={{0,2},{2,0},{1,3},{3,1},{4,6},{6,4},{5,7},{7,5},{8,10},{10,8},{9,1... | collective-permute-start | bytes 196616 | tf_op jit(solution)/shard_map/ppermute | solution.py:172
  41.1 6.9 %copy-start.3 = (f32[256]{0:T(256)S(1)}, f32[256]{0:T(256)}, u32[]{:S(2)}) copy-start(f32[256]{0:T(256)} %param.6) | copy-start | bytes 3076
  41.1 30.1 %all-to-all-start = ((bf16[16,256,256]{2,1,0:T(8,128)(2,1)}), bf16[16,256,256]{2,1,0:T(8,128)(2,1)S(1)}, u32[]{:S(2)}, u32[]{:S(2)}) async-start(bf16[16,256,256]{2,1,0:T(8,128)(2,1)} %broadcast_in_dim.4), calls=%async_computation | async-start | bytes 4194304 | tf_op jit(solution)/shard_map/all_to_all | solution.py:196
  48.0 109.6 %all-gather.5.cloned.1.call-start = ((), (), s32[]{:S(2)}) async-start(), calls=%async_computation.4 | async-start | bytes 4456448 | tf_op jit(solution)/shard_map/all_gather | solution.py:208
  48.1 4.7 %collective-permute-start.3 = (f32[128]{0:T(128)S(1)}, f32[128]{0:T(128)S(1)}, u32[]{:S(2)}, u32[]{:S(2)}) collective-permute-start(f32[128]{0:T(128)S(1)} %broadcast_select_fusion.2), channel_id=1, source_target_pairs={{0,2},{2,0},{1,3},{3,1},{4,6},{6,4},{5,7},{7,5},{8,10},{10,8},{9,1... | collective-permute-start | bytes 1544 | tf_op jit(solution)/shard_map/ppermute | solution.py:172
  71.2 15.5 %copy-start = (bf16[16,256,256]{2,1,0:T(8,128)(2,1)}, bf16[16,256,256]{2,1,0:T(8,128)(2,1)S(1)}, u32[]{:S(2)}) copy-start(bf16[16,256,256]{2,1,0:T(8,128)(2,1)S(1)} %all-to-all-done.land_ref) | copy-start | bytes 6291460
  86.7 5.9 %copy-start.2 = (s32[2,1024]{1,0:T(2,128)S(1)}, s32[2,1024]{1,0:T(2,128)}, u32[]{:S(2)}) copy-start(s32[2,1024]{1,0:T(2,128)} %param.7) | copy-start | bytes 24580
  92.7 17.1 %collective-permute-start.4 = (s32[2,2,256]{2,1,0:T(2,128)S(1)}, s32[2,2,256]{2,1,0:T(2,128)S(1)}, u32[]{:S(2)}, u32[]{:S(2)}) collective-permute-start(s32[2,2,256]{2,1,0:T(2,128)S(1)} %get-tuple-element.17), channel_id=1, source_target_pairs={{0,16},{16,0},{1,17},{17,1},{2,18},{18,2},{3,19},{19,3},{4,20},{20... | collective-permute-start | bytes 12296 | tf_op jit(solution)/shard_map/ppermute | solution.py:172
  101.9 23.4 %all-to-all-start.1 = ((f32[16,1,512]{2,1,0:T(1,128)}), f32[16,1,512]{2,1,0:T(1,128)S(1)}, u32[]{:S(2)}, u32[]{:S(2)}) async-start(f32[16,1,512]{2,1,0:T(1,128)} %broadcast_in_dim.5), calls=%async_computation.1 | async-start | bytes 65536 | tf_op jit(solution)/shard_map/all_to_all | solution.py:210
  110.0 47.6 %copy-start.1 = (s32[2,2,2,256]{2,3,1,0:T(8,128)}, s32[2,2,2,256]{2,3,1,0:T(8,128)S(1)}, u32[]{:S(2)}) copy-start(s32[2,2,2,256]{2,3,1,0:T(8,128)S(1)} %copy.23) | copy-start | bytes 24580
Sparse Core Ops, SparseCore 0:
  15.8 70.8 all-gather.2
  92.7 64.8 all-gather.4

commit v7 on v6

--- a/solution.py
+++ b/solution.py
@@ -16,12 +16,34 @@
 NT = (((1,), (1,)), ((), ()))
 
 
-def features_kernel(emb_ref, land_ref, alpha_ref, out_ref, score_ref):
+def norms_kernel(land_ref, out_ref):
+    chunks, count, width = land_ref.shape
+    total = jnp.zeros((count, 128), jnp.float32)
+    for j in range(chunks):
+        for lane in range(0, width, 128):
+            part = land_ref[j, :, lane : lane + 128].astype(jnp.float32)
+            total += part * part
+    ones = jnp.ones((8, 128), jnp.float32)
+    norm = lax.dot_general(ones, total, NT, precision=lax.Precision.HIGHEST, preferred_element_type=jnp.float32)
+    out_ref[...] = lax.rsqrt(norm[0:1] + 1e-06)
+
+
+def make_norms(land):
+    return pl.pallas_call(
+        norms_kernel,
+        in_specs=[pl.BlockSpec(memory_space=pltpu.VMEM)],
+        out_specs=pl.BlockSpec(memory_space=pltpu.VMEM),
+        out_shape=jax.ShapeDtypeStruct((1, land.shape[1]), jnp.float32),
+        compiler_params=pltpu.CompilerParams(vmem_limit_bytes=16 * 1024 * 1024),
+        cost_estimate=pl.CostEstimate(flops=2 * land.size, bytes_accessed=2 * land.size, transcendentals=256),
+    )(land)
+
+
+def features_kernel(emb_ref, land_ref, norm_ref, alpha_ref, out_ref, score_ref):
     chunks, rows, width = emb_ref.shape
     count = land_ref.shape[1]
     total = jnp.zeros((rows, count), jnp.float32)
     resp = jnp.zeros((rows, 128), jnp.float32)
-    land = jnp.zeros((count, 128), jnp.float32)
     for j in range(chunks):
         zm, c, zp = j // 4, j // 2 % 2, j % 2
         at = zm * 4 + zp * 2 + c
@@ -29,18 +51,14 @@
         for lane in range(0, width, 128):
             part = emb_ref[j, :, lane : lane + 128].astype(jnp.float32)
             resp += part * part
-            part = land_ref[at, :, lane : lane + 128].astype(jnp.float32)
-            land += part * part
-    ones = jnp.ones((8, 128), jnp.float32)
-    norm = lax.dot_general(ones, land, NT, precision=lax.Precision.HIGHEST, preferred_element_type=jnp.float32)[0:1]
     square = jnp.sum(resp, axis=1, keepdims=True)
-    value = BETA * total * lax.rsqrt(square + 1e-06) * lax.rsqrt(norm + 1e-06)
+    value = BETA * total * lax.rsqrt(square + 1e-06) * norm_ref[...]
     features = jnp.exp(value).T.astype(out_ref.dtype)
     out_ref[...] = features
     score_ref[...] = jnp.sum(features.astype(jnp.float32) * alpha_ref[...], axis=0, keepdims=True)
 
 
-def make_features(emb, land, alpha, slabs):
+def make_features(emb, land, norms, alpha, slabs):
     chunks, rows, part = emb.shape
     count = land.shape[1]
     each = chunks // slabs
@@ -50,6 +68,7 @@
         in_specs=[
             pl.BlockSpec((each, rows, part), lambda s: (s, 0, 0)),
             pl.BlockSpec(land.shape, lambda s: (0, 0, 0)),
+            pl.BlockSpec((1, count), lambda s: (0, 0)),
             pl.BlockSpec((count, 1), lambda s: (0, 0)),
         ],
         out_specs=[
@@ -66,7 +85,7 @@
             bytes_accessed=2 * chunks * rows * part,
             transcendentals=count * slabs * rows,
         ),
-    )(emb, land, alpha)
+    )(emb, land, norms, alpha)
 
 
 def gram_kernel(scale, at_ref, feat_ref, score_ref, row_ref, col_ref, out_ref, own_ref, half_ref, v_ref, sems):
@@ -161,7 +180,7 @@
             pltpu.VMEM((responses, 8 * BLOCK_ROWS), jnp.bfloat16),
             pltpu.SemaphoreType.DMA((5,)),
         ],
-        compiler_params=pltpu.CompilerParams(vmem_limit_bytes=60 * 1024 * 1024),
+        compiler_params=pltpu.CompilerParams(vmem_limit_bytes=50 * 1024 * 1024),
         cost_estimate=pl.CostEstimate(
             flops=2 * count * responses * 512, bytes_accessed=count * responses, transcendentals=1024
         ),
@@ -204,7 +223,7 @@
     row_pairs = in_order(zh, local, swap(local, "zh")).reshape(blocks, 2, -1)
     col_pairs = row_pairs.transpose(0, 2, 1)
 
-    mine, score = make_features(emb, land, own_alpha, slabs)
+    mine, score = make_features(emb, land, make_norms(land), own_alpha, slabs)
     features = lax.all_gather(mine, RING, axis=0, tiled=True)
     ring = lax.axis_size(RING)
     scores = lax.all_to_all(jnp.broadcast_to(score, (ring, score.shape[1])), RING, 0, 0, tiled=True)

time: 212 us -> 208 us (0.981)
  no operation moved by 1% of the time
where the time goes in v7:
time: 208 us
  waiting for transfers between devices  89.6 us (43%)
  starting transfers between devices  46.9 us (23%)
  blocking collectives  36.7 us (18%)
  between operations  14.2 us (7%)
  Pallas kernels  11.1 us (5%)
  local copies, waits for them, and re-layouts  5.85 us (3%)
  other arithmetic  3.49 us (2%)
    all_to_all x1, blocking collectives, per_device(): parts = lax.all_to_all(parts, PLANE + ('zp',), 0, 0, tiled=True)  36.7 us
    all_gather x1, waiting for transfers between devices, per_device(): features = lax.all_gather(mine, RING, axis=0, tiled=True)  33.5 us
    ppermute x5, starting transfers between devices, swap(): return lax.ppermute(value, axis, [(0, 1), (1, 0)])  32.7 us
    all_to_all x1, waiting for transfers between devices, per_device(): lax.all_to_all(jnp.broadcast_to(part[None], (planes,) + part.shape), PLAN...  17.6 us
    all_to_all x1, waiting for transfers between devices, per_device(): lax.all_to_all(jnp.broadcast_to(score, (ring, score.shape[1])), RING, 0,...  15 us
    all_gather x1, waiting for transfers between devices, per_device(): emb = lax.all_gather(in_order(zp, kept, swap(sent, 'zp')), RING)  14.2 us
    ppermute x5, waiting for transfers between devices, swap(): return lax.ppermute(value, axis, [(0, 1), (1, 0)])  9.27 us
    all_to_all x1, starting transfers between devices, per_device(): lax.all_to_all(jnp.broadcast_to(score, (ring, score.shape[1])), RING, 0,...  7.25 us
  transfers between devices with their start and end apart: 9, of which 8 were waited for; matrix products, arithmetic and copies ran while one was open for 3% of the time, Pallas kernels for 0%

profile of v7, /device:TPU:1, one launch (start us, length us, event | category | flops | bytes accessed | tf_op | source)
XLA Modules:
  0.0 207.9 jit_solution(8699498946983671658)
XLA Ops:
  7.2 0.0 all-gather.3.cloned.1.call-start
  7.2 1.0 select_bitcast_fusion
  8.2 4.4 %collective-permute-start = (bf16[256,256]{1,0:T(8,128)(2,1)S(1)}, bf16[256,256]{1,0:T(8,128)(2,1)S(1)}, u32[]{:S(2)}, u32[]{:S(2)}) collective-permute-start(bf16[256,256]{1,0:T(8,128)(2,1)S(1)} %get-tuple-element.7), channel_id=1, source_target_pairs={{0,2},{2,0},{1,3},{3,1},{4,6},{6,4},{5,7},{7,5},{8,10},{10,8},{9,1... | collective-permute-start | bytes 393224 | tf_op jit(solution)/shard_map/ppermute | solution.py:191
  12.6 2.3 %collective-permute-done = bf16[256,256]{1,0:T(8,128)(2,1)S(1)} collective-permute-done((bf16[256,256]{1,0:T(8,128)(2,1)S(1)}, bf16[256,256]{1,0:T(8,128)(2,1)S(1)}, u32[]{:S(2)}, u32[]{:S(2)}) %collective-permute-start) | collective-permute-done | bytes 131104 | tf_op jit(solution)/shard_map/ppermute | solution.py:191
  14.9 0.7 maximum_select_fusion
  15.7 0.0 all-gather.3.cloned.1.call-update
  15.7 0.8 fusion.5
  16.5 0.1 copy.26
  16.6 0.1 copy.27
  16.7 15.8 %collective-permute-start.1 = (bf16[128,128]{0,1:T(8,128)(2,1)S(1)}, bf16[128,128]{0,1:T(8,128)(2,1)S(1)}, u32[]{:S(2)}, u32[]{:S(2)}) collective-permute-start(bf16[128,128]{0,1:T(8,128)(2,1)S(1)} %get-tuple-element.13), channel_id=1, source_target_pairs={{0,16},{16,0},{1,17},{17,1},{2,18},{18,2},{3,19},{19,3},{4,20},{20... | collective-permute-start | bytes 98312 | tf_op jit(solution)/shard_map/ppermute | solution.py:191
  32.6 1.4 collective-permute-done.1
  34.0 2.5 %collective-permute-start.2 = (bf16[128,256]{0,1:T(8,128)(2,1)S(1)}, bf16[128,256]{0,1:T(8,128)(2,1)S(1)}, u32[]{:S(2)}, u32[]{:S(2)}) collective-permute-start(bf16[128,256]{0,1:T(8,128)(2,1)S(1)} %bitcast.43), channel_id=1, source_target_pairs={{0,2},{2,0},{1,3},{3,1},{4,6},{6,4},{5,7},{7,5},{8,10},{10,8},{9,1... | collective-permute-start | bytes 196616 | tf_op jit(solution)/shard_map/ppermute | solution.py:191
  36.5 2.9 %collective-permute-done.2 = bf16[128,256]{0,1:T(8,128)(2,1)S(1)} collective-permute-done((bf16[128,256]{0,1:T(8,128)(2,1)S(1)}, bf16[128,256]{0,1:T(8,128)(2,1)S(1)}, u32[]{:S(2)}, u32[]{:S(2)}) %collective-permute-start.2) | collective-permute-done | bytes 65568 | tf_op jit(solution)/shard_map/ppermute | solution.py:191
  39.5 0.1 copy.21
  39.6 1.5 broadcast_in_dim.4
  41.1 0.0 copy-start.3
  41.1 6.9 %all-to-all-start = ((bf16[16,256,256]{2,1,0:T(8,128)(2,1)}), bf16[16,256,256]{2,1,0:T(8,128)(2,1)S(1)}, u32[]{:S(2)}, u32[]{:S(2)}) async-start(bf16[16,256,256]{2,1,0:T(8,128)(2,1)} %broadcast_in_dim.4), calls=%async_computation | async-start | bytes 4194304 | tf_op jit(solution)/shard_map/all_to_all | solution.py:215
  48.0 0.0 all-gather.5.cloned.1.call-start
  48.1 0.0 copy-done.3
  48.1 2.1 collective-permute-start.3
  50.2 2.6 %collective-permute-done.3 = f32[128]{0:T(128)S(1)} collective-permute-done((f32[128]{0:T(128)S(1)}, f32[128]{0:T(128)S(1)}, u32[]{:S(2)}, u32[]{:S(2)}) %collective-permute-start.3) | collective-permute-done | bytes 544 | tf_op jit(solution)/shard_map/ppermute | solution.py:191
  52.8 0.8 copy.22.alpha_ref
  53.6 17.6 %all-to-all-done.land_ref = bf16[16,256,256]{2,1,0:T(8,128)(2,1)S(1)} async-done(((bf16[16,256,256]{2,1,0:T(8,128)(2,1)}), bf16[16,256,256]{2,1,0:T(8,128)(2,1)S(1)}, u32[]{:S(2)}, u32[]{:S(2)}) %all-to-all-start) | async-done | bytes 2097184 | tf_op jit(solution)/shard_map/all_to_all | solution.py:215
  71.2 0.0 copy-start
  71.2 0.6 shard_map.59.norm_ref
  71.8 0.0 copy-start.1
  71.8 0.6 copy-done.1
  72.5 14.2 %all-gather.3.cloned.1.call-done = bf16[16,2,256,256]{3,2,1,0:T(8,128)(2,1)} async-done(((bf16[1,2,256,256]{3,2,1,0:T(8,128)(2,1)}), bf16[16,2,256,256]{3,2,1,0:T(8,128)(2,1)}) %all-gather.3.cloned.1.call-update) | async-done | bytes 4194320 | tf_op jit(solution)/shard_map/all_gather | solution.py:207
  86.7 0.0 copy-done
  86.7 0.0 copy-start.2
  86.7 5.1 %shard_map.60 = (bf16[256,512]{1,0:T(8,128)(2,1)}, f32[1,512]{1,0:T(1,128)}) custom-call(bf16[32,256,256]{2,1,0:T(8,128)(2,1)} %bitcast.41, bf16[16,256,256]{2,1,0:T(8,128)(2,1)} %copy-done, f32[1,256]{1,0:T(1,128)} %copy-done.1, f32[256,1]{1,0:T(8,128)} %copy.22.alpha_ref), custom_call_target="tpu_custom_call" | custom-call | flops 1073741824 | bytes 4194304 | tf_op jit(solution)/shard_map/pallas_call | solution.py:65
  91.8 0.0 all-gather.5.cloned.1.call-update
  91.8 0.0 copy-done.2
  91.8 0.1 broadcast_subtract_fusion
  91.9 7.9 %collective-permute-start.4 = (s32[2,2,256]{2,1,0:T(2,128)S(1)}, s32[2,2,256]{2,1,0:T(2,128)S(1)}, u32[]{:S(2)}, u32[]{:S(2)}) collective-permute-start(s32[2,2,256]{2,1,0:T(2,128)S(1)} %get-tuple-element.17), channel_id=1, source_target_pairs={{0,16},{16,0},{1,17},{17,1},{2,18},{18,2},{3,19},{19,3},{4,20},{20... | collective-permute-start | bytes 12296 | tf_op jit(solution)/shard_map/ppermute | solution.py:191
  99.8 1.3 broadcast_in_dim.5
  101.1 7.3 %all-to-all-start.1 = ((f32[16,1,512]{2,1,0:T(1,128)}), f32[16,1,512]{2,1,0:T(1,128)S(1)}, u32[]{:S(2)}, u32[]{:S(2)}) async-start(f32[16,1,512]{2,1,0:T(1,128)} %broadcast_in_dim.5), calls=%async_computation.1 | async-start | bytes 65536 | tf_op jit(solution)/shard_map/all_to_all | solution.py:229
  108.4 0.1 pad_add_fusion.at_ref
  108.4 0.0 collective-permute-done.4
  108.4 0.2 copy.23
  108.7 0.2 copy.24.row_ref
  108.9 15.0 %all-to-all-done.1 = f32[16,1,512]{2,1,0:T(1,128)S(1)} async-done(((f32[16,1,512]{2,1,0:T(1,128)}), f32[16,1,512]{2,1,0:T(1,128)S(1)}, u32[]{:S(2)}, u32[]{:S(2)}) %all-to-all-start.1) | async-done | bytes 32800 | tf_op jit(solution)/shard_map/all_to_all | solution.py:229
  123.9 33.5 %all-gather.5.cloned.1.call-done.feat_ref = bf16[4096,512]{1,0:T(8,128)(2,1)} async-done(((bf16[256,512]{1,0:T(8,128)(2,1)}), bf16[4096,512]{1,0:T(8,128)(2,1)}) %all-gather.5.cloned.1.call-update) | async-done | bytes 4194320 | tf_op jit(solution)/shard_map/all_gather | solution.py:227
  157.3 5.4 %shard_map.61 = bf16[32,272,128]{2,1,0:T(8,128)(2,1)S(1)} custom-call(s32[2]{0:T(128)S(1)} %pad_add_fusion.at_ref, bf16[4096,512]{1,0:T(8,128)(2,1)} %all-gather.5.cloned.1.call-done.feat_ref, f32[16,512]{1,0:T(8,128)S(1)} %bitcast.40, s32[4,2,256]{2,1,0:T(2,128)S(1)} %copy.24.row_ref, s32[4,256,2]{2,1,0:T(8,128)S(1)} %bitcast.39), custom_call_target="tpu_custom_call" | custom-call | flops 2147483648 | bytes 2097152 | tf_op jit(solution)/shard_map/pallas_call | solution.py:166
  162.8 36.7 %all_to_all.18 = bf16[32,272,128]{2,1,0:T(8,128)(2,1)S(1)} all-to-all(bf16[32,272,128]{2,1,0:T(8,128)(2,1)S(1)} %shard_map.61), channel_id=1, replica_groups=mesh['y'=4,'x'=4,'zh'=2,'zm'=4,'zp'=2,'c'=2] {'y','x','zp'}, dimensions={0} | all-to-all | bytes 4456448 | tf_op jit(solution)/shard_map/all_to_all | solution.py:232
  199.5 0.3 convert_reduce_fusion
  199.8 0.6 pad_maximum_fusion.1
  200.4 0.7 pad_maximum_fusion
  (12 shorter events, 0.1 us)
Async XLA Ops:
  7.2 79.5 %all-gather.3.cloned.1.call-start = ((), (), s32[]{:S(2)}) async-start(), calls=%async_computation.3 | async-start | bytes 4456448 | tf_op jit(solution)/shard_map/all_gather | solution.py:207
  8.2 6.7 %collective-permute-start = (bf16[256,256]{1,0:T(8,128)(2,1)S(1)}, bf16[256,256]{1,0:T(8,128)(2,1)S(1)}, u32[]{:S(2)}, u32[]{:S(2)}) collective-permute-start(bf16[256,256]{1,0:T(8,128)(2,1)S(1)} %get-tuple-element.7), channel_id=1, source_target_pairs={{0,2},{2,0},{1,3},{3,1},{4,6},{6,4},{5,7},{7,5},{8,10},{10,8},{9,1... | collective-permute-start | bytes 393224 | tf_op jit(solution)/shard_map/ppermute | solution.py:191
  16.7 17.2 %collective-permute-start.1 = (bf16[128,128]{0,1:T(8,128)(2,1)S(1)}, bf16[128,128]{0,1:T(8,128)(2,1)S(1)}, u32[]{:S(2)}, u32[]{:S(2)}) collective-permute-start(bf16[128,128]{0,1:T(8,128)(2,1)S(1)} %get-tuple-element.13), channel_id=1, source_target_pairs={{0,16},{16,0},{1,17},{17,1},{2,18},{18,2},{3,19},{19,3},{4,20},{20... | collective-permute-start | bytes 98312 | tf_op jit(solution)/shard_map/ppermute | solution.py:191
  34.0 5.5 %collective-permute-start.2 = (bf16[128,256]{0,1:T(8,128)(2,1)S(1)}, bf16[128,256]{0,1:T(8,128)(2,1)S(1)}, u32[]{:S(2)}, u32[]{:S(2)}) collective-permute-start(bf16[128,256]{0,1:T(8,128)(2,1)S(1)} %bitcast.43), channel_id=1, source_target_pairs={{0,2},{2,0},{1,3},{3,1},{4,6},{6,4},{5,7},{7,5},{8,10},{10,8},{9,1... | collective-permute-start | bytes 196616 | tf_op jit(solution)/shard_map/ppermute | solution.py:191
  41.1 6.9 %copy-start.3 = (f32[256]{0:T(256)S(1)}, f32[256]{0:T(256)}, u32[]{:S(2)}) copy-start(f32[256]{0:T(256)} %param.6) | copy-start | bytes 3076
  41.1 30.1 %all-to-all-start = ((bf16[16,256,256]{2,1,0:T(8,128)(2,1)}), bf16[16,256,256]{2,1,0:T(8,128)(2,1)S(1)}, u32[]{:S(2)}, u32[]{:S(2)}) async-start(bf16[16,256,256]{2,1,0:T(8,128)(2,1)} %broadcast_in_dim.4), calls=%async_computation | async-start | bytes 4194304 | tf_op jit(solution)/shard_map/all_to_all | solution.py:215
  48.0 109.3 %all-gather.5.cloned.1.call-start = ((), (), s32[]{:S(2)}) async-start(), calls=%async_computation.4 | async-start | bytes 4456448 | tf_op jit(solution)/shard_map/all_gather | solution.py:227
  48.1 4.7 %collective-permute-start.3 = (f32[128]{0:T(128)S(1)}, f32[128]{0:T(128)S(1)}, u32[]{:S(2)}, u32[]{:S(2)}) collective-permute-start(f32[128]{0:T(128)S(1)} %broadcast_select_fusion.2), channel_id=1, source_target_pairs={{0,2},{2,0},{1,3},{3,1},{4,6},{6,4},{5,7},{7,5},{8,10},{10,8},{9,1... | collective-permute-start | bytes 1544 | tf_op jit(solution)/shard_map/ppermute | solution.py:191
  71.2 15.5 %copy-start = (bf16[16,256,256]{2,1,0:T(8,128)(2,1)}, bf16[16,256,256]{2,1,0:T(8,128)(2,1)S(1)}, u32[]{:S(2)}) copy-start(bf16[16,256,256]{2,1,0:T(8,128)(2,1)S(1)} %all-to-all-done.land_ref) | copy-start | bytes 6291460
  71.8 0.6 copy-start.1
  86.7 5.2 %copy-start.2 = (s32[2,1024]{1,0:T(2,128)S(1)}, s32[2,1024]{1,0:T(2,128)}, u32[]{:S(2)}) copy-start(s32[2,1024]{1,0:T(2,128)} %param.7) | copy-start | bytes 24580
  91.9 16.5 %collective-permute-start.4 = (s32[2,2,256]{2,1,0:T(2,128)S(1)}, s32[2,2,256]{2,1,0:T(2,128)S(1)}, u32[]{:S(2)}, u32[]{:S(2)}) collective-permute-start(s32[2,2,256]{2,1,0:T(2,128)S(1)} %get-tuple-element.17), channel_id=1, source_target_pairs={{0,16},{16,0},{1,17},{17,1},{2,18},{18,2},{3,19},{19,3},{4,20},{20... | collective-permute-start | bytes 12296 | tf_op jit(solution)/shard_map/ppermute | solution.py:191
  101.1 22.8 %all-to-all-start.1 = ((f32[16,1,512]{2,1,0:T(1,128)}), f32[16,1,512]{2,1,0:T(1,128)S(1)}, u32[]{:S(2)}, u32[]{:S(2)}) async-start(f32[16,1,512]{2,1,0:T(1,128)} %broadcast_in_dim.5), calls=%async_computation.1 | async-start | bytes 65536 | tf_op jit(solution)/shard_map/all_to_all | solution.py:229
Sparse Core Ops, SparseCore 0:
  15.8 70.8 all-gather.2
  91.9 65.3 all-gather.4

commit v8 on v7

--- a/solution.py
+++ b/solution.py
@@ -88,7 +88,44 @@
     )(emb, land, norms, alpha)
 
 
-def gram_kernel(scale, at_ref, feat_ref, score_ref, row_ref, col_ref, out_ref, own_ref, half_ref, v_ref, sems):
+def pairs_kernel(scale, score_ref, row_ref, col_ref, select_ref, back_ref, weight_ref, rest_ref):
+    pairs = 2 * BLOCK_ROWS
+    scores = jnp.sum(score_ref[...], axis=0, keepdims=True)
+    lane = lax.broadcasted_iota(jnp.int32, (pairs, BLOCK_ROWS), 1)
+    sub = lax.broadcasted_iota(jnp.int32, (BLOCK_ROWS, pairs), 0)
+    for b in range(col_ref.shape[0]):
+        cols = slice(b * BLOCK_ROWS, (b + 1) * BLOCK_ROWS)
+        select = jnp.where(col_ref[b, :, 0:1] == lane, 1.0, 0.0) - jnp.where(col_ref[b, :, 1:2] == lane, 1.0, 0.0)
+        margin = jnp.sum(select * scores[:, cols], axis=1, keepdims=True)
+        prob = 1.0 / (1.0 + jnp.exp(-margin))
+        weight_ref[b] = prob * (1.0 - prob) * scale
+        rest_ref[b] = (1.0 - prob) * scale
+        select_ref[b] = select.astype(jnp.bfloat16)
+        back = jnp.where(row_ref[b, 0:1, :] == sub, 1.0, 0.0) - jnp.where(row_ref[b, 1:2, :] == sub, 1.0, 0.0)
+        back_ref[b] = back.astype(jnp.bfloat16)
+
+
+def make_pairs(scores, row_pairs, col_pairs, scale):
+    blocks, _, pairs = row_pairs.shape
+    vmem = pl.BlockSpec(memory_space=pltpu.VMEM)
+    return pl.pallas_call(
+        functools.partial(pairs_kernel, scale),
+        in_specs=[vmem] * 3,
+        out_specs=[vmem] * 4,
+        out_shape=[
+            jax.ShapeDtypeStruct((blocks, pairs, BLOCK_ROWS), jnp.bfloat16),
+            jax.ShapeDtypeStruct((blocks, BLOCK_ROWS, pairs), jnp.bfloat16),
+            jax.ShapeDtypeStruct((blocks, pairs, 1), jnp.float32),
+            jax.ShapeDtypeStruct((blocks, pairs, 1), jnp.float32),
+        ],
+        compiler_params=pltpu.CompilerParams(vmem_limit_bytes=16 * 1024 * 1024),
+        cost_estimate=pl.CostEstimate(flops=1000000, bytes_accessed=2000000, transcendentals=1024),
+    )(scores, row_pairs, col_pairs)
+
+
+def gram_kernel(
+    at_ref, feat_ref, select_ref, back_ref, weight_ref, rest_ref, out_ref, own_ref, half_ref, v_ref, sems
+):
     half, own = at_ref[0], at_ref[1]
     count, responses = feat_ref.shape
     blocks = responses // BLOCK_ROWS
@@ -107,27 +144,17 @@
     copies.append(pltpu.make_async_copy(feat_ref.at[rows], half_ref, sems.at[4]))
     for copy in copies:
         copy.start()
-    scores = jnp.sum(score_ref[...], axis=0, keepdims=True)
     for copy in copies[:4]:
         copy.wait()
 
     grad = jnp.zeros((1, wide), jnp.float32)
-    lane = lax.broadcasted_iota(jnp.int32, (pairs, BLOCK_ROWS), 1)
-    sub = lax.broadcasted_iota(jnp.int32, (BLOCK_ROWS, pairs), 0)
     for b in range(blocks):
         cols = slice(b * BLOCK_ROWS, (b + 1) * BLOCK_ROWS)
-        select = jnp.where(col_ref[b, :, 0:1] == lane, 1.0, 0.0) - jnp.where(col_ref[b, :, 1:2] == lane, 1.0, 0.0)
-        margin = jnp.sum(select * scores[:, cols], axis=1, keepdims=True)
-        prob = 1.0 / (1.0 + jnp.exp(-margin))
-        weight = prob * (1.0 - prob) * scale
-        diffs = lax.dot_general(
-            select.astype(jnp.bfloat16), own_ref[:, cols], NT, preferred_element_type=jnp.float32
-        )
+        diffs = lax.dot_general(select_ref[b], own_ref[:, cols], NT, preferred_element_type=jnp.float32)
         diffs = diffs.astype(jnp.bfloat16).astype(jnp.float32)
-        weighted = (diffs * weight).astype(jnp.bfloat16)
-        grad += jnp.sum(diffs * ((1.0 - prob) * scale), axis=0, keepdims=True)
-        back = jnp.where(row_ref[b, 0:1, :] == sub, 1.0, 0.0) - jnp.where(row_ref[b, 1:2, :] == sub, 1.0, 0.0)
-        v = jnp.dot(back.astype(jnp.bfloat16), weighted, preferred_element_type=jnp.float32)
+        weighted = (diffs * weight_ref[b]).astype(jnp.bfloat16)
+        grad += jnp.sum(diffs * rest_ref[b], axis=0, keepdims=True)
+        v = jnp.dot(back_ref[b], weighted, preferred_element_type=jnp.float32)
         v_high = v.astype(jnp.bfloat16)
         v_ref[cols, 0:wide] = v_high
         v_ref[cols, wide : 2 * wide] = (v - v_high.astype(jnp.float32)).astype(jnp.bfloat16)
@@ -160,14 +187,15 @@
                 out_ref[2 * d + k, 2 * BLOCK_ROWS :, :] = tails[k]
 
 
-def make_gram(at, features, scores, row_pairs, col_pairs, scale, owners):
+def make_gram(at, features, chosen, owners):
     count, responses = features.shape
     vmem = pl.BlockSpec(memory_space=pltpu.VMEM)
     return pl.pallas_call(
-        functools.partial(gram_kernel, scale),
+        gram_kernel,
         in_specs=[
             pl.BlockSpec(memory_space=pltpu.SMEM),
             pl.BlockSpec(memory_space=pl.ANY),
+            vmem,
             vmem,
             vmem,
             vmem,
@@ -184,7 +212,7 @@
         cost_estimate=pl.CostEstimate(
             flops=2 * count * responses * 512, bytes_accessed=count * responses, transcendentals=1024
         ),
-    )(at, features, scores, row_pairs, col_pairs)
+    )(at, features, *chosen)
 
 
 def swap(value, axis):
@@ -202,8 +230,8 @@
     scale = 1.0 / math.sqrt(pair_count * slabs * planes)
     zh, zp = lax.axis_index("zh"), lax.axis_index("zp")
 
-    low, high = embeddings[: rows // 2], embeddings[rows // 2 :]
-    kept, sent = jnp.where(zp == 0, low, high), jnp.where(zp == 0, high, low)
+    sent = lax.dynamic_slice_in_dim(embeddings, (1 - zp) * (rows // 2), rows // 2)
+    kept = lax.dynamic_slice_in_dim(embeddings, zp * (rows // 2), rows // 2)
     emb = lax.all_gather(in_order(zp, kept, swap(sent, "zp")), RING)
     emb = emb.reshape((-1,) + emb.shape[-2:])
 
@@ -228,7 +256,8 @@
     ring = lax.axis_size(RING)
     scores = lax.all_to_all(jnp.broadcast_to(score, (ring, score.shape[1])), RING, 0, 0, tiled=True)
     at = jnp.stack([zh, lax.axis_index(("zm", "c"))]).astype(jnp.int32)
-    parts = make_gram(at, features, scores, row_pairs, col_pairs, scale, 2 * planes)
+    chosen = make_pairs(scores, row_pairs, col_pairs, scale)
+    parts = make_gram(at, features, chosen, 2 * planes)
     parts = lax.all_to_all(parts, PLANE + ("zp",), 0, 0, tiled=True)
     total = jnp.sum(parts.astype(jnp.float32), axis=0)
     gram = jnp.concatenate([total[:BLOCK_ROWS], total[BLOCK_ROWS : 2 * BLOCK_ROWS]], axis=1)

time: 208 us -> 207 us (level)
    pallas_call x1 -> x2, Pallas kernels: 5.41 us -> 6.02 us  [the longest x1 5.23 us: make_gram(): pl.pallas_call(gram_kernel, in_specs=[pl.BlockSpec(memory_space=pltpu.SME...]
  transfers between devices with their start and end apart: 9 -> 9, of which waited for: 8 -> 8; matrix products, arithmetic and copies ran while one was open for 3% -> 3% of each run, Pallas kernels for 0% -> 1%
where the time goes in v8:
time: 207 us
  waiting for transfers between devices  88.9 us (43%)
  starting transfers between devices  46.8 us (23%)
  blocking collectives  36 us (17%)
  between operations  14.2 us (7%)
  Pallas kernels  11.7 us (6%)
  local copies, waits for them, and re-layouts  6.87 us (3%)
  other arithmetic  2.49 us (1%)
    all_to_all x1, blocking collectives, per_device(): parts = lax.all_to_all(parts, PLANE + ('zp',), 0, 0, tiled=True)  36 us
    ppermute x5, starting transfers between devices, swap(): return lax.ppermute(value, axis, [(0, 1), (1, 0)])  32.4 us
    all_gather x1, waiting for transfers between devices, per_device(): features = lax.all_gather(mine, RING, axis=0, tiled=True)  32 us
    all_to_all x1, waiting for transfers between devices, per_device(): lax.all_to_all(jnp.broadcast_to(part[None], (planes,) + part.shape), PLAN...  17.6 us
    all_to_all x1, waiting for transfers between devices, per_device(): lax.all_to_all(jnp.broadcast_to(score, (ring, score.shape[1])), RING, 0,...  15.7 us
    all_gather x1, waiting for transfers between devices, per_device(): emb = lax.all_gather(in_order(zp, kept, swap(sent, 'zp')), RING)  14.3 us
    ppermute x5, waiting for transfers between devices, swap(): return lax.ppermute(value, axis, [(0, 1), (1, 0)])  9.26 us
    all_to_all x1, starting transfers between devices, per_device(): lax.all_to_all(jnp.broadcast_to(score, (ring, score.shape[1])), RING, 0,...  7.41 us
  transfers between devices with their start and end apart: 9, of which 8 were waited for; matrix products, arithmetic and copies ran while one was open for 3% of the time, Pallas kernels for 1%

profile of v8, /device:TPU:1, one launch (start us, length us, event | category | flops | bytes accessed | tf_op | source)
XLA Modules:
  0.0 207.0 jit_solution(3722740073468036989)
XLA Ops:
  7.2 0.0 all-gather.3.cloned.1.call-start
  7.2 1.0 dynamic-slice_bitcast_fusion
  8.2 4.4 %collective-permute-start = (bf16[256,256]{1,0:T(8,128)(2,1)S(1)}, bf16[256,256]{1,0:T(8,128)(2,1)S(1)}, u32[]{:S(2)}, u32[]{:S(2)}) collective-permute-start(bf16[256,256]{1,0:T(8,128)(2,1)S(1)} %get-tuple-element.15), channel_id=1, source_target_pairs={{0,2},{2,0},{1,3},{3,1},{4,6},{6,4},{5,7},{7,5},{8,10},{10,8},{9,1... | collective-permute-start | bytes 393224 | tf_op jit(solution)/shard_map/ppermute | solution.py:219
  12.6 2.3 %collective-permute-done = bf16[256,256]{1,0:T(8,128)(2,1)S(1)} collective-permute-done((bf16[256,256]{1,0:T(8,128)(2,1)S(1)}, bf16[256,256]{1,0:T(8,128)(2,1)S(1)}, u32[]{:S(2)}, u32[]{:S(2)}) %collective-permute-start) | collective-permute-done | bytes 131104 | tf_op jit(solution)/shard_map/ppermute | solution.py:219
  14.9 0.7 maximum_select_fusion
  15.7 0.0 all-gather.3.cloned.1.call-update
  15.7 0.8 fusion.5
  16.5 0.1 copy.26
  16.6 0.1 copy.27
  16.7 15.8 %collective-permute-start.1 = (bf16[128,128]{0,1:T(8,128)(2,1)S(1)}, bf16[128,128]{0,1:T(8,128)(2,1)S(1)}, u32[]{:S(2)}, u32[]{:S(2)}) collective-permute-start(bf16[128,128]{0,1:T(8,128)(2,1)S(1)} %get-tuple-element.21), channel_id=1, source_target_pairs={{0,16},{16,0},{1,17},{17,1},{2,18},{18,2},{3,19},{19,3},{4,20},{20... | collective-permute-start | bytes 98312 | tf_op jit(solution)/shard_map/ppermute | solution.py:219
  32.6 1.4 collective-permute-done.1
  34.0 2.5 %collective-permute-start.2 = (bf16[128,256]{0,1:T(8,128)(2,1)S(1)}, bf16[128,256]{0,1:T(8,128)(2,1)S(1)}, u32[]{:S(2)}, u32[]{:S(2)}) collective-permute-start(bf16[128,256]{0,1:T(8,128)(2,1)S(1)} %bitcast.43), channel_id=1, source_target_pairs={{0,2},{2,0},{1,3},{3,1},{4,6},{6,4},{5,7},{7,5},{8,10},{10,8},{9,1... | collective-permute-start | bytes 196616 | tf_op jit(solution)/shard_map/ppermute | solution.py:219
  36.5 2.9 %collective-permute-done.2 = bf16[128,256]{0,1:T(8,128)(2,1)S(1)} collective-permute-done((bf16[128,256]{0,1:T(8,128)(2,1)S(1)}, bf16[128,256]{0,1:T(8,128)(2,1)S(1)}, u32[]{:S(2)}, u32[]{:S(2)}) %collective-permute-start.2) | collective-permute-done | bytes 65568 | tf_op jit(solution)/shard_map/ppermute | solution.py:219
  39.5 0.1 copy.21
  39.6 1.5 broadcast_in_dim.4
  41.1 0.0 copy-start.3
  41.1 6.9 %all-to-all-start = ((bf16[16,256,256]{2,1,0:T(8,128)(2,1)}), bf16[16,256,256]{2,1,0:T(8,128)(2,1)S(1)}, u32[]{:S(2)}, u32[]{:S(2)}) async-start(bf16[16,256,256]{2,1,0:T(8,128)(2,1)} %broadcast_in_dim.4), calls=%async_computation | async-start | bytes 4194304 | tf_op jit(solution)/shard_map/all_to_all | solution.py:243
  48.0 0.0 all-gather.5.cloned.1.call-start
  48.1 0.0 copy-done.3
  48.1 2.1 collective-permute-start.3
  50.2 2.6 %collective-permute-done.3 = f32[128]{0:T(128)S(1)} collective-permute-done((f32[128]{0:T(128)S(1)}, f32[128]{0:T(128)S(1)}, u32[]{:S(2)}, u32[]{:S(2)}) %collective-permute-start.3) | collective-permute-done | bytes 544 | tf_op jit(solution)/shard_map/ppermute | solution.py:219
  52.8 0.8 copy.22.alpha_ref
  53.6 17.6 %all-to-all-done.land_ref = bf16[16,256,256]{2,1,0:T(8,128)(2,1)S(1)} async-done(((bf16[16,256,256]{2,1,0:T(8,128)(2,1)}), bf16[16,256,256]{2,1,0:T(8,128)(2,1)S(1)}, u32[]{:S(2)}, u32[]{:S(2)}) %all-to-all-start) | async-done | bytes 2097184 | tf_op jit(solution)/shard_map/all_to_all | solution.py:243
  71.2 0.0 copy-start
  71.2 0.6 shard_map.59.norm_ref
  71.8 0.0 copy-start.1
  71.8 0.7 copy-done.1
  72.4 14.3 %all-gather.3.cloned.1.call-done = bf16[16,2,256,256]{3,2,1,0:T(8,128)(2,1)} async-done(((bf16[1,2,256,256]{3,2,1,0:T(8,128)(2,1)}), bf16[16,2,256,256]{3,2,1,0:T(8,128)(2,1)}) %all-gather.3.cloned.1.call-update) | async-done | bytes 4194320 | tf_op jit(solution)/shard_map/all_gather | solution.py:235
  86.7 0.0 copy-done
  86.7 5.1 %shard_map.60 = (bf16[256,512]{1,0:T(8,128)(2,1)}, f32[1,512]{1,0:T(1,128)}) custom-call(bf16[32,256,256]{2,1,0:T(8,128)(2,1)} %bitcast.41, bf16[16,256,256]{2,1,0:T(8,128)(2,1)} %copy-done, f32[1,256]{1,0:T(1,128)} %copy-done.1, f32[256,1]{1,0:T(8,128)} %copy.22.alpha_ref), custom_call_target="tpu_custom_call" | custom-call | flops 1073741824 | bytes 4194304 | tf_op jit(solution)/shard_map/pallas_call | solution.py:65
  91.9 0.0 all-gather.5.cloned.1.call-update
  91.9 0.0 copy-done.2
  91.9 0.1 broadcast_subtract_fusion
  92.0 7.6 %collective-permute-start.4 = (s32[2,2,256]{2,1,0:T(2,128)S(1)}, s32[2,2,256]{2,1,0:T(2,128)S(1)}, u32[]{:S(2)}, u32[]{:S(2)}) collective-permute-start(s32[2,2,256]{2,1,0:T(2,128)S(1)} %get-tuple-element.25), channel_id=1, source_target_pairs={{0,16},{16,0},{1,17},{17,1},{2,18},{18,2},{3,19},{19,3},{4,20},{20... | collective-permute-start | bytes 12296 | tf_op jit(solution)/shard_map/ppermute | solution.py:219
  99.6 1.3 broadcast_in_dim.5
  100.9 7.4 %all-to-all-start.1 = ((f32[16,1,512]{2,1,0:T(1,128)}), f32[16,1,512]{2,1,0:T(1,128)S(1)}, u32[]{:S(2)}, u32[]{:S(2)}) async-start(f32[16,1,512]{2,1,0:T(1,128)} %broadcast_in_dim.5), calls=%async_computation.1 | async-start | bytes 65536 | tf_op jit(solution)/shard_map/all_to_all | solution.py:257
  108.4 0.1 pad_add_fusion.at_ref
  108.4 0.0 collective-permute-done.4
  108.4 0.2 copy.23
  108.7 0.2 copy.24.row_ref
  108.9 15.7 %all-to-all-done.1 = f32[16,1,512]{2,1,0:T(1,128)S(1)} async-done(((f32[16,1,512]{2,1,0:T(1,128)}), f32[16,1,512]{2,1,0:T(1,128)S(1)}, u32[]{:S(2)}, u32[]{:S(2)}) %all-to-all-start.1) | async-done | bytes 32800 | tf_op jit(solution)/shard_map/all_to_all | solution.py:257
  124.5 0.8 shard_map.61
  125.3 32.0 %all-gather.5.cloned.1.call-done.feat_ref = bf16[4096,512]{1,0:T(8,128)(2,1)} async-done(((bf16[256,512]{1,0:T(8,128)(2,1)}), bf16[4096,512]{1,0:T(8,128)(2,1)}) %all-gather.5.cloned.1.call-update) | async-done | bytes 4194320 | tf_op jit(solution)/shard_map/all_gather | solution.py:255
  157.4 5.2 %shard_map.62 = bf16[32,272,128]{2,1,0:T(8,128)(2,1)S(1)} custom-call(s32[2]{0:T(128)S(1)} %pad_add_fusion.at_ref, bf16[4096,512]{1,0:T(8,128)(2,1)} %all-gather.5.cloned.1.call-done.feat_ref, bf16[4,256,128]{2,1,0:T(8,128)(2,1)S(1)} %get-tuple-element.10.select_ref, bf16[4,128,256]{2,1,0:T(8,128)(2,1)S(1)} %get-tuple-element.11.back_ref, ...), custom_call_target="tpu_custom_call" | custom-call | flops 2147483648 | bytes 2097152 | tf_op jit(solution)/shard_map/pallas_call | solution.py:193
  162.6 36.0 %all_to_all.18 = bf16[32,272,128]{2,1,0:T(8,128)(2,1)S(1)} all-to-all(bf16[32,272,128]{2,1,0:T(8,128)(2,1)S(1)} %shard_map.62), channel_id=1, replica_groups=mesh['y'=4,'x'=4,'zh'=2,'zm'=4,'zp'=2,'c'=2] {'y','x','zp'}, dimensions={0} | all-to-all | bytes 4456448 | tf_op jit(solution)/shard_map/all_to_all | solution.py:261
  198.6 0.3 convert_reduce_fusion
  198.9 0.7 pad_maximum_fusion
  199.6 0.6 pad_maximum_fusion.1
  (13 shorter events, 0.1 us)
Async XLA Ops:
  7.2 79.5 %all-gather.3.cloned.1.call-start = ((), (), s32[]{:S(2)}) async-start(), calls=%async_computation.3 | async-start | bytes 4456448 | tf_op jit(solution)/shard_map/all_gather | solution.py:235
  8.2 6.7 %collective-permute-start = (bf16[256,256]{1,0:T(8,128)(2,1)S(1)}, bf16[256,256]{1,0:T(8,128)(2,1)S(1)}, u32[]{:S(2)}, u32[]{:S(2)}) collective-permute-start(bf16[256,256]{1,0:T(8,128)(2,1)S(1)} %get-tuple-element.15), channel_id=1, source_target_pairs={{0,2},{2,0},{1,3},{3,1},{4,6},{6,4},{5,7},{7,5},{8,10},{10,8},{9,1... | collective-permute-start | bytes 393224 | tf_op jit(solution)/shard_map/ppermute | solution.py:219
  16.7 17.2 %collective-permute-start.1 = (bf16[128,128]{0,1:T(8,128)(2,1)S(1)}, bf16[128,128]{0,1:T(8,128)(2,1)S(1)}, u32[]{:S(2)}, u32[]{:S(2)}) collective-permute-start(bf16[128,128]{0,1:T(8,128)(2,1)S(1)} %get-tuple-element.21), channel_id=1, source_target_pairs={{0,16},{16,0},{1,17},{17,1},{2,18},{18,2},{3,19},{19,3},{4,20},{20... | collective-permute-start | bytes 98312 | tf_op jit(solution)/shard_map/ppermute | solution.py:219
  34.0 5.5 %collective-permute-start.2 = (bf16[128,256]{0,1:T(8,128)(2,1)S(1)}, bf16[128,256]{0,1:T(8,128)(2,1)S(1)}, u32[]{:S(2)}, u32[]{:S(2)}) collective-permute-start(bf16[128,256]{0,1:T(8,128)(2,1)S(1)} %bitcast.43), channel_id=1, source_target_pairs={{0,2},{2,0},{1,3},{3,1},{4,6},{6,4},{5,7},{7,5},{8,10},{10,8},{9,1... | collective-permute-start | bytes 196616 | tf_op jit(solution)/shard_map/ppermute | solution.py:219
  41.1 6.9 %copy-start.3 = (f32[256]{0:T(256)S(1)}, f32[256]{0:T(256)}, u32[]{:S(2)}) copy-start(f32[256]{0:T(256)} %param.6) | copy-start | bytes 3076
  41.1 30.1 %all-to-all-start = ((bf16[16,256,256]{2,1,0:T(8,128)(2,1)}), bf16[16,256,256]{2,1,0:T(8,128)(2,1)S(1)}, u32[]{:S(2)}, u32[]{:S(2)}) async-start(bf16[16,256,256]{2,1,0:T(8,128)(2,1)} %broadcast_in_dim.4), calls=%async_computation | async-start | bytes 4194304 | tf_op jit(solution)/shard_map/all_to_all | solution.py:243
  48.0 109.3 %all-gather.5.cloned.1.call-start = ((), (), s32[]{:S(2)}) async-start(), calls=%async_computation.4 | async-start | bytes 4456448 | tf_op jit(solution)/shard_map/all_gather | solution.py:255
  48.1 4.7 %collective-permute-start.3 = (f32[128]{0:T(128)S(1)}, f32[128]{0:T(128)S(1)}, u32[]{:S(2)}, u32[]{:S(2)}) collective-permute-start(f32[128]{0:T(128)S(1)} %broadcast_select_fusion.1), channel_id=1, source_target_pairs={{0,2},{2,0},{1,3},{3,1},{4,6},{6,4},{5,7},{7,5},{8,10},{10,8},{9,1... | collective-permute-start | bytes 1544 | tf_op jit(solution)/shard_map/ppermute | solution.py:219
  71.2 15.5 %copy-start = (bf16[16,256,256]{2,1,0:T(8,128)(2,1)}, bf16[16,256,256]{2,1,0:T(8,128)(2,1)S(1)}, u32[]{:S(2)}) copy-start(bf16[16,256,256]{2,1,0:T(8,128)(2,1)S(1)} %all-to-all-done.land_ref) | copy-start | bytes 6291460
  71.8 0.7 copy-start.1
  86.7 5.2 %copy-start.2 = (s32[2,1024]{1,0:T(2,128)S(1)}, s32[2,1024]{1,0:T(2,128)}, u32[]{:S(2)}) copy-start(s32[2,1024]{1,0:T(2,128)} %param.7) | copy-start | bytes 24580
  92.0 16.4 %collective-permute-start.4 = (s32[2,2,256]{2,1,0:T(2,128)S(1)}, s32[2,2,256]{2,1,0:T(2,128)S(1)}, u32[]{:S(2)}, u32[]{:S(2)}) collective-permute-start(s32[2,2,256]{2,1,0:T(2,128)S(1)} %get-tuple-element.25), channel_id=1, source_target_pairs={{0,16},{16,0},{1,17},{17,1},{2,18},{18,2},{3,19},{19,3},{4,20},{20... | collective-permute-start | bytes 12296 | tf_op jit(solution)/shard_map/ppermute | solution.py:219
  100.9 23.6 %all-to-all-start.1 = ((f32[16,1,512]{2,1,0:T(1,128)}), f32[16,1,512]{2,1,0:T(1,128)S(1)}, u32[]{:S(2)}, u32[]{:S(2)}) async-start(f32[16,1,512]{2,1,0:T(1,128)} %broadcast_in_dim.5), calls=%async_computation.1 | async-start | bytes 65536 | tf_op jit(solution)/shard_map/all_to_all | solution.py:257
Sparse Core Ops, SparseCore 0:
  15.8 70.8 all-gather.2
  92.0 65.3 all-gather.4

commit v9 on v8

--- a/solution.py
+++ b/solution.py
@@ -132,19 +132,14 @@
     pairs = 2 * BLOCK_ROWS
     wide = 4 * BLOCK_ROWS
     copies = []
-    for k in range(4):
-        zp, zh = k // 2, k % 2
-        rows = pl.ds(
-            pl.multiple_of(zh * (count // 2) + own * pairs + zp * BLOCK_ROWS, BLOCK_ROWS), BLOCK_ROWS
-        )
-        copies.append(
-            pltpu.make_async_copy(feat_ref.at[rows], own_ref.at[pl.ds(k * BLOCK_ROWS, BLOCK_ROWS)], sems.at[k])
-        )
+    for zh in range(2):
+        rows = pl.ds(pl.multiple_of(zh * (count // 2) + own * pairs, BLOCK_ROWS), pairs)
+        copies.append(pltpu.make_async_copy(feat_ref.at[rows], own_ref.at[pl.ds(zh * pairs, pairs)], sems.at[zh]))
     rows = pl.ds(pl.multiple_of(half * (count // 2), BLOCK_ROWS), count // 2)
-    copies.append(pltpu.make_async_copy(feat_ref.at[rows], half_ref, sems.at[4]))
+    copies.append(pltpu.make_async_copy(feat_ref.at[rows], half_ref, sems.at[2]))
     for copy in copies:
         copy.start()
-    for copy in copies[:4]:
+    for copy in copies[:2]:
         copy.wait()
 
     grad = jnp.zeros((1, wide), jnp.float32)
@@ -164,25 +159,29 @@
     row = lax.broadcasted_iota(jnp.int32, (16, BLOCK_ROWS), 0)
     tails = []
     for k in range(2):
-        left = slice(2 * k * BLOCK_ROWS, (2 * k + 1) * BLOCK_ROWS)
-        right = slice((2 * k + 1) * BLOCK_ROWS, (2 * k + 2) * BLOCK_ROWS)
+        left = slice(k * BLOCK_ROWS, (k + 1) * BLOCK_ROWS)
+        right = slice((k + 2) * BLOCK_ROWS, (k + 3) * BLOCK_ROWS)
         tail = jnp.zeros((16, BLOCK_ROWS), jnp.float32)
         for at, value in enumerate((high[:, left], high[:, right], low[:, left], low[:, right])):
             tail = jnp.where(row == at, value, tail)
         tails.append(tail.astype(jnp.bfloat16))
-    copies[4].wait()
-    for e in range(0, count // 2 // BLOCK_ROWS, 2):
+    copies[2].wait()
+    group = 16
+    for start in range(0, count // 2 // BLOCK_ROWS, group):
         part = jnp.dot(
-            half_ref[e * BLOCK_ROWS : (e + 2) * BLOCK_ROWS, :], v_ref[...], preferred_element_type=jnp.float32
+            half_ref[start * BLOCK_ROWS : (start + group) * BLOCK_ROWS, :],
+            v_ref[...],
+            preferred_element_type=jnp.float32,
         )
         part = (part[:, 0:wide] + part[:, wide:]).astype(jnp.bfloat16)
-        for zp in range(2):
-            d = e // 4 * 4 + zp * 2 + e // 2 % 2
+        for e in range(start, start + group):
+            d = e // 4 * 4 + e % 2 * 2 + e // 2 % 2
+            rows = slice((e - start) * BLOCK_ROWS, (e - start + 1) * BLOCK_ROWS)
             for k in range(2):
                 for side in range(2):
-                    at = (2 * k + side) * BLOCK_ROWS
+                    at = (2 * side + k) * BLOCK_ROWS
                     out_ref[2 * d + k, side * BLOCK_ROWS : (side + 1) * BLOCK_ROWS, :] = part[
-                        zp * BLOCK_ROWS : (zp + 1) * BLOCK_ROWS, at : at + BLOCK_ROWS
+                        rows, at : at + BLOCK_ROWS
                     ]
                 out_ref[2 * d + k, 2 * BLOCK_ROWS :, :] = tails[k]
 
@@ -206,7 +205,7 @@
             pltpu.VMEM((4 * BLOCK_ROWS, responses), jnp.bfloat16),
             pltpu.VMEM((count // 2, responses), jnp.bfloat16),
             pltpu.VMEM((responses, 8 * BLOCK_ROWS), jnp.bfloat16),
-            pltpu.SemaphoreType.DMA((5,)),
+            pltpu.SemaphoreType.DMA((3,)),
         ],
         compiler_params=pltpu.CompilerParams(vmem_limit_bytes=50 * 1024 * 1024),
         cost_estimate=pl.CostEstimate(

time: 207 us -> 207 us (level)
  no operation moved by 1% of the time
where the time goes in v9:
time: 207 us
  waiting for transfers between devices  88.9 us (43%)
  starting transfers between devices  46.8 us (23%)
  blocking collectives  36 us (17%)
  between operations  14.2 us (7%)
  Pallas kernels  11.7 us (6%)
  local copies, waits for them, and re-layouts  6.87 us (3%)
  other arithmetic  2.49 us (1%)
    all_to_all x1, blocking collectives, per_device(): parts = lax.all_to_all(parts, PLANE + ('zp',), 0, 0, tiled=True)  36 us
    ppermute x5, starting transfers between devices, swap(): return lax.ppermute(value, axis, [(0, 1), (1, 0)])  32.4 us
    all_gather x1, waiting for transfers between devices, per_device(): features = lax.all_gather(mine, RING, axis=0, tiled=True)  32 us
    all_to_all x1, waiting for transfers between devices, per_device(): lax.all_to_all(jnp.broadcast_to(part[None], (planes,) + part.shape), PLAN...  17.6 us
    all_to_all x1, waiting for transfers between devices, per_device(): lax.all_to_all(jnp.broadcast_to(score, (ring, score.shape[1])), RING, 0,...  15.7 us
    all_gather x1, waiting for transfers between devices, per_device(): emb = lax.all_gather(in_order(zp, kept, swap(sent, 'zp')), RING)  14.3 us
    ppermute x5, waiting for transfers between devices, swap(): return lax.ppermute(value, axis, [(0, 1), (1, 0)])  9.26 us
    all_to_all x1, starting transfers between devices, per_device(): lax.all_to_all(jnp.broadcast_to(score, (ring, score.shape[1])), RING, 0,...  7.41 us
  transfers between devices with their start and end apart: 9, of which 8 were waited for; matrix products, arithmetic and copies ran while one was open for 3% of the time, Pallas kernels for 1%

profile of v9, /device:TPU:1, one launch (start us, length us, event | category | flops | bytes accessed | tf_op | source)
XLA Modules:
  0.0 206.9 jit_solution(2909106952278416003)
XLA Ops:
  7.2 0.0 all-gather.3.cloned.1.call-start
  7.2 1.0 dynamic-slice_bitcast_fusion
  8.2 4.4 %collective-permute-start = (bf16[256,256]{1,0:T(8,128)(2,1)S(1)}, bf16[256,256]{1,0:T(8,128)(2,1)S(1)}, u32[]{:S(2)}, u32[]{:S(2)}) collective-permute-start(bf16[256,256]{1,0:T(8,128)(2,1)S(1)} %get-tuple-element.15), channel_id=1, source_target_pairs={{0,2},{2,0},{1,3},{3,1},{4,6},{6,4},{5,7},{7,5},{8,10},{10,8},{9,1... | collective-permute-start | bytes 393224 | tf_op jit(solution)/shard_map/ppermute | solution.py:218
  12.6 2.3 %collective-permute-done = bf16[256,256]{1,0:T(8,128)(2,1)S(1)} collective-permute-done((bf16[256,256]{1,0:T(8,128)(2,1)S(1)}, bf16[256,256]{1,0:T(8,128)(2,1)S(1)}, u32[]{:S(2)}, u32[]{:S(2)}) %collective-permute-start) | collective-permute-done | bytes 131104 | tf_op jit(solution)/shard_map/ppermute | solution.py:218
  14.9 0.7 maximum_select_fusion
  15.7 0.0 all-gather.3.cloned.1.call-update
  15.7 0.8 fusion.5
  16.5 0.1 copy.26
  16.6 0.1 copy.27
  16.7 15.8 %collective-permute-start.1 = (bf16[128,128]{0,1:T(8,128)(2,1)S(1)}, bf16[128,128]{0,1:T(8,128)(2,1)S(1)}, u32[]{:S(2)}, u32[]{:S(2)}) collective-permute-start(bf16[128,128]{0,1:T(8,128)(2,1)S(1)} %get-tuple-element.21), channel_id=1, source_target_pairs={{0,16},{16,0},{1,17},{17,1},{2,18},{18,2},{3,19},{19,3},{4,20},{20... | collective-permute-start | bytes 98312 | tf_op jit(solution)/shard_map/ppermute | solution.py:218
  32.6 1.4 collective-permute-done.1
  34.0 2.5 %collective-permute-start.2 = (bf16[128,256]{0,1:T(8,128)(2,1)S(1)}, bf16[128,256]{0,1:T(8,128)(2,1)S(1)}, u32[]{:S(2)}, u32[]{:S(2)}) collective-permute-start(bf16[128,256]{0,1:T(8,128)(2,1)S(1)} %bitcast.43), channel_id=1, source_target_pairs={{0,2},{2,0},{1,3},{3,1},{4,6},{6,4},{5,7},{7,5},{8,10},{10,8},{9,1... | collective-permute-start | bytes 196616 | tf_op jit(solution)/shard_map/ppermute | solution.py:218
  36.5 2.9 %collective-permute-done.2 = bf16[128,256]{0,1:T(8,128)(2,1)S(1)} collective-permute-done((bf16[128,256]{0,1:T(8,128)(2,1)S(1)}, bf16[128,256]{0,1:T(8,128)(2,1)S(1)}, u32[]{:S(2)}, u32[]{:S(2)}) %collective-permute-start.2) | collective-permute-done | bytes 65568 | tf_op jit(solution)/shard_map/ppermute | solution.py:218
  39.5 0.1 copy.21
  39.6 1.5 broadcast_in_dim.4
  41.1 0.0 copy-start.3
  41.1 6.9 %all-to-all-start = ((bf16[16,256,256]{2,1,0:T(8,128)(2,1)}), bf16[16,256,256]{2,1,0:T(8,128)(2,1)S(1)}, u32[]{:S(2)}, u32[]{:S(2)}) async-start(bf16[16,256,256]{2,1,0:T(8,128)(2,1)} %broadcast_in_dim.4), calls=%async_computation | async-start | bytes 4194304 | tf_op jit(solution)/shard_map/all_to_all | solution.py:242
  48.0 0.0 all-gather.5.cloned.1.call-start
  48.1 0.0 copy-done.3
  48.1 2.1 collective-permute-start.3
  50.2 2.6 %collective-permute-done.3 = f32[128]{0:T(128)S(1)} collective-permute-done((f32[128]{0:T(128)S(1)}, f32[128]{0:T(128)S(1)}, u32[]{:S(2)}, u32[]{:S(2)}) %collective-permute-start.3) | collective-permute-done | bytes 544 | tf_op jit(solution)/shard_map/ppermute | solution.py:218
  52.8 0.8 copy.22.alpha_ref
  53.6 17.6 %all-to-all-done.land_ref = bf16[16,256,256]{2,1,0:T(8,128)(2,1)S(1)} async-done(((bf16[16,256,256]{2,1,0:T(8,128)(2,1)}), bf16[16,256,256]{2,1,0:T(8,128)(2,1)S(1)}, u32[]{:S(2)}, u32[]{:S(2)}) %all-to-all-start) | async-done | bytes 2097184 | tf_op jit(solution)/shard_map/all_to_all | solution.py:242
  71.2 0.0 copy-start
  71.2 0.6 shard_map.59.norm_ref
  71.8 0.0 copy-start.1
  71.8 0.7 copy-done.1
  72.4 14.3 %all-gather.3.cloned.1.call-done = bf16[16,2,256,256]{3,2,1,0:T(8,128)(2,1)} async-done(((bf16[1,2,256,256]{3,2,1,0:T(8,128)(2,1)}), bf16[16,2,256,256]{3,2,1,0:T(8,128)(2,1)}) %all-gather.3.cloned.1.call-update) | async-done | bytes 4194320 | tf_op jit(solution)/shard_map/all_gather | solution.py:234
  86.7 0.0 copy-done
  86.7 5.1 %shard_map.60 = (bf16[256,512]{1,0:T(8,128)(2,1)}, f32[1,512]{1,0:T(1,128)}) custom-call(bf16[32,256,256]{2,1,0:T(8,128)(2,1)} %bitcast.41, bf16[16,256,256]{2,1,0:T(8,128)(2,1)} %copy-done, f32[1,256]{1,0:T(1,128)} %copy-done.1, f32[256,1]{1,0:T(8,128)} %copy.22.alpha_ref), custom_call_target="tpu_custom_call" | custom-call | flops 1073741824 | bytes 4194304 | tf_op jit(solution)/shard_map/pallas_call | solution.py:65
  91.9 0.0 all-gather.5.cloned.1.call-update
  91.9 0.0 copy-done.2
  91.9 0.1 broadcast_subtract_fusion
  92.0 7.6 %collective-permute-start.4 = (s32[2,2,256]{2,1,0:T(2,128)S(1)}, s32[2,2,256]{2,1,0:T(2,128)S(1)}, u32[]{:S(2)}, u32[]{:S(2)}) collective-permute-start(s32[2,2,256]{2,1,0:T(2,128)S(1)} %get-tuple-element.25), channel_id=1, source_target_pairs={{0,16},{16,0},{1,17},{17,1},{2,18},{18,2},{3,19},{19,3},{4,20},{20... | collective-permute-start | bytes 12296 | tf_op jit(solution)/shard_map/ppermute | solution.py:218
  99.6 1.3 broadcast_in_dim.5
  100.9 7.4 %all-to-all-start.1 = ((f32[16,1,512]{2,1,0:T(1,128)}), f32[16,1,512]{2,1,0:T(1,128)S(1)}, u32[]{:S(2)}, u32[]{:S(2)}) async-start(f32[16,1,512]{2,1,0:T(1,128)} %broadcast_in_dim.5), calls=%async_computation.1 | async-start | bytes 65536 | tf_op jit(solution)/shard_map/all_to_all | solution.py:256
  108.4 0.1 pad_add_fusion.at_ref
  108.4 0.0 collective-permute-done.4
  108.4 0.2 copy.23
  108.7 0.2 copy.24.row_ref
  108.9 15.7 %all-to-all-done.1 = f32[16,1,512]{2,1,0:T(1,128)S(1)} async-done(((f32[16,1,512]{2,1,0:T(1,128)}), f32[16,1,512]{2,1,0:T(1,128)S(1)}, u32[]{:S(2)}, u32[]{:S(2)}) %all-to-all-start.1) | async-done | bytes 32800 | tf_op jit(solution)/shard_map/all_to_all | solution.py:256
  124.5 0.8 shard_map.61
  125.3 32.0 %all-gather.5.cloned.1.call-done.feat_ref = bf16[4096,512]{1,0:T(8,128)(2,1)} async-done(((bf16[256,512]{1,0:T(8,128)(2,1)}), bf16[4096,512]{1,0:T(8,128)(2,1)}) %all-gather.5.cloned.1.call-update) | async-done | bytes 4194320 | tf_op jit(solution)/shard_map/all_gather | solution.py:254
  157.4 5.2 %shard_map.62 = bf16[32,272,128]{2,1,0:T(8,128)(2,1)S(1)} custom-call(s32[2]{0:T(128)S(1)} %pad_add_fusion.at_ref, bf16[4096,512]{1,0:T(8,128)(2,1)} %all-gather.5.cloned.1.call-done.feat_ref, bf16[4,256,128]{2,1,0:T(8,128)(2,1)S(1)} %get-tuple-element.10.select_ref, bf16[4,128,256]{2,1,0:T(8,128)(2,1)S(1)} %get-tuple-element.11.back_ref, ...), custom_call_target="tpu_custom_call" | custom-call | flops 2147483648 | bytes 2097152 | tf_op jit(solution)/shard_map/pallas_call | solution.py:192
  162.5 36.0 %all_to_all.18 = bf16[32,272,128]{2,1,0:T(8,128)(2,1)S(1)} all-to-all(bf16[32,272,128]{2,1,0:T(8,128)(2,1)S(1)} %shard_map.62), channel_id=1, replica_groups=mesh['y'=4,'x'=4,'zh'=2,'zm'=4,'zp'=2,'c'=2] {'y','x','zp'}, dimensions={0} | all-to-all | bytes 4456448 | tf_op jit(solution)/shard_map/all_to_all | solution.py:260
  198.5 0.3 convert_reduce_fusion
  198.8 0.7 pad_maximum_fusion
  199.5 0.6 pad_maximum_fusion.1
  (13 shorter events, 0.1 us)
Async XLA Ops:
  7.2 79.5 %all-gather.3.cloned.1.call-start = ((), (), s32[]{:S(2)}) async-start(), calls=%async_computation.3 | async-start | bytes 4456448 | tf_op jit(solution)/shard_map/all_gather | solution.py:234
  8.2 6.7 %collective-permute-start = (bf16[256,256]{1,0:T(8,128)(2,1)S(1)}, bf16[256,256]{1,0:T(8,128)(2,1)S(1)}, u32[]{:S(2)}, u32[]{:S(2)}) collective-permute-start(bf16[256,256]{1,0:T(8,128)(2,1)S(1)} %get-tuple-element.15), channel_id=1, source_target_pairs={{0,2},{2,0},{1,3},{3,1},{4,6},{6,4},{5,7},{7,5},{8,10},{10,8},{9,1... | collective-permute-start | bytes 393224 | tf_op jit(solution)/shard_map/ppermute | solution.py:218
  16.7 17.2 %collective-permute-start.1 = (bf16[128,128]{0,1:T(8,128)(2,1)S(1)}, bf16[128,128]{0,1:T(8,128)(2,1)S(1)}, u32[]{:S(2)}, u32[]{:S(2)}) collective-permute-start(bf16[128,128]{0,1:T(8,128)(2,1)S(1)} %get-tuple-element.21), channel_id=1, source_target_pairs={{0,16},{16,0},{1,17},{17,1},{2,18},{18,2},{3,19},{19,3},{4,20},{20... | collective-permute-start | bytes 98312 | tf_op jit(solution)/shard_map/ppermute | solution.py:218
  34.0 5.5 %collective-permute-start.2 = (bf16[128,256]{0,1:T(8,128)(2,1)S(1)}, bf16[128,256]{0,1:T(8,128)(2,1)S(1)}, u32[]{:S(2)}, u32[]{:S(2)}) collective-permute-start(bf16[128,256]{0,1:T(8,128)(2,1)S(1)} %bitcast.43), channel_id=1, source_target_pairs={{0,2},{2,0},{1,3},{3,1},{4,6},{6,4},{5,7},{7,5},{8,10},{10,8},{9,1... | collective-permute-start | bytes 196616 | tf_op jit(solution)/shard_map/ppermute | solution.py:218
  41.1 6.9 %copy-start.3 = (f32[256]{0:T(256)S(1)}, f32[256]{0:T(256)}, u32[]{:S(2)}) copy-start(f32[256]{0:T(256)} %param.6) | copy-start | bytes 3076
  41.1 30.1 %all-to-all-start = ((bf16[16,256,256]{2,1,0:T(8,128)(2,1)}), bf16[16,256,256]{2,1,0:T(8,128)(2,1)S(1)}, u32[]{:S(2)}, u32[]{:S(2)}) async-start(bf16[16,256,256]{2,1,0:T(8,128)(2,1)} %broadcast_in_dim.4), calls=%async_computation | async-start | bytes 4194304 | tf_op jit(solution)/shard_map/all_to_all | solution.py:242
  48.0 109.3 %all-gather.5.cloned.1.call-start = ((), (), s32[]{:S(2)}) async-start(), calls=%async_computation.4 | async-start | bytes 4456448 | tf_op jit(solution)/shard_map/all_gather | solution.py:254
  48.1 4.7 %collective-permute-start.3 = (f32[128]{0:T(128)S(1)}, f32[128]{0:T(128)S(1)}, u32[]{:S(2)}, u32[]{:S(2)}) collective-permute-start(f32[128]{0:T(128)S(1)} %broadcast_select_fusion.1), channel_id=1, source_target_pairs={{0,2},{2,0},{1,3},{3,1},{4,6},{6,4},{5,7},{7,5},{8,10},{10,8},{9,1... | collective-permute-start | bytes 1544 | tf_op jit(solution)/shard_map/ppermute | solution.py:218
  71.2 15.5 %copy-start = (bf16[16,256,256]{2,1,0:T(8,128)(2,1)}, bf16[16,256,256]{2,1,0:T(8,128)(2,1)S(1)}, u32[]{:S(2)}) copy-start(bf16[16,256,256]{2,1,0:T(8,128)(2,1)S(1)} %all-to-all-done.land_ref) | copy-start | bytes 6291460
  71.8 0.7 copy-start.1
  86.7 5.2 %copy-start.2 = (s32[2,1024]{1,0:T(2,128)S(1)}, s32[2,1024]{1,0:T(2,128)}, u32[]{:S(2)}) copy-start(s32[2,1024]{1,0:T(2,128)} %param.7) | copy-start | bytes 24580
  92.0 16.4 %collective-permute-start.4 = (s32[2,2,256]{2,1,0:T(2,128)S(1)}, s32[2,2,256]{2,1,0:T(2,128)S(1)}, u32[]{:S(2)}, u32[]{:S(2)}) collective-permute-start(s32[2,2,256]{2,1,0:T(2,128)S(1)} %get-tuple-element.25), channel_id=1, source_target_pairs={{0,16},{16,0},{1,17},{17,1},{2,18},{18,2},{3,19},{19,3},{4,20},{20... | collective-permute-start | bytes 12296 | tf_op jit(solution)/shard_map/ppermute | solution.py:218
  100.9 23.6 %all-to-all-start.1 = ((f32[16,1,512]{2,1,0:T(1,128)}), f32[16,1,512]{2,1,0:T(1,128)S(1)}, u32[]{:S(2)}, u32[]{:S(2)}) async-start(f32[16,1,512]{2,1,0:T(1,128)} %broadcast_in_dim.5), calls=%async_computation.1 | async-start | bytes 65536 | tf_op jit(solution)/shard_map/all_to_all | solution.py:256
Sparse Core Ops, SparseCore 0:
  15.8 70.8 all-gather.2
  92.0 65.3 all-gather.4
